TPU v7x, 32 devices: a whole 2x2x4 slice. The times are simulated.
32 devices in a mesh: region: 8 (over z, x), obs: 4 (over y, core).
Axes of the slice: x: 2, y: 2, z: 4, core: 2. Of those that a mesh axis runs over, the one named last changes fastest.
Arguments:
- pattern: int32 [262144], P(('region', 'obs')), may hold values from 0 to 511
- amplitude: float32 [5, 262144], P(None, ('region', 'obs')), may hold values from 0.5 to 1.5
- basis_table: bfloat16 [5, 512, 128], replicated, may hold values from -2 to 2, as said below
- fields: bfloat16 [64, 262144], P(None, ('region', 'obs')), may hold values from -24 to 24
- prior_precision: float32 [5, 128], replicated, may hold values from 16 to 512
Outputs:
- fitted: float32 [64, 262144], P(None, ('region', 'obs'))
Inputs may be any that keep to these rules, and one draw needn't show every extreme that they name: `basis_table`: basis rows of different tiers for one pattern are correlated.
All inputs are finite; a program needn't handle non-finite values.
Results may differ from a plain program's by a relative error of at most 0.0062.
Values sent between devices are 32-bit elements; how exact they have to be, the bound alone decides.
No kernel may reach another device: no remote copies, remote signals or barrier semaphores. Data moves between devices by JAX's collectives and lax.ppermute only.
A program may use at most 64 MiB of HBM per device.

v0:
```python
import functools

import jax
import jax.numpy as jnp
from jax import lax
from jax.experimental import pallas as pl
from jax.experimental.pallas import tpu as pltpu
from jax.sharding import PartitionSpec as P

highest = lax.Precision.HIGHEST
f32 = jnp.float32
bf16 = jnp.bfloat16
SUB = 8
vmem = pl.BlockSpec(memory_space=pltpu.VMEM)


def pair_index(tier, other):
    return tier * (tier + 1) // 2 + other


def dot(a, b):
    return jnp.dot(a, b, preferred_element_type=f32)


def dot_nt(a, b, precision=None):
    return lax.dot_general(
        a, b, (((1,), (1,)), ((), ())), precision=precision, preferred_element_type=f32
    )


def dot_tn(a, b):
    return lax.dot_general(
        a, b, (((0,), (0,)), ((), ())), precision=highest, preferred_element_type=f32
    )


def dot_hi(a, b):
    return jnp.dot(a, b, precision=highest, preferred_element_type=f32)


def split(value):
    high = value.astype(bf16)
    return high, (value - high.astype(f32)).astype(bf16)


def one_hot(pattern_row, pattern_count):
    rows = lax.broadcasted_iota(jnp.int16, (pattern_count, pattern_row.shape[1]), 0)
    return jnp.where(rows == pattern_row.astype(jnp.int16), jnp.asarray(1, bf16), jnp.asarray(0, bf16))


def stats_kernel(pattern_ref, amplitude_ref, fields_ref, basis_ref, pairs_ref, project_ref,
                 prods, acc):
    step = pl.program_id(0)
    tier_count, pattern_count, knots = basis_ref.shape
    field_count = fields_ref.shape[0]
    pair_rows = prods.shape[0]
    amp = amplitude_ref[...]
    prods[...] = jnp.zeros_like(prods)
    for tier in range(tier_count):
        first = pair_index(tier, 0)
        prods[first:first + tier + 1, :] = amp[:tier + 1] * amp[tier:tier + 1]
    pair_high, pair_low = split(prods[...])
    plain = fields_ref[...]
    field_rows = plain.astype(f32)
    shifted = amp - 1.0
    values = jnp.concatenate(
        [pair_high, pair_low, plain]
        + [(field_rows * shifted[tier:tier + 1]).astype(bf16) for tier in range(tier_count)],
        axis=0,
    )
    part = dot_nt(values, one_hot(pattern_ref[...], pattern_count))

    @pl.when(step == 0)
    def _():
        acc[...] = part

    @pl.when(step > 0)
    def _():
        acc[...] += part

    @pl.when(step == pl.num_programs(0) - 1)
    def _():
        pairs_ref[...] = acc[:pair_rows] + acc[pair_rows:2 * pair_rows]
        base = 2 * pair_rows
        plain_sum = acc[base:base + field_count]
        for tier in range(tier_count):
            first = base + (tier + 1) * field_count
            high, low = split(plain_sum + acc[first:first + field_count])
            project_ref[:, tier * knots:(tier + 1) * knots] = (
                dot(high, basis_ref[tier]) + dot(low, basis_ref[tier])
            )


def statistics(pattern, amplitude, fields, basis_table):
    tier_count, pattern_count, knots = basis_table.shape
    field_count, obs = fields.shape
    block = min(4096, obs)
    pair_rows = -(-pair_index(tier_count, 0) // 16) * 16
    rows = 2 * pair_rows + (1 + tier_count) * field_count
    return pl.pallas_call(
        stats_kernel,
        grid=(obs // block,),
        in_specs=[
            pl.BlockSpec((1, block), lambda i: (0, i)),
            pl.BlockSpec((tier_count, block), lambda i: (0, i)),
            pl.BlockSpec((field_count, block), lambda i: (0, i)),
            pl.BlockSpec(basis_table.shape, lambda i: (0, 0, 0)),
        ],
        out_specs=[
            pl.BlockSpec((pair_rows, pattern_count), lambda i: (0, 0)),
            pl.BlockSpec((field_count, tier_count * knots), lambda i: (0, 0)),
        ],
        out_shape=[
            jax.ShapeDtypeStruct((pair_rows, pattern_count), f32),
            jax.ShapeDtypeStruct((field_count, tier_count * knots), f32),
        ],
        scratch_shapes=[
            pltpu.VMEM((pair_rows, block), f32),
            pltpu.VMEM((rows, pattern_count), f32),
        ],
        compiler_params=pltpu.CompilerParams(vmem_limit_bytes=58 * 2**20),
        cost_estimate=pl.CostEstimate(
            flops=2 * rows * pattern_count * obs, bytes_accessed=4 * 2**20, transcendentals=0
        ),
        name="statistics",
    )(pattern.reshape(1, obs), amplitude, fields, basis_table)


def along_rows(x, row):
    return jnp.broadcast_to(x[row:row + 1, :], x.shape)


def along_lanes(x, lane):
    return jnp.broadcast_to(x[:, lane:lane + 1], x.shape)


def tree_sum(values):
    while len(values) > 1:
        ends = values[len(values) - len(values) % 2:]
        values = [values[i] + values[i + 1] for i in range(0, len(values) - 1, 2)] + ends
    return values[0]


def sweep(rows, first, group, lane0, sub, lane):
    count, blocks, size = len(rows), len(rows[0]), SUB * group
    here = (lane >= lane0) & (lane < lane0 + size)
    columns, pivot = [], []
    for m in range(count):
        block = rows[m][first:first + group]
        columns.append([[along_lanes(b, lane0 + j) for b in block] for j in range(size)])
        pivot.append([
            jnp.where(here, (lane - lane0 - SUB * a == sub).astype(f32), b)
            for a, b in enumerate(block)
        ])
    for k in range(size):
        at, row = divmod(k, SUB)
        is_row = sub == row
        scale = [
            pltpu.reciprocal(along_rows(columns[m][k][at], row), approx=True) for m in range(count)
        ]

        def eliminated(parts, m):
            scaled = along_rows(parts[at], row) * scale[m]
            out = [part - c * scaled for part, c in zip(parts, columns[m][k])]
            out[at] = jnp.where(is_row, scaled, out[at])
            return out

        for j in range(k + 1, size):
            for m in range(count):
                columns[m][j] = eliminated(columns[m][j], m)
        for m in range(count):
            pivot[m] = eliminated(pivot[m], m)
    solved = [[along_rows(pivot[m][j // SUB], j % SUB) for j in range(size)] for m in range(count)]
    out = [list(r) for r in rows]
    for step in range(blocks - group):
        i = (first + group + step) % blocks
        for m in range(count):
            total = tree_sum([along_lanes(rows[m][i], lane0 + j) * solved[m][j] for j in range(size)])
            out[m][i] = jnp.where(here, 0.0, rows[m][i]) - total
    for m in range(count):
        out[m][first:first + group] = pivot[m]
    return out


def invert(refs, panel_refs):
    size = refs[0].shape[0]
    count = len(refs)
    panel, group = (min(64, size), 2) if count <= 2 else (min(32, size), 1)
    blocks = panel // SUB
    sub = lax.broadcasted_iota(jnp.int32, (SUB, size), 0)
    lane = lax.broadcasted_iota(jnp.int32, (SUB, size), 1)
    wide = lax.broadcasted_iota(jnp.int32, (size, size), 1)
    for m in range(count):
        panel_refs[m][...] = jnp.zeros((size, size), f32)
    for p in range(size // panel):
        first = p * panel
        rows = [
            [refs[m][first + SUB * i:first + SUB * (i + 1), :] for i in range(blocks)]
            for m in range(count)
        ]
        for q in range(0, blocks, group):
            rows = sweep(rows, q, group, first + SUB * q, sub, lane)
        for m in range(count):
            if p > 0:
                panel_refs[m][first - panel:first, :] = jnp.zeros((panel, size), f32)
            for i in range(blocks):
                panel_refs[m][first + SUB * i:first + SUB * (i + 1), :] = rows[m][i]
        old = [refs[m][...] for m in range(count)]
        change = [dot_hi(old[m], panel_refs[m][...]) for m in range(count)]
        here = (wide >= first) & (wide < first + panel)
        for m in range(count):
            refs[m][...] = jnp.where(here, 0.0, old[m]) - change[m]
            for i in range(blocks):
                refs[m][first + SUB * i:first + SUB * (i + 1), :] = rows[m][i]


def diagonal(row):
    size = row.shape[1]
    rows = lax.broadcasted_iota(jnp.int32, (size, size), 0)
    columns = lax.broadcasted_iota(jnp.int32, (size, size), 1)
    return jnp.where(rows == columns, row, 0.0)


def gram_row(basis_ref, turned_ref, pairs, tier, node_count):
    turned = turned_ref[tier].astype(f32)
    knots = turned.shape[0]
    blocks = []
    for other in range(tier + 1):
        index = pair_index(tier, other)
        high, low = zip(*[split(turned * pairs[n][index:index + 1, :]) for n in range(node_count)])
        both = dot(jnp.concatenate(high + low, axis=0), basis_ref[other])
        blocks.append(both[:node_count * knots] + both[node_count * knots:])
    return jnp.concatenate(blocks, axis=1)


def eliminate(rows, tier, lower, prior_ref, inverse_ref, coupling_ref, panel_ref):
    knots = prior_ref.shape[1]
    width = tier * knots
    nodes = len(rows)
    prior = diagonal(prior_ref[tier:tier + 1, :])
    for n in range(nodes):
        inverse_ref[n] = rows[n][:, width:] + prior
    invert([inverse_ref.at[n] for n in range(nodes)], [panel_ref.at[n] for n in range(nodes)])
    couplings = [dot_hi(inverse_ref[n], rows[n][:, :width]) for n in range(nodes)]
    for n in range(nodes):
        coupling_ref[n] = couplings[n]
    for below in range(tier - 1, -1, -1):
        share = nodes // len(lower[below])
        first, last = below * knots, (below + 1) * knots
        for n in range(nodes):
            lower[below][n // share] -= dot_tn(rows[n][:, first:last], couplings[n][:, :last])


def store_rest(rest_ref, lower, top):
    knots = rest_ref.shape[0] // top
    for tier in range(top):
        size = (tier + 1) * knots
        rest_ref[size - knots:size, :size] = lower[tier][0]
        if tier < top - 1:
            rest_ref[size - knots:size, size:] = jnp.zeros((knots, (top - 1 - tier) * knots), f32)


def leaf_kernel(basis_ref, turned_ref, prior_ref, *refs, top):
    tier = basis_ref.shape[0] - 1
    leaves = 2 ** (tier - top)
    slot_refs, refs = refs[:leaves], refs[leaves:]
    inverse_ref, coupling_ref, rest_ref, panel_ref = refs[0], refs[1], refs[-2], refs[-1]
    row_refs = refs[2:-2]
    knots = basis_ref.shape[2]
    pairs = [ref[...] for ref in slot_refs]
    rows = gram_row(basis_ref, turned_ref, pairs, tier, leaves)
    lower = {}
    for below in range(tier - 1, -1, -1):
        if len(pairs) > 1:
            pairs = [pairs[2 * n] + pairs[2 * n + 1] for n in range(len(pairs) // 2)]
        part = gram_row(basis_ref, turned_ref, pairs, below, len(pairs))
        lower[below] = [part[n * knots:(n + 1) * knots] for n in range(len(pairs))]
    rows = [rows[n * knots:(n + 1) * knots] for n in range(leaves)]
    eliminate(rows, tier, lower, prior_ref, inverse_ref, coupling_ref, panel_ref)
    for ref, below in zip(row_refs, range(tier - 1, top - 1, -1)):
        for n, value in enumerate(lower[below]):
            ref[n] = value
    store_rest(rest_ref, lower, top)


def inner_kernel(*refs, top, count):
    row_refs, (rest_in, prior_ref), refs = refs[:count], refs[count:count + 2], refs[count + 2:]
    inverse_refs, coupling_refs, (rest_ref, panel_ref) = refs[:count], refs[count:-2], refs[-2:]
    knots = prior_ref.shape[1]
    lower = {
        top + count - 1 - i: [ref[n] for n in range(ref.shape[0])]
        for i, ref in enumerate(row_refs)
    }
    for tier in range(top):
        size = (tier + 1) * knots
        lower[tier] = [rest_in[size - knots:size, :size]]
    for i in range(count):
        tier = top + count - 1 - i
        eliminate(
            lower[tier], tier, lower, prior_ref, inverse_refs[i], coupling_refs[i], panel_ref
        )
    store_rest(rest_ref, lower, top)


def whole_call(kernel, args, shapes, scratch, name, limit=8, flops=10**10):
    return pl.pallas_call(
        kernel,
        in_specs=[vmem] * len(args),
        out_specs=[vmem] * len(shapes),
        out_shape=[jax.ShapeDtypeStruct(shape, f32) for shape in shapes],
        scratch_shapes=[pltpu.VMEM(shape, f32) for shape in scratch],
        compiler_params=pltpu.CompilerParams(vmem_limit_bytes=limit * 2**20),
        cost_estimate=pl.CostEstimate(flops=flops, bytes_accessed=2**20, transcendentals=0),
        name=name,
    )(*args)


def leaf_tier(slots, basis_table, turned, prior_precision, top):
    tier_count, _, knots = basis_table.shape
    tier = tier_count - 1
    leaves = len(slots)
    shapes = [(leaves, knots, knots), (leaves, knots, tier * knots)]
    shapes += [(2 ** (t - top), knots, (t + 1) * knots) for t in range(tier - 1, top - 1, -1)]
    shapes.append((top * knots, top * knots))
    inverse, coupling, *rows, rest = whole_call(
        functools.partial(leaf_kernel, top=top),
        (basis_table, turned, prior_precision, *slots),
        shapes, [(leaves, knots, knots)], "leaf_tier", limit=16, flops=2 * 10**10,
    )
    return inverse, coupling, rows, rest


def inner_tiers(rows, rest, prior_precision, top):
    knots = prior_precision.shape[1]
    count = len(rows)
    nodes = [value.shape[0] for value in rows]
    shapes = [(n, knots, knots) for n in nodes]
    shapes += [(n, knots, value.shape[2] - knots) for n, value in zip(nodes, rows)]
    shapes.append(rest.shape)
    out = whole_call(
        functools.partial(inner_kernel, top=top, count=count),
        (*rows, rest, prior_precision),
        shapes, [(max(nodes), knots, knots)], "inner_tiers", limit=16, flops=2 * 10**10,
    )
    return list(out[:count]), list(out[count:-1]), out[-1]


def forward_kernel(*refs, leaves):
    slot_refs, refs = refs[:leaves], refs[leaves:]
    out_refs = refs[-2:]
    coupling_refs = refs[:-2]
    knots = coupling_refs[0].shape[1]
    current = [ref[...] for ref in slot_refs]
    own = []
    for ref in coupling_refs:
        width = ref.shape[2]
        own.append(current[0][:, width:width + knots])
        reduced = [
            c[:, :width] - dot_hi(c[:, width:width + knots], ref[n]) for n, c in enumerate(current)
        ]
        current = (
            [reduced[2 * n] + reduced[2 * n + 1] for n in range(len(reduced) // 2)]
            if len(reduced) > 1 else reduced
        )
    out_refs[0][...] = current[0]
    out_refs[1][...] = jnp.concatenate(own, axis=1)


def forward(slots, couplings):
    fields = slots[0].shape[0]
    knots, width = couplings[-1].shape[1:]
    return pl.pallas_call(
        functools.partial(forward_kernel, leaves=len(slots)),
        in_specs=[vmem] * (len(slots) + len(couplings)),
        out_specs=[vmem] * 2,
        out_shape=[
            jax.ShapeDtypeStruct((fields, width), f32),
            jax.ShapeDtypeStruct((fields, knots * len(couplings)), f32),
        ],
        compiler_params=pltpu.CompilerParams(vmem_limit_bytes=8 * 2**20),
        name="forward",
    )(*slots, *couplings)


def top_step(rest, other, right, other_right, prior_row, inverse_ref, panel_ref):
    knots = inverse_ref.shape[0]
    total = rest + other
    right = right + other_right
    row = total[knots:]
    inverse_ref[...] = row[:, knots:] + diagonal(prior_row)
    invert([inverse_ref], [panel_ref])
    coupling = dot_hi(inverse_ref[...], row[:, :knots])
    schur = total[:knots, :knots] - dot_tn(row[:, :knots], coupling)
    top_right = right[:, knots:]
    return coupling, schur, top_right, right[:, :knots] - dot_hi(top_right, coupling)


def root_step(schur, root_right, prior_row, inverse_ref, panel_ref):
    inverse_ref[...] = schur + diagonal(prior_row)
    invert([inverse_ref], [panel_ref])
    return dot_hi(root_right, inverse_ref[...])


def path_step(path, right, inverse, coupling):
    local = dot_hi(right, inverse) - dot_nt(path, coupling, highest)
    return jnp.concatenate([path, local], axis=1)


def descend(path, own_ref, refs):
    count = len(refs) // 2
    knots = refs[0].shape[1]
    for depth in range(count - 1, -1, -1):
        own = own_ref[:, depth * knots:(depth + 1) * knots]
        path = path_step(path, own, refs[depth][0], refs[count + depth][0])
    return path


def both_kernel(*refs):
    rest_ref, other_ref, right_ref, other_right_ref, prior_ref, own_ref = refs[:6]
    refs, (out_ref, top_ref, root_ref, panel_ref) = refs[6:-4], refs[-4:]
    coupling, schur, top_right, root_right = top_step(
        rest_ref[...], other_ref[...], right_ref[...], other_right_ref[...], prior_ref[1:2, :],
        top_ref, panel_ref,
    )
    path = root_step(schur, root_right, prior_ref[0:1, :], root_ref, panel_ref)
    path = path_step(path, top_right, top_ref[...], coupling)
    out_ref[...] = descend(path, own_ref, refs)


def top_kernel(*refs):
    rest_ref, other_ref, right_ref, other_right_ref, prior_ref = refs[:5]
    inverse_ref, coupling_ref, schur_ref, top_right_ref, root_right_ref, panel_ref = refs[5:]
    coupling_ref[...], schur_ref[...], top_right_ref[...], root_right_ref[...] = top_step(
        rest_ref[...], other_ref[...], right_ref[...], other_right_ref[...], prior_ref[1:2, :],
        inverse_ref, panel_ref,
    )


def root_kernel(*refs):
    schur_ref, root_right_ref, prior_ref, top_inverse_ref, top_coupling_ref = refs[:5]
    top_right_ref, own_ref = refs[5:7]
    refs, (out_ref, root_ref, panel_ref) = refs[7:-3], refs[-3:]
    path = root_step(
        schur_ref[...], root_right_ref[...], prior_ref[0:1, :], root_ref, panel_ref
    )
    path = path_step(path, top_right_ref[...], top_inverse_ref[...], top_coupling_ref[...])
    out_ref[...] = descend(path, own_ref, refs)


def path_weights(rest, right, own, prior_precision, inverses, couplings, leaves):
    knots = prior_precision.shape[1]
    fields = right.shape[0]
    square = (knots, knots)
    weight_shape = (fields, prior_precision.shape[0] * knots)
    region_count = lax.axis_size("region")
    ends = (rest, swapped(rest, "obs", 1), right, swapped(right, "obs", 1), prior_precision)
    if region_count == leaves:
        args = (*ends, own, *inverses, *couplings)
        return whole_call(both_kernel, args, [weight_shape], [square] * 3, "top_and_root")[0]
    shapes = [square] * 3 + [(fields, knots)] * 2
    inverse, coupling, schur, top_right, root_right = whole_call(
        top_kernel, ends, shapes, [square], "top"
    )
    schur = sum_over(schur, "region", leaves, region_count)
    root_right = sum_over(root_right, "region", leaves, region_count)
    args = (schur, root_right, prior_precision, inverse, coupling, top_right, own)
    args += (*inverses, *couplings)
    return whole_call(root_kernel, args, [weight_shape], [square] * 2, "root")[0]


def fitted_kernel(pattern_ref, amplitude_ref, weight_ref, turned_ref, out_ref, table):
    tier_count, knots, pattern_count = turned_ref.shape
    field_count = weight_ref.shape[0]

    @pl.when(pl.program_id(0) == 0)
    def _():
        for tier in range(tier_count):
            high, low = split(weight_ref[:, tier * knots:(tier + 1) * knots])
            table[tier * field_count:(tier + 1) * field_count, :] = (
                dot(high, turned_ref[tier]) + dot(low, turned_ref[tier])
            ).astype(bf16)

    picked = dot(table[...], one_hot(pattern_ref[...], pattern_count))
    amp = amplitude_ref[...]
    total = picked[:field_count] * amp[0:1]
    for tier in range(1, tier_count):
        total = total + picked[tier * field_count:(tier + 1) * field_count] * amp[tier:tier + 1]
    out_ref[...] = total


def fitted_fields(pattern, amplitude, weights, turned):
    tier_count, knots, pattern_count = turned.shape
    obs = pattern.shape[0]
    field_count = weights.shape[0]
    block = min(2048, obs)
    return pl.pallas_call(
        fitted_kernel,
        grid=(obs // block,),
        in_specs=[
            pl.BlockSpec((1, block), lambda i: (0, i)),
            pl.BlockSpec((tier_count, block), lambda i: (0, i)),
            pl.BlockSpec(weights.shape, lambda i: (0, 0)),
            pl.BlockSpec(turned.shape, lambda i: (0, 0, 0)),
        ],
        out_specs=pl.BlockSpec((field_count, block), lambda i: (0, i)),
        out_shape=jax.ShapeDtypeStruct((field_count, obs), f32),
        scratch_shapes=[pltpu.VMEM((tier_count * field_count, pattern_count), bf16)],
        compiler_params=pltpu.CompilerParams(vmem_limit_bytes=16 * 2**20),
        name="fitted_fields",
    )(pattern.reshape(1, obs), amplitude, weights, turned)


def swapped(value, axis, mask):
    pairs = [(source, source ^ mask) for source in range(lax.axis_size(axis))]
    return lax.ppermute(value, axis, pairs)


def sum_over(value, axis, first_mask, size):
    mask = first_mask
    while mask < size:
        value = value + swapped(value, axis, mask)
        mask *= 2
    return value


def in_own_half(leaves):
    return (lax.axis_index("region") % leaves) // (leaves // 2) == lax.axis_index("obs") % 2


def sum_for_half(value, leaves):
    region_count, obs_count = lax.axis_size("region"), lax.axis_size("obs")
    half = leaves // 2
    total = jnp.where(in_own_half(leaves), value, 0.0)
    for offset in range(obs_count // 2):
        pairs = []
        for region in range(region_count):
            for obs in range(obs_count):
                source = region * obs_count + obs
                if (region % leaves) // half != obs % 2:
                    pairs.append((source, (region ^ half) * obs_count + (obs ^ 1 ^ 2 * offset)))
                elif offset > 0:
                    pairs.append((source, region * obs_count + (obs ^ 2 * offset)))
        total = total + lax.ppermute(value, ("region", "obs"), pairs)
    return total


def gather_half(value, leaves):
    return [value] + [swapped(value, "region", offset) for offset in range(1, leaves // 2)]


def spread_weights(weights, leaves):
    region_count, obs_count = lax.axis_size("region"), lax.axis_size("obs")
    half = leaves // 2
    pairs = []
    for region in range(region_count):
        holder = (region % leaves) // half
        for obs in range(holder, obs_count, 2):
            source = region * obs_count + obs
            pairs.append((source, region * obs_count + (obs ^ 1)))
    other = lax.ppermute(weights, ("region", "obs"), pairs)
    return jnp.where(in_own_half(leaves), weights, other)


def shards(pattern, amplitude, basis_table, fields, prior_precision):
    tier_count = basis_table.shape[0]
    leaves = 2 ** (tier_count - 2)
    turned = jnp.swapaxes(basis_table, 1, 2)
    pairs, project = statistics(pattern, amplitude, fields, basis_table)
    pairs = pairs + swapped(pairs, "obs", 1)
    project = project + swapped(project, "obs", 1)
    pairs = sum_for_half(pairs, leaves)
    pair_slots = gather_half(pairs, leaves)
    pair_slots, project = lax.optimization_barrier((pair_slots, project))
    inverse, coupling, rows, rest = leaf_tier(pair_slots, basis_table, turned, prior_precision, 2)
    project = sum_for_half(project, leaves)
    rows, rest, project = lax.optimization_barrier((rows, rest, project))
    inverses, couplings, rest = inner_tiers(rows, rest, prior_precision, 2)
    inverses, couplings = [inverse] + inverses, [coupling] + couplings
    project_slots = gather_half(project, leaves)
    right, own = forward(project_slots, couplings)
    rest, right = lax.optimization_barrier((rest, right))
    weights = path_weights(rest, right, own, prior_precision, inverses, couplings, leaves)
    weights = spread_weights(weights, leaves)
    return fitted_fields(pattern, amplitude, weights, turned)


def solution(mesh):
    return jax.shard_map(
        shards,
        mesh=mesh,
        in_specs=(
            P(("region", "obs")),
            P(None, ("region", "obs")),
            P(),
            P(None, ("region", "obs")),
            P(),
        ),
        out_specs=P(None, ("region", "obs")),
        check_vma=False,
    )
```

profile of v0, /device:TPU:0, one launch (start us, length us, event | category | flops | bytes accessed | tf_op | source)
XLA Modules:
  0.0 74.7 jit_solution(11635894221446358024)
XLA Ops:
  0.0 6.5 %statistics.1 = (f32[16,512]{1,0:T(8,128)}, f32[64,640]{1,0:T(8,128)}) custom-call(s32[1,8192]{1,0:T(1,128)} %bitcast.4, f32[5,8192]{1,0:T(8,128)} %amplitude_ref.3, bf16[64,8192]{1,0:T(8,128)(2,1)} %fields_ref.1, bf16[5,512,128]{2,1,0:T(8,128)(2,1)} %basis_ref.3), custom_call_target="tpu_custom_call" | custom-call | flops 3489660928 | bytes 4194304 | tf_op jit(solution)/shard_map/statistics/pallas_call | solution.py:100
  6.5 0.5 collective-permute-start
  7.0 1.1 %collective-permute-done = f32[16,512]{1,0:T(8,128)S(1)} collective-permute-done((f32[16,512]{1,0:T(8,128)}, f32[16,512]{1,0:T(8,128)S(1)}, u32[]{:S(2)}, u32[]{:S(2)}) %collective-permute-start) | collective-permute-done | bytes 32800 | tf_op jit(solution)/shard_map/ppermute | solution.py:515
  8.1 0.8 %add.32 = f32[16,512]{1,0:T(8,128)S(1)} add(f32[16,512]{1,0:T(8,128)} %get-tuple-element.30, f32[16,512]{1,0:T(8,128)S(1)} %collective-permute-done) | non-fusion elementwise | flops 8192 | bytes 98304 | tf_op jit(solution)/shard_map/add | solution.py:569
  8.8 2.9 %collective-permute-start.2 = (f32[16,512]{1,0:T(8,128)S(1)}, f32[16,512]{1,0:T(8,128)S(1)}, u32[]{:S(2)}, u32[]{:S(2)}) collective-permute-start(f32[16,512]{1,0:T(8,128)S(1)} %add.32), channel_id=1, source_target_pairs={{0,2},{1,18},{2,0},{3,16},{4,6},{5,22},{6,4},{7,20},{8,10},{9,26},... | collective-permute-start | bytes 98312 | tf_op jit(solution)/shard_map/ppermute | solution.py:543
  11.7 0.7 collective-permute-start.1
  12.3 3.6 %collective-permute-start.6 = (f32[64,640]{1,0:T(8,128)}, f32[64,640]{1,0:T(8,128)S(1)}, u32[]{:S(2)}, u32[]{:S(2)}) collective-permute-start(f32[64,640]{1,0:T(8,128)} %get-tuple-element.31), channel_id=1, source_target_pairs={{0,1},{1,0},{2,3},{3,2},{4,5},{5,4},{6,7},{7,6},{8,9},{9,8},{10,11... | collective-permute-start | bytes 491528 | tf_op jit(solution)/shard_map/ppermute | solution.py:515
  15.9 0.0 collective-permute-done.1
  15.9 2.6 %collective-permute-start.5 = (f32[16,512]{1,0:T(8,128)S(1)}, f32[16,512]{1,0:T(8,128)S(1)}, u32[]{:S(2)}, u32[]{:S(2)}) collective-permute-start(f32[16,512]{1,0:T(8,128)S(1)} %add_add_fusion.1.refs_0_), channel_id=1, source_target_pairs={{0,12},{4,8},{8,4},{12,0},{16,28},{20,24},{24,20},{28,16},{1,13},{... | collective-permute-start | bytes 98312 | tf_op jit(solution)/shard_map/ppermute | solution.py:515
  18.5 0.4 collective-permute-start.4
  18.9 0.5 collective-permute-start.3
  19.5 0.2 copy.6
  19.7 0.9 %add.35 = f32[64,640]{1,0:T(8,128)S(1)} add(f32[64,640]{1,0:T(8,128)} %get-tuple-element.31, f32[64,640]{1,0:T(8,128)S(1)} %collective-permute-done.6) | non-fusion elementwise | flops 40960 | bytes 491520 | tf_op jit(solution)/shard_map/add | solution.py:570
  20.7 0.1 collective-permute-done.5.refs_3_
  20.8 1.6 %collective-permute-done.4.refs_2_ = f32[16,512]{1,0:T(8,128)S(1)} collective-permute-done((f32[16,512]{1,0:T(8,128)S(1)}, f32[16,512]{1,0:T(8,128)S(1)}, u32[]{:S(2)}, u32[]{:S(2)}) %collective-permute-start.4) | collective-permute-done | bytes 32800 | tf_op jit(solution)/shard_map/ppermute | solution.py:515
  22.4 0.4 collective-permute-done.3.refs_1_
  22.9 0.5 collective-permute-start.8
  23.4 0.8 %collective-permute-start.7 = (f32[64,640]{1,0:T(8,128)S(1)}, f32[64,640]{1,0:T(8,128)S(1)}, u32[]{:S(2)}, u32[]{:S(2)}) collective-permute-start(f32[64,640]{1,0:T(8,128)S(1)} %add.35), channel_id=1, source_target_pairs={{1,16},{3,18},{5,20},{7,22},{9,24},{11,26},{13,28},{15,30},{16,1},... | collective-permute-start | bytes 491528 | tf_op jit(solution)/shard_map/ppermute | solution.py:543
  24.2 11.9 %leaf_tier.1 = (f32[4,128,128]{2,1,0:T(8,128)S(1)}, f32[4,128,512]{2,1,0:T(8,128)S(1)}, f32[2,128,512]{2,1,0:T(8,128)S(1)}, f32[1,128,384]{2,1,0:T(8,128)S(1)}, f32[256,256]{1,0:T(8,128)S(1)}) custom-call(bf16[5,512,128]{2,1,0:T(8,128)(2,1)S(1)} %copy-done, bf16[5,128,512]{2,1,0:T(8,128)(2,1)S(1)} %bitcast.2, f32[5,128]{1,0:T(8,128)S(1)} %copy-done.3, ...), custom_call_target="tpu_custom_call" | custom-call | flops 20000000000 | bytes 1048576 | tf_op jit(solution)/shard_map/leaf_tier/pallas_call | solution.py:306
  36.1 1.6 %collective-permute-start.11 = (f32[64,640]{1,0:T(8,128)S(1)}, f32[64,640]{1,0:T(8,128)S(1)}, u32[]{:S(2)}, u32[]{:S(2)}) collective-permute-start(f32[64,640]{1,0:T(8,128)S(1)} %add_add_fusion.refs_0_), channel_id=1, source_target_pairs={{0,12},{4,8},{8,4},{12,0},{16,28},{20,24},{24,20},{28,16},{1,13},{... | collective-permute-start | bytes 491528 | tf_op jit(solution)/shard_map/ppermute | solution.py:515
  37.8 0.4 collective-permute-start.10
  38.2 1.5 %collective-permute-start.9 = (f32[64,640]{1,0:T(8,128)S(1)}, f32[64,640]{1,0:T(8,128)S(1)}, u32[]{:S(2)}, u32[]{:S(2)}) collective-permute-start(f32[64,640]{1,0:T(8,128)S(1)} %add_add_fusion.refs_0_), channel_id=1, source_target_pairs={{0,4},{4,0},{8,12},{12,8},{16,20},{20,16},{24,28},{28,24},{1,5},{5... | collective-permute-start | bytes 491528 | tf_op jit(solution)/shard_map/ppermute | solution.py:515
  39.7 10.9 %inner_tiers.1 = (f32[2,128,128]{2,1,0:T(8,128)S(1)}, f32[1,128,128]{2,1,0:T(8,128)S(1)}, f32[2,128,384]{2,1,0:T(8,128)S(1)}, f32[1,128,256]{2,1,0:T(8,128)S(1)}, f32[256,256]{1,0:T(8,128)S(1)}) custom-call(f32[2,128,512]{2,1,0:T(8,128)S(1)} %get-tuple-element.40.refs_0_, f32[1,128,384]{2,1,0:T(8,128)S(1)} %get-tuple-element.41.refs_1_, ...), custom_call_target="tpu_custom_call" | custom-call | flops 20000000000 | bytes 1048576 | tf_op jit(solution)/shard_map/inner_tiers/pallas_call | solution.py:306
  50.7 0.0 collective-permute-done.10.refs_2_
  50.7 1.1 %forward.1 = (f32[64,256]{1,0:T(8,128)S(1)}, f32[64,384]{1,0:T(8,128)S(1)}) custom-call(f32[64,640]{1,0:T(8,128)S(1)} %add_add_fusion.refs_0_, f32[64,640]{1,0:T(8,128)S(1)} %collective-permute-done.9.refs_1_, f32[64,640]{1,0:T(8,128)S(1)} %collective-permute-done.10.refs_2_, f32[64,640]{1,0:T(8,128)S(1)} %collective-permute-done.11.refs_3_, ...), custom_call_target="tpu_custom_call" | custom-call | tf_op jit(solution)/shard_map/forward/pallas_call | solution.py:372
  51.8 4.9 %collective-permute-start.12 = (f32[256,256]{1,0:T(8,128)S(1)}, f32[256,256]{1,0:T(8,128)S(1)}, u32[]{:S(2)}, u32[]{:S(2)}) collective-permute-start(f32[256,256]{1,0:T(8,128)S(1)} %get-tuple-element.49.refs_0_), channel_id=1, source_target_pairs={{0,1},{1,0},{2,3},{3,2},{4,5},{5,4},{6,7},{7,6},{8,9},{9,8},{10,11... | collective-permute-start | bytes 786440 | tf_op jit(solution)/shard_map/ppermute | solution.py:515
  56.7 0.1 collective-permute-start.13
  56.8 1.2 %collective-permute-done.13.refs_3_ = f32[64,256]{1,0:T(8,128)S(1)} collective-permute-done((f32[64,256]{1,0:T(8,128)S(1)}, f32[64,256]{1,0:T(8,128)S(1)}, u32[]{:S(2)}, u32[]{:S(2)}) %collective-permute-start.13) | collective-permute-done | bytes 65568 | tf_op jit(solution)/shard_map/ppermute | solution.py:515
  58.0 8.8 %top_and_root.1 = f32[64,640]{1,0:T(8,128)S(1)} custom-call(f32[256,256]{1,0:T(8,128)S(1)} %get-tuple-element.49.refs_0_, f32[256,256]{1,0:T(8,128)S(1)} %collective-permute-done.12.refs_1_, f32[64,256]{1,0:T(8,128)S(1)} %get-tuple-element.50.refs_2_, f32[64,256]{1,0:T(8,128)S(1)} %collective-permute-done.13.refs_3_, f32[5,128]{1,0:T(8,128)S(1)} %copy-done.3, ...), custom_call_target="tpu_custom_call" | custom-call | flops 10000000000 | bytes 1048576 | tf_op jit(solution)/shard_map/top_and_root/pallas_call | solution.py:306
  66.8 2.3 %collective-permute-start.14 = (f32[64,640]{1,0:T(8,128)S(1)}, f32[64,640]{1,0:T(8,128)S(1)}, u32[]{:S(2)}, u32[]{:S(2)}) collective-permute-start(f32[64,640]{1,0:T(8,128)S(1)} %top_and_root.1), channel_id=1, source_target_pairs={{0,1},{2,3},{4,5},{6,7},{8,9},{10,11},{12,13},{14,15},{17,16},{19,... | collective-permute-start | bytes 491528 | tf_op jit(solution)/shard_map/ppermute | solution.py:560
  69.1 1.0 %collective-permute-done.14 = f32[64,640]{1,0:T(8,128)S(1)} collective-permute-done((f32[64,640]{1,0:T(8,128)S(1)}, f32[64,640]{1,0:T(8,128)S(1)}, u32[]{:S(2)}, u32[]{:S(2)}) %collective-permute-start.14) | collective-permute-done | bytes 163872 | tf_op jit(solution)/shard_map/ppermute | solution.py:560
  70.1 4.6 %fitted_fields.1 = f32[64,8192]{1,0:T(8,128)} custom-call(s32[1,8192]{1,0:T(1,128)S(1)} %bitcast.5, f32[5,8192]{1,0:T(8,128)S(1)} %copy-done.1, f32[64,640]{1,0:T(8,128)S(1)} %broadcast_select_fusion.weight_ref, bf16[5,128,512]{2,1,0:T(8,128)(2,1)S(1)} %bitcast.3), custom_call_target="tpu_custom_call" | custom-call | tf_op jit(solution)/shard_map/fitted_fields/pallas_call | solution.py:496
  (18 shorter events, 0.1 us)
Async XLA Ops:
  0.0 19.5 %copy-start = (bf16[5,512,128]{2,1,0:T(8,128)(2,1)S(1)}, bf16[5,512,128]{2,1,0:T(8,128)(2,1)}, u32[]{:S(2)}) copy-start(bf16[5,512,128]{2,1,0:T(8,128)(2,1)} %basis_ref.3) | copy-start | bytes 1966084
  6.5 17.7 %copy-start.3 = (f32[5,128]{1,0:T(8,128)S(1)}, f32[5,128]{1,0:T(8,128)}, u32[]{:S(2)}) copy-start(f32[5,128]{1,0:T(8,128)} %refs_4_.1) | copy-start | bytes 7684
  6.5 1.5 %collective-permute-start = (f32[16,512]{1,0:T(8,128)}, f32[16,512]{1,0:T(8,128)S(1)}, u32[]{:S(2)}, u32[]{:S(2)}) collective-permute-start(f32[16,512]{1,0:T(8,128)} %get-tuple-element.30), channel_id=1, source_target_pairs={{0,1},{1,0},{2,3},{3,2},{4,5},{5,4},{6,7},{7,6},{8,9},{9,8},{10,11... | collective-permute-start | bytes 98312 | tf_op jit(solution)/shard_map/ppermute | solution.py:515
  8.8 7.1 %collective-permute-start.2 = (f32[16,512]{1,0:T(8,128)S(1)}, f32[16,512]{1,0:T(8,128)S(1)}, u32[]{:S(2)}, u32[]{:S(2)}) collective-permute-start(f32[16,512]{1,0:T(8,128)S(1)} %add.32), channel_id=1, source_target_pairs={{0,2},{1,18},{2,0},{3,16},{4,6},{5,22},{6,4},{7,20},{8,10},{9,26},... | collective-permute-start | bytes 98312 | tf_op jit(solution)/shard_map/ppermute | solution.py:543
  11.7 4.2 %collective-permute-start.1 = (f32[16,512]{1,0:T(8,128)S(1)}, f32[16,512]{1,0:T(8,128)S(1)}, u32[]{:S(2)}, u32[]{:S(2)}) collective-permute-start(f32[16,512]{1,0:T(8,128)S(1)} %add.32), channel_id=1, source_target_pairs={{1,16},{3,18},{5,20},{7,22},{9,24},{11,26},{13,28},{15,30},{16,1},... | collective-permute-start | bytes 98312 | tf_op jit(solution)/shard_map/ppermute | solution.py:543
  12.3 7.4 %collective-permute-start.6 = (f32[64,640]{1,0:T(8,128)}, f32[64,640]{1,0:T(8,128)S(1)}, u32[]{:S(2)}, u32[]{:S(2)}) collective-permute-start(f32[64,640]{1,0:T(8,128)} %get-tuple-element.31), channel_id=1, source_target_pairs={{0,1},{1,0},{2,3},{3,2},{4,5},{5,4},{6,7},{7,6},{8,9},{9,8},{10,11... | collective-permute-start | bytes 491528 | tf_op jit(solution)/shard_map/ppermute | solution.py:515
  15.9 4.9 %collective-permute-start.5 = (f32[16,512]{1,0:T(8,128)S(1)}, f32[16,512]{1,0:T(8,128)S(1)}, u32[]{:S(2)}, u32[]{:S(2)}) collective-permute-start(f32[16,512]{1,0:T(8,128)S(1)} %add_add_fusion.1.refs_0_), channel_id=1, source_target_pairs={{0,12},{4,8},{8,4},{12,0},{16,28},{20,24},{24,20},{28,16},{1,13},{... | collective-permute-start | bytes 98312 | tf_op jit(solution)/shard_map/ppermute | solution.py:515
  18.5 3.9 %collective-permute-start.4 = (f32[16,512]{1,0:T(8,128)S(1)}, f32[16,512]{1,0:T(8,128)S(1)}, u32[]{:S(2)}, u32[]{:S(2)}) collective-permute-start(f32[16,512]{1,0:T(8,128)S(1)} %add_add_fusion.1.refs_0_), channel_id=1, source_target_pairs={{0,8},{4,12},{8,0},{12,4},{16,24},{20,28},{24,16},{28,20},{1,9},{5... | collective-permute-start | bytes 98312 | tf_op jit(solution)/shard_map/ppermute | solution.py:515
  18.9 3.9 %collective-permute-start.3 = (f32[16,512]{1,0:T(8,128)S(1)}, f32[16,512]{1,0:T(8,128)S(1)}, u32[]{:S(2)}, u32[]{:S(2)}) collective-permute-start(f32[16,512]{1,0:T(8,128)S(1)} %add_add_fusion.1.refs_0_), channel_id=1, source_target_pairs={{0,4},{4,0},{8,12},{12,8},{16,20},{20,16},{24,28},{28,24},{1,5},{5... | collective-permute-start | bytes 98312 | tf_op jit(solution)/shard_map/ppermute | solution.py:515
  22.9 13.2 %collective-permute-start.8 = (f32[64,640]{1,0:T(8,128)S(1)}, f32[64,640]{1,0:T(8,128)S(1)}, u32[]{:S(2)}, u32[]{:S(2)}) collective-permute-start(f32[64,640]{1,0:T(8,128)S(1)} %add.35), channel_id=1, source_target_pairs={{0,2},{1,18},{2,0},{3,16},{4,6},{5,22},{6,4},{7,20},{8,10},{9,26},... | collective-permute-start | bytes 491528 | tf_op jit(solution)/shard_map/ppermute | solution.py:543
  23.4 12.7 %collective-permute-start.7 = (f32[64,640]{1,0:T(8,128)S(1)}, f32[64,640]{1,0:T(8,128)S(1)}, u32[]{:S(2)}, u32[]{:S(2)}) collective-permute-start(f32[64,640]{1,0:T(8,128)S(1)} %add.35), channel_id=1, source_target_pairs={{1,16},{3,18},{5,20},{7,22},{9,24},{11,26},{13,28},{15,30},{16,1},... | collective-permute-start | bytes 491528 | tf_op jit(solution)/shard_map/ppermute | solution.py:543
  36.1 14.5 %collective-permute-start.11 = (f32[64,640]{1,0:T(8,128)S(1)}, f32[64,640]{1,0:T(8,128)S(1)}, u32[]{:S(2)}, u32[]{:S(2)}) collective-permute-start(f32[64,640]{1,0:T(8,128)S(1)} %add_add_fusion.refs_0_), channel_id=1, source_target_pairs={{0,12},{4,8},{8,4},{12,0},{16,28},{20,24},{24,20},{28,16},{1,13},{... | collective-permute-start | bytes 491528 | tf_op jit(solution)/shard_map/ppermute | solution.py:515
  37.8 12.9 %collective-permute-start.10 = (f32[64,640]{1,0:T(8,128)S(1)}, f32[64,640]{1,0:T(8,128)S(1)}, u32[]{:S(2)}, u32[]{:S(2)}) collective-permute-start(f32[64,640]{1,0:T(8,128)S(1)} %add_add_fusion.refs_0_), channel_id=1, source_target_pairs={{0,8},{4,12},{8,0},{12,4},{16,24},{20,28},{24,16},{28,20},{1,9},{5... | collective-permute-start | bytes 491528 | tf_op jit(solution)/shard_map/ppermute | solution.py:515
  38.2 12.5 %collective-permute-start.9 = (f32[64,640]{1,0:T(8,128)S(1)}, f32[64,640]{1,0:T(8,128)S(1)}, u32[]{:S(2)}, u32[]{:S(2)}) collective-permute-start(f32[64,640]{1,0:T(8,128)S(1)} %add_add_fusion.refs_0_), channel_id=1, source_target_pairs={{0,4},{4,0},{8,12},{12,8},{16,20},{20,16},{24,28},{28,24},{1,5},{5... | collective-permute-start | bytes 491528 | tf_op jit(solution)/shard_map/ppermute | solution.py:515
  51.8 6.2 %collective-permute-start.12 = (f32[256,256]{1,0:T(8,128)S(1)}, f32[256,256]{1,0:T(8,128)S(1)}, u32[]{:S(2)}, u32[]{:S(2)}) collective-permute-start(f32[256,256]{1,0:T(8,128)S(1)} %get-tuple-element.49.refs_0_), channel_id=1, source_target_pairs={{0,1},{1,0},{2,3},{3,2},{4,5},{5,4},{6,7},{7,6},{8,9},{9,8},{10,11... | collective-permute-start | bytes 786440 | tf_op jit(solution)/shard_map/ppermute | solution.py:515
  56.7 1.3 %collective-permute-start.13 = (f32[64,256]{1,0:T(8,128)S(1)}, f32[64,256]{1,0:T(8,128)S(1)}, u32[]{:S(2)}, u32[]{:S(2)}) collective-permute-start(f32[64,256]{1,0:T(8,128)S(1)} %get-tuple-element.50.refs_2_), channel_id=1, source_target_pairs={{0,1},{1,0},{2,3},{3,2},{4,5},{5,4},{6,7},{7,6},{8,9},{9,8},{10,11... | collective-permute-start | bytes 196616 | tf_op jit(solution)/shard_map/ppermute | solution.py:515
  58.0 12.1 %copy-start.1 = (f32[5,8192]{1,0:T(8,128)S(1)}, f32[5,8192]{1,0:T(8,128)}, u32[]{:S(2)}) copy-start(f32[5,8192]{1,0:T(8,128)} %amplitude_ref.3) | copy-start | bytes 491524
  58.0 12.1 %copy-start.2 = (s32[8192]{0:T(1024)S(1)}, s32[8192]{0:T(1024)}, u32[]{:S(2)}) copy-start(s32[8192]{0:T(1024)} %param.5) | copy-start | bytes 98308
  66.8 3.3 %collective-permute-start.14 = (f32[64,640]{1,0:T(8,128)S(1)}, f32[64,640]{1,0:T(8,128)S(1)}, u32[]{:S(2)}, u32[]{:S(2)}) collective-permute-start(f32[64,640]{1,0:T(8,128)S(1)} %top_and_root.1), channel_id=1, source_target_pairs={{0,1},{2,3},{4,5},{6,7},{8,9},{10,11},{12,13},{14,15},{17,16},{19,... | collective-permute-start | bytes 491528 | tf_op jit(solution)/shard_map/ppermute | solution.py:560
where the time goes:
time: 75 us; the launch traced here: 74.7 us
  Pallas kernels  43.8 us (58%)
  starting transfers between devices  23.3 us (31%)
  waiting for transfers between devices  5.44 us (7%)
  other arithmetic  1.77 us (2%)
    pallas_call x3, Pallas kernels, whole_call(): pl.pallas_call(kernel, in_specs=[vmem] * len(args), out_specs=[vmem] * le...  31.6 us
    ppermute x10, starting transfers between devices, swapped(): return lax.ppermute(value, axis, pairs)  16.1 us
    pallas_call x1, Pallas kernels, statistics(): pl.pallas_call(stats_kernel, grid=(obs // block,), in_specs=[pl.BlockSpec...  6.53 us
    ppermute x4, starting transfers between devices, sum_for_half(): total = total + lax.ppermute(value, ('region', 'obs'), pairs)  4.86 us
    pallas_call x1, Pallas kernels, fitted_fields(): pl.pallas_call(fitted_kernel, grid=(obs // block,), in_specs=[pl.BlockSpe...  4.61 us
    ppermute x10, waiting for transfers between devices, swapped(): return lax.ppermute(value, axis, pairs)  4.43 us
    ppermute x1, starting transfers between devices, spread_weights(): other = lax.ppermute(weights, ('region', 'obs'), pairs)  2.29 us
  transfers between devices with their start and end apart: 15, of which 6 were waited for; matrix products, arithmetic and copies ran while one was open for 2% of the time, Pallas kernels for 31%

commit v1 on v0

v1 whole, which is shorter than its diff:
```python
import functools

import jax
import jax.numpy as jnp
from jax import lax
from jax.experimental import pallas as pl
from jax.experimental.pallas import tpu as pltpu
from jax.sharding import PartitionSpec as P

highest = lax.Precision.HIGHEST
f32 = jnp.float32
bf16 = jnp.bfloat16
SUB = 8
vmem = pl.BlockSpec(memory_space=pltpu.VMEM)


def pair_index(tier, other):
    return tier * (tier + 1) // 2 + other


def dot(a, b):
    return jnp.dot(a, b, preferred_element_type=f32)


def dot_nt(a, b, precision=None):
    return lax.dot_general(
        a, b, (((1,), (1,)), ((), ())), precision=precision, preferred_element_type=f32
    )


def dot_tn(a, b):
    return lax.dot_general(
        a, b, (((0,), (0,)), ((), ())), precision=highest, preferred_element_type=f32
    )


def dot_hi(a, b):
    return jnp.dot(a, b, precision=highest, preferred_element_type=f32)


def split(value):
    high = value.astype(bf16)
    return high, (value - high.astype(f32)).astype(bf16)


def split3(value):
    high = value.astype(bf16)
    rest = value - high.astype(f32)
    middle = rest.astype(bf16)
    return high, middle, (rest - middle.astype(f32)).astype(bf16)


def one_hot(pattern_row, pattern_count):
    rows = lax.broadcasted_iota(jnp.int16, (pattern_count, pattern_row.shape[1]), 0)
    return jnp.where(rows == pattern_row.astype(jnp.int16), jnp.asarray(1, bf16), jnp.asarray(0, bf16))


def stats_kernel(pattern_ref, amplitude_ref, fields_ref, basis_ref, out_ref, prods, acc):
    step = pl.program_id(0)
    tier_count, pattern_count, knots = basis_ref.shape
    field_count = fields_ref.shape[0]
    pair_rows = prods.shape[0]
    amp = amplitude_ref[...]
    prods[...] = jnp.zeros_like(prods)
    for tier in range(tier_count):
        first = pair_index(tier, 0)
        prods[first:first + tier + 1, :] = amp[:tier + 1] * amp[tier:tier + 1]
    pair_parts = split3(prods[...])
    plain = fields_ref[...]
    field_rows = plain.astype(f32)
    shifted = amp - 1.0
    values = jnp.concatenate(
        [*pair_parts, plain]
        + [(field_rows * shifted[tier:tier + 1]).astype(bf16) for tier in range(tier_count)],
        axis=0,
    )
    part = dot_nt(values, one_hot(pattern_ref[...], pattern_count))

    @pl.when(step == 0)
    def _():
        acc[...] = part

    @pl.when(step > 0)
    def _():
        acc[...] += part

    @pl.when(step == pl.num_programs(0) - 1)
    def _():
        base = 3 * pair_rows
        out_ref[...] = jnp.zeros_like(out_ref)
        out_ref[:pair_rows, :pattern_count] = acc[:pair_rows] + (
            acc[pair_rows:2 * pair_rows] + acc[2 * pair_rows:base]
        )
        plain_sum = acc[base:base + field_count]
        for tier in range(tier_count):
            first = base + (tier + 1) * field_count
            high, low = split(plain_sum + acc[first:first + field_count])
            out_ref[pair_rows:, tier * knots:(tier + 1) * knots] = (
                dot(high, basis_ref[tier]) + dot(low, basis_ref[tier])
            )


def statistics(pattern, amplitude, fields, basis_table):
    tier_count, pattern_count, knots = basis_table.shape
    field_count, obs = fields.shape
    block = min(4096, obs)
    pair_rows = -(-pair_index(tier_count, 0) // 16) * 16
    rows = 3 * pair_rows + (1 + tier_count) * field_count
    width = max(pattern_count, tier_count * knots)
    return pl.pallas_call(
        stats_kernel,
        grid=(obs // block,),
        in_specs=[
            pl.BlockSpec((1, block), lambda i: (0, i)),
            pl.BlockSpec((tier_count, block), lambda i: (0, i)),
            pl.BlockSpec((field_count, block), lambda i: (0, i)),
            pl.BlockSpec(basis_table.shape, lambda i: (0, 0, 0)),
        ],
        out_specs=pl.BlockSpec((pair_rows + field_count, width), lambda i: (0, 0)),
        out_shape=pltpu.VMEM((pair_rows + field_count, width), f32),
        scratch_shapes=[
            pltpu.VMEM((pair_rows, block), f32),
            pltpu.VMEM((rows, pattern_count), f32),
        ],
        compiler_params=pltpu.CompilerParams(vmem_limit_bytes=58 * 2**20),
        cost_estimate=pl.CostEstimate(
            flops=2 * rows * pattern_count * obs, bytes_accessed=4 * 2**20, transcendentals=0
        ),
        name="statistics",
    )(pattern.reshape(1, obs), amplitude, fields, basis_table)


def along_rows(x, row):
    return jnp.broadcast_to(x[row:row + 1, :], x.shape)


def along_lanes(x, lane):
    return jnp.broadcast_to(x[:, lane:lane + 1], x.shape)


def tree_sum(values):
    while len(values) > 1:
        ends = values[len(values) - len(values) % 2:]
        values = [values[i] + values[i + 1] for i in range(0, len(values) - 1, 2)] + ends
    return values[0]


def sweep(rows, first, group, lane0, sub, lane):
    count, blocks, size = len(rows), len(rows[0]), SUB * group
    here = (lane >= lane0) & (lane < lane0 + size)
    columns, pivot = [], []
    for m in range(count):
        block = rows[m][first:first + group]
        columns.append([[along_lanes(b, lane0 + j) for b in block] for j in range(size)])
        pivot.append([
            jnp.where(here, (lane - lane0 - SUB * a == sub).astype(f32), b)
            for a, b in enumerate(block)
        ])
    for k in range(size):
        at, row = divmod(k, SUB)
        is_row = sub == row
        scale = [
            pltpu.reciprocal(along_rows(columns[m][k][at], row), approx=True) for m in range(count)
        ]

        def eliminated(parts, m):
            scaled = along_rows(parts[at], row) * scale[m]
            out = [part - c * scaled for part, c in zip(parts, columns[m][k])]
            out[at] = jnp.where(is_row, scaled, out[at])
            return out

        for j in range(k + 1, size):
            for m in range(count):
                columns[m][j] = eliminated(columns[m][j], m)
        for m in range(count):
            pivot[m] = eliminated(pivot[m], m)
    solved = [[along_rows(pivot[m][j // SUB], j % SUB) for j in range(size)] for m in range(count)]
    out = [list(r) for r in rows]
    for step in range(blocks - group):
        i = (first + group + step) % blocks
        for m in range(count):
            total = tree_sum([along_lanes(rows[m][i], lane0 + j) * solved[m][j] for j in range(size)])
            out[m][i] = jnp.where(here, 0.0, rows[m][i]) - total
    for m in range(count):
        out[m][first:first + group] = pivot[m]
    return out


def invert(refs, panel_refs, others=()):
    others = list(others)
    size = refs[0].shape[0]
    count = len(refs)
    panel, group = (min(64, size), 2) if count <= 2 else (min(32, size), 1)
    blocks = panel // SUB
    steps = size // (SUB * group)
    each = -(-len(others) // steps)
    sub = lax.broadcasted_iota(jnp.int32, (SUB, size), 0)
    lane = lax.broadcasted_iota(jnp.int32, (SUB, size), 1)
    wide = lax.broadcasted_iota(jnp.int32, (size, size), 1)
    for m in range(count):
        panel_refs[m][...] = jnp.zeros((size, size), f32)
    for p in range(size // panel):
        first = p * panel
        rows = [
            [refs[m][first + SUB * i:first + SUB * (i + 1), :] for i in range(blocks)]
            for m in range(count)
        ]
        for q in range(0, blocks, group):
            for work in others[:each]:
                work()
            others = others[each:]
            rows = sweep(rows, q, group, first + SUB * q, sub, lane)
        for m in range(count):
            if p > 0:
                panel_refs[m][first - panel:first, :] = jnp.zeros((panel, size), f32)
            for i in range(blocks):
                panel_refs[m][first + SUB * i:first + SUB * (i + 1), :] = rows[m][i]
        old = [refs[m][...] for m in range(count)]
        change = [dot_hi(old[m], panel_refs[m][...]) for m in range(count)]
        here = (wide >= first) & (wide < first + panel)
        for m in range(count):
            refs[m][...] = jnp.where(here, 0.0, old[m]) - change[m]
            for i in range(blocks):
                refs[m][first + SUB * i:first + SUB * (i + 1), :] = rows[m][i]


def diagonal(row):
    size = row.shape[1]
    rows = lax.broadcasted_iota(jnp.int32, (size, size), 0)
    columns = lax.broadcasted_iota(jnp.int32, (size, size), 1)
    return jnp.where(rows == columns, row, 0.0)


def gram_block(basis_ref, turned_ref, pairs, tier, other):
    turned = turned_ref[tier].astype(f32)
    index = pair_index(tier, other)
    parts = zip(*[split3(turned * pair[index:index + 1, :]) for pair in pairs])
    product = dot(jnp.concatenate(sum(parts, ()), axis=0), basis_ref[other])
    size = len(pairs) * turned.shape[0]
    return product[:size] + (product[size:2 * size] + product[2 * size:])


def update(target_ref, below, row_ref, coupling_ref):
    nodes, knots = row_ref.shape[:2]
    share = nodes // target_ref.shape[0]
    first, last = below * knots, (below + 1) * knots
    for n in range(target_ref.shape[0]):
        part = slice(n * share, (n + 1) * share)
        left = row_ref[part, :, first:last].reshape(share * knots, knots)
        right = coupling_ref[part, :, :last].reshape(share * knots, last)
        target_ref[n, :, :last] -= dot_tn(left, right)


def couple(row_ref, inverse_ref, coupling_ref):
    width = coupling_ref.shape[2]
    for n in range(inverse_ref.shape[0]):
        coupling_ref[n] = dot_hi(inverse_ref[n], row_ref[n, :, :width])


def leaf_kernel(basis_ref, turned_ref, prior_ref, *refs, top):
    tier = basis_ref.shape[0] - 1
    leaves = 2 ** (tier - top)
    slot_refs, refs = refs[:leaves], refs[leaves:]
    inverse_ref, coupling_ref, row_ref = refs[:3]
    lower_refs, rest_ref, panel_ref = refs[3:-2], refs[-2], refs[-1]
    knots = basis_ref.shape[2]
    pairs = [ref[...] for ref in slot_refs]
    prior = diagonal(prior_ref[tier:tier + 1, :])
    own = gram_block(basis_ref, turned_ref, pairs, tier, tier)
    for n in range(leaves):
        inverse_ref[n] = own[n * knots:(n + 1) * knots] + prior

    def gram(target_ref, pairs, below, other):
        block = gram_block(basis_ref, turned_ref, pairs, below, other)
        columns = slice(other * knots, (other + 1) * knots)
        for n in range(len(pairs)):
            target_ref[n, :, columns] = block[n * knots:(n + 1) * knots]

    others = [functools.partial(gram, row_ref, pairs, tier, other) for other in range(tier)]
    targets = list(lower_refs) + [rest_ref.at[pl.ds(below, 1)] for below in range(top - 1, -1, -1)]
    for target_ref, below in zip(targets, range(tier - 1, -1, -1)):
        if len(pairs) > 1:
            pairs = [pairs[2 * n] + pairs[2 * n + 1] for n in range(len(pairs) // 2)]
        others += [
            functools.partial(gram, target_ref, pairs, below, other) for other in range(below + 1)
        ]
    for below in range(top - 1):
        rest_ref[below, :, (below + 1) * knots:] = jnp.zeros((knots, (top - 1 - below) * knots), f32)
    invert(
        [inverse_ref.at[n] for n in range(leaves)], [panel_ref.at[n] for n in range(leaves)], others
    )
    couple(row_ref, inverse_ref, coupling_ref)
    update(targets[0], tier - 1, row_ref, coupling_ref)


def inner_kernel(*refs, top, count):
    row_ref, coupling_ref = refs[:2]
    row_refs, (rest_in, prior_ref), refs = refs[2:2 + count], refs[2 + count:4 + count], refs[4 + count:]
    inverse_refs, coupling_refs, refs = refs[:count], refs[count:2 * count], refs[2 * count:]
    rest_ref, panel_ref, work_refs = refs[0], refs[1], refs[2:]
    knots = prior_ref.shape[1]
    for work_ref, ref in zip(work_refs, row_refs):
        work_ref[...] = ref[...]
    rest_ref[...] = rest_in[...]
    targets = list(work_refs) + [rest_ref.at[pl.ds(below, 1)] for below in range(top - 1, -1, -1)]
    for i in range(count):
        tier = top + count - 1 - i
        nodes = work_refs[i].shape[0]
        prior = diagonal(prior_ref[tier:tier + 1, :])
        for n in range(nodes):
            inverse_refs[i][n] = work_refs[i][n, :, tier * knots:] + prior
        others = [
            functools.partial(update, targets[i + tier - below], below, row_ref, coupling_ref)
            for below in range(tier - 1, -1, -1)
        ]
        invert(
            [inverse_refs[i].at[n] for n in range(nodes)],
            [panel_ref.at[n] for n in range(nodes)],
            others,
        )
        couple(work_refs[i], inverse_refs[i], coupling_refs[i])
        row_ref, coupling_ref = work_refs[i], coupling_refs[i]
        if i + 1 < count:
            update(targets[i + 1], tier - 1, row_ref, coupling_ref)
    for below in range(top - 1, -1, -1):
        update(targets[count + top - 1 - below], below, row_ref, coupling_ref)


def whole_call(kernel, args, shapes, scratch, name, limit=8, flops=10**10):
    return pl.pallas_call(
        kernel,
        in_specs=[vmem] * len(args),
        out_specs=[vmem] * len(shapes),
        out_shape=[jax.ShapeDtypeStruct(shape, f32) for shape in shapes],
        scratch_shapes=[pltpu.VMEM(shape, f32) for shape in scratch],
        compiler_params=pltpu.CompilerParams(vmem_limit_bytes=limit * 2**20),
        cost_estimate=pl.CostEstimate(flops=flops, bytes_accessed=2**20, transcendentals=0),
        name=name,
    )(*args)


def leaf_tier(slots, basis_table, turned, prior_precision, top):
    tier_count, _, knots = basis_table.shape
    tier = tier_count - 1
    leaves = len(slots)
    shapes = [(leaves, knots, knots)] + [(leaves, knots, tier * knots)] * 2
    shapes += [(2 ** (t - top), knots, (t + 1) * knots) for t in range(tier - 1, top - 1, -1)]
    shapes.append((top, knots, top * knots))
    inverse, coupling, row, *lower, rest = whole_call(
        functools.partial(leaf_kernel, top=top),
        (basis_table, turned, prior_precision, *slots),
        shapes, [(leaves, knots, knots)], "leaf_tier", limit=16, flops=2 * 10**10,
    )
    return inverse, coupling, row, lower, rest


def inner_tiers(row, coupling, lower, rest, prior_precision, top):
    knots = prior_precision.shape[1]
    count = len(lower)
    nodes = [value.shape[0] for value in lower]
    shapes = [(n, knots, knots) for n in nodes]
    shapes += [(n, knots, value.shape[2] - knots) for n, value in zip(nodes, lower)]
    shapes.append(rest.shape)
    out = whole_call(
        functools.partial(inner_kernel, top=top, count=count),
        (row, coupling, *lower, rest, prior_precision),
        shapes, [(max(nodes), knots, knots)] + [value.shape for value in lower],
        "inner_tiers", limit=16, flops=2 * 10**10,
    )
    rest = out[-1].reshape(top * knots, top * knots)
    return list(out[:count]), list(out[count:-1]), rest


def forward_kernel(*refs, leaves):
    slot_refs, refs = refs[:leaves], refs[leaves:]
    out_refs = refs[-2:]
    coupling_refs = refs[:-2]
    knots = coupling_refs[0].shape[1]
    current = [ref[...] for ref in slot_refs]
    own = []
    for ref in coupling_refs:
        width = ref.shape[2]
        own.append(current[0][:, width:width + knots])
        reduced = [
            c[:, :width] - dot_hi(c[:, width:width + knots], ref[n]) for n, c in enumerate(current)
        ]
        current = (
            [reduced[2 * n] + reduced[2 * n + 1] for n in range(len(reduced) // 2)]
            if len(reduced) > 1 else reduced
        )
    out_refs[0][...] = current[0]
    out_refs[1][...] = jnp.concatenate(own, axis=1)


def forward(slots, couplings):
    fields = slots[0].shape[0]
    knots, width = couplings[-1].shape[1:]
    return pl.pallas_call(
        functools.partial(forward_kernel, leaves=len(slots)),
        in_specs=[vmem] * (len(slots) + len(couplings)),
        out_specs=[vmem] * 2,
        out_shape=[
            jax.ShapeDtypeStruct((fields, width), f32),
            jax.ShapeDtypeStruct((fields, knots * len(couplings)), f32),
        ],
        compiler_params=pltpu.CompilerParams(vmem_limit_bytes=8 * 2**20),
        name="forward",
    )(*slots, *couplings)


def top_step(total, prior_row, inverse_ref, panel_ref):
    knots = inverse_ref.shape[0]
    row = total[knots:]
    inverse_ref[...] = row[:, knots:] + diagonal(prior_row)
    invert([inverse_ref], [panel_ref])
    coupling = dot_hi(inverse_ref[...], row[:, :knots])
    return coupling, total[:knots, :knots] - dot_tn(row[:, :knots], coupling)


def root_step(schur, prior_row, inverse_ref, panel_ref):
    inverse_ref[...] = schur + diagonal(prior_row)
    invert([inverse_ref], [panel_ref])


def both_kernel(rest_ref, other_ref, prior_ref, top_ref, coupling_ref, root_ref, panel_ref):
    coupling_ref[...], schur = top_step(
        rest_ref[...] + other_ref[...], prior_ref[1:2, :], top_ref, panel_ref
    )
    root_step(schur, prior_ref[0:1, :], root_ref, panel_ref)


def top_kernel(rest_ref, other_ref, prior_ref, top_ref, coupling_ref, schur_ref, panel_ref):
    coupling_ref[...], schur_ref[...] = top_step(
        rest_ref[...] + other_ref[...], prior_ref[1:2, :], top_ref, panel_ref
    )


def root_kernel(schur_ref, prior_ref, root_ref, panel_ref):
    root_step(schur_ref[...], prior_ref[0:1, :], root_ref, panel_ref)


def right_kernel(right_ref, other_ref, coupling_ref, out_ref):
    knots = coupling_ref.shape[0]
    right = right_ref[...] + other_ref[...]
    out_ref[:, knots:] = right[:, knots:]
    out_ref[:, :knots] = right[:, :knots] - dot_hi(right[:, knots:], coupling_ref[...])


def path_step(path, right, inverse, coupling):
    local = dot_hi(right, inverse) - dot_nt(path, coupling, highest)
    return jnp.concatenate([path, local], axis=1)


def descend_kernel(right_ref, other_ref, top_ref, coupling_ref, root_ref, own_ref, *refs, reduced):
    refs, out_ref = refs[:-1], refs[-1]
    count = len(refs) // 2
    knots = top_ref.shape[0]
    right = right_ref[...]
    if reduced:
        root_right = right[:, :knots]
    else:
        right = right + other_ref[...]
        root_right = right[:, :knots] - dot_hi(right[:, knots:], coupling_ref[...])
    path = dot_hi(root_right, root_ref[...])
    path = path_step(path, right[:, knots:], top_ref[...], coupling_ref[...])
    for depth in range(count - 1, -1, -1):
        own = own_ref[:, depth * knots:(depth + 1) * knots]
        path = path_step(path, own, refs[depth][0], refs[count + depth][0])
    out_ref[...] = path


def path_weights(rest, right, own, prior_precision, inverses, couplings, leaves):
    knots = prior_precision.shape[1]
    fields = right.shape[0]
    square = (knots, knots)
    region_count = lax.axis_size("region")
    other_right = moved(right, leaves, (leaves // 2, 1), (leaves // 2, 1))
    ends = (rest, swapped(rest, "obs", 1), prior_precision)
    reduced = region_count > leaves
    if reduced:
        top, coupling, schur = whole_call(top_kernel, ends, [square] * 3, [square], "top")
        schur = sum_over(schur, "region", leaves, region_count)
        root = whole_call(root_kernel, (schur, prior_precision), [square], [square], "root")[0]
        right = whole_call(right_kernel, (right, other_right, coupling), [right.shape], [], "right")[0]
        other_right = sum_over(right[:, :knots], "region", leaves, region_count)
        right = jnp.concatenate([other_right, right[:, knots:]], axis=1)
    else:
        top, coupling, root = whole_call(both_kernel, ends, [square] * 3, [square], "top_and_root")
    args = (right, other_right, top, coupling, root, own, *inverses, *couplings)
    shape = (fields, prior_precision.shape[0] * knots)
    kernel = functools.partial(descend_kernel, reduced=reduced)
    return whole_call(kernel, args, [shape], [], "descend", flops=10**9)[0]


def fitted_kernel(pattern_ref, amplitude_ref, weight_ref, turned_ref, out_ref, table):
    tier_count, knots, pattern_count = turned_ref.shape
    field_count = weight_ref.shape[0]

    @pl.when(pl.program_id(0) == 0)
    def _():
        for tier in range(tier_count):
            high, low = split(weight_ref[:, tier * knots:(tier + 1) * knots])
            table[tier * field_count:(tier + 1) * field_count, :] = (
                dot(high, turned_ref[tier]) + dot(low, turned_ref[tier])
            ).astype(bf16)

    picked = dot(table[...], one_hot(pattern_ref[...], pattern_count))
    amp = amplitude_ref[...]
    total = picked[:field_count] * amp[0:1]
    for tier in range(1, tier_count):
        total = total + picked[tier * field_count:(tier + 1) * field_count] * amp[tier:tier + 1]
    out_ref[...] = total


def fitted_fields(pattern, amplitude, weights, turned):
    tier_count, knots, pattern_count = turned.shape
    obs = pattern.shape[0]
    field_count = weights.shape[0]
    block = min(2048, obs)
    return pl.pallas_call(
        fitted_kernel,
        grid=(obs // block,),
        in_specs=[
            pl.BlockSpec((1, block), lambda i: (0, i)),
            pl.BlockSpec((tier_count, block), lambda i: (0, i)),
            pl.BlockSpec(weights.shape, lambda i: (0, 0)),
            pl.BlockSpec(turned.shape, lambda i: (0, 0, 0)),
        ],
        out_specs=pl.BlockSpec((field_count, block), lambda i: (0, i)),
        out_shape=jax.ShapeDtypeStruct((field_count, obs), f32),
        scratch_shapes=[pltpu.VMEM((tier_count * field_count, pattern_count), bf16)],
        compiler_params=pltpu.CompilerParams(vmem_limit_bytes=16 * 2**20),
        name="fitted_fields",
    )(pattern.reshape(1, obs), amplitude, weights, turned)


def swapped(value, axis, mask):
    pairs = [(source, source ^ mask) for source in range(lax.axis_size(axis))]
    return lax.ppermute(value, axis, pairs)


def sum_over(value, axis, first_mask, size):
    mask = first_mask
    while mask < size:
        value = value + swapped(value, axis, mask)
        mask *= 2
    return value


def in_own_half(leaves):
    return (lax.axis_index("region") % leaves) // (leaves // 2) == lax.axis_index("obs") % 2


def moved(value, leaves, own_move, other_move):
    region_count, obs_count = lax.axis_size("region"), lax.axis_size("obs")
    pairs = []
    for region in range(region_count):
        for obs in range(obs_count):
            own = (region % leaves) // (leaves // 2) == obs % 2
            region_mask, obs_mask = own_move if own else other_move
            target = (region ^ region_mask) * obs_count + (obs ^ obs_mask)
            pairs.append((region * obs_count + obs, target))
    return lax.ppermute(value, ("region", "obs"), pairs)


def sum_for_half(value, leaves):
    half = leaves // 2
    parts = lax.axis_size("obs") // 2
    got = [
        moved(value, leaves, (0, 2 * max(offset, 1)), (half, 1 ^ 2 * offset))
        for offset in range(parts)
    ]
    own = value
    for part in got[1:]:
        own = own + part
    other = got[0]
    for part in got[1:]:
        other = other + part
    return jnp.where(in_own_half(leaves), own, other)


def gather_half(value, leaves):
    return [value] + [swapped(value, "region", offset) for offset in range(1, leaves // 2)]


def spread_weights(weights, leaves):
    return jnp.where(in_own_half(leaves), weights, swapped(weights, "obs", 1))


def shards(pattern, amplitude, basis_table, fields, prior_precision):
    tier_count = basis_table.shape[0]
    leaves = 2 ** (tier_count - 2)
    order = tier_count * basis_table.shape[2]
    turned = jnp.swapaxes(basis_table, 1, 2)
    sums = statistics(pattern, amplitude, fields, basis_table)
    pair_rows = sums.shape[0] - fields.shape[0]
    sums = sums + swapped(sums, "obs", 1)
    pairs, project = sums[:pair_rows, :basis_table.shape[1]], sums[pair_rows:, :order]
    pairs = sum_for_half(pairs, leaves)
    pair_slots = gather_half(pairs, leaves)
    pair_slots, project = lax.optimization_barrier((pair_slots, project))
    inverse, coupling, row, lower, rest = leaf_tier(
        pair_slots, basis_table, turned, prior_precision, 2
    )
    project = sum_over(project, "obs", 2, lax.axis_size("obs"))
    lower, rest, project = lax.optimization_barrier((lower, rest, project))
    inverses, couplings, rest = inner_tiers(row, coupling, lower, rest, prior_precision, 2)
    inverses, couplings = [inverse] + inverses, [coupling] + couplings
    project_slots = gather_half(project, leaves)
    right, own = forward(project_slots, couplings)
    rest, right = lax.optimization_barrier((rest, right))
    weights = path_weights(rest, right, own, prior_precision, inverses, couplings, leaves)
    weights = spread_weights(weights, leaves)
    return fitted_fields(pattern, amplitude, weights, turned)


def solution(mesh):
    return jax.shard_map(
        shards,
        mesh=mesh,
        in_specs=(
            P(("region", "obs")),
            P(None, ("region", "obs")),
            P(),
            P(None, ("region", "obs")),
            P(),
        ),
        out_specs=P(None, ("region", "obs")),
        check_vma=False,
    )
```

time: 75 us -> 67.9 us (0.905)
  starting transfers between devices: 23.3 us -> 14.9 us
  waiting for transfers between devices: 5.44 us -> 9.37 us
  other arithmetic: 1.77 us -> 0.08 us
  Pallas kernels: 43.8 us -> 42.9 us
    ppermute x10, starting transfers between devices: 16.1 us -> 8.89 us  [swapped(): return lax.ppermute(value, axis, pairs)]
    ppermute x5 -> x3, waiting for transfers between devices: 1.01 us -> 3.84 us  [moved(): return lax.ppermute(value, ('region', 'obs'), pairs)]
    add x4 -> x2, other arithmetic: 1.74 us -> 0.05 us  [the longest x1 0.03 us: shards(): sums = sums + swapped(sums, 'obs', 1)]
    ppermute x5 -> x3, starting transfers between devices: 7.15 us -> 5.99 us  [moved(): return lax.ppermute(value, ('region', 'obs'), pairs)]
    ppermute x10, waiting for transfers between devices: 4.43 us -> 5.53 us  [swapped(): return lax.ppermute(value, axis, pairs)]
    pallas_call x3 -> x4, Pallas kernels: 31.6 us -> 31.2 us  [whole_call(): pl.pallas_call(kernel, in_specs=[vmem] * len(args), out_specs=[vmem] * le...]
  transfers between devices with their start and end apart: 15 -> 13, of which waited for: 6 -> 7; matrix products, arithmetic and copies ran while one was open for 2% -> 0% of each run, Pallas kernels for 31% -> 44%
where the time goes in v1:
time: 67.9 us; the launch traced here: 67.7 us
  Pallas kernels  42.9 us (63%)
  starting transfers between devices  14.9 us (22%)
  waiting for transfers between devices  9.37 us (14%)
    pallas_call x4, Pallas kernels, whole_call(): pl.pallas_call(kernel, in_specs=[vmem] * len(args), out_specs=[vmem] * le...  31.2 us
    ppermute x10, starting transfers between devices, swapped(): return lax.ppermute(value, axis, pairs)  8.89 us
    pallas_call x1, Pallas kernels, statistics(): pl.pallas_call(stats_kernel, grid=(obs // block,), in_specs=[pl.BlockSpec...  6.03 us
    ppermute x3, starting transfers between devices, moved(): return lax.ppermute(value, ('region', 'obs'), pairs)  5.99 us
    ppermute x10, waiting for transfers between devices, swapped(): return lax.ppermute(value, axis, pairs)  5.53 us
    pallas_call x1, Pallas kernels, fitted_fields(): pl.pallas_call(fitted_kernel, grid=(obs // block,), in_specs=[pl.BlockSpe...  4.6 us
    ppermute x3, waiting for transfers between devices, moved(): return lax.ppermute(value, ('region', 'obs'), pairs)  3.84 us
  transfers between devices with their start and end apart: 13, of which 7 were waited for; matrix products, arithmetic and copies ran while one was open for 0% of the time, Pallas kernels for 44%

profile of v1, /device:TPU:0, one launch (start us, length us, event | category | flops | bytes accessed | tf_op | source)
XLA Modules:
  0.0 67.7 jit_solution(1113812999621494302)
XLA Ops:
  0.0 6.0 %statistics.1 = f32[80,640]{1,0:T(8,128)S(1)} custom-call(s32[1,8192]{1,0:T(1,128)} %bitcast.5, f32[5,8192]{1,0:T(8,128)} %amplitude_ref.3, bf16[64,8192]{1,0:T(8,128)(2,1)} %fields_ref.1, bf16[5,512,128]{2,1,0:T(8,128)(2,1)} %basis_ref.3), custom_call_target="tpu_custom_call" | custom-call | flops 3623878656 | bytes 4194304 | tf_op jit(solution)/shard_map/statistics/pallas_call | solution.py:110
  6.0 0.0 copy-start.3
  6.1 0.5 collective-permute-start
  6.6 1.1 %collective-permute-done = f32[80,640]{1,0:T(8,128)S(1)} collective-permute-done((f32[80,640]{1,0:T(8,128)S(1)}, f32[80,640]{1,0:T(8,128)S(1)}, u32[]{:S(2)}, u32[]{:S(2)}) %collective-permute-start) | collective-permute-done | bytes 204832 | tf_op jit(solution)/shard_map/ppermute | solution.py:539
  7.7 3.0 %collective-permute-start.2 = (f32[16,512]{1,0:T(8,128)S(1)}, f32[16,512]{1,0:T(8,128)S(1)}, u32[]{:S(2)}, u32[]{:S(2)}) collective-permute-start(f32[16,512]{1,0:T(8,128)S(1)} %slice.8), channel_id=1, source_target_pairs={{0,2},{1,16},{2,0},{3,18},{4,6},{5,20},{6,4},{7,22},{8,10},{9,24},... | collective-permute-start | bytes 98312 | tf_op jit(solution)/shard_map/ppermute | solution.py:563
  10.6 0.1 collective-permute-start.1
  10.7 1.8 %collective-permute-done.2 = f32[16,512]{1,0:T(8,128)S(1)} collective-permute-done((f32[16,512]{1,0:T(8,128)S(1)}, f32[16,512]{1,0:T(8,128)S(1)}, u32[]{:S(2)}, u32[]{:S(2)}) %collective-permute-start.2) | collective-permute-done | bytes 32800 | tf_op jit(solution)/shard_map/ppermute | solution.py:563
  12.5 2.0 %collective-permute-done.1 = f32[16,512]{1,0:T(8,128)S(1)} collective-permute-done((f32[16,512]{1,0:T(8,128)S(1)}, f32[16,512]{1,0:T(8,128)S(1)}, u32[]{:S(2)}, u32[]{:S(2)}) %collective-permute-start.1) | collective-permute-done | bytes 32800 | tf_op jit(solution)/shard_map/ppermute | solution.py:563
  14.6 2.6 %collective-permute-start.5 = (f32[16,512]{1,0:T(8,128)S(1)}, f32[16,512]{1,0:T(8,128)S(1)}, u32[]{:S(2)}, u32[]{:S(2)}) collective-permute-start(f32[16,512]{1,0:T(8,128)S(1)} %add_select_fusion.refs_0_), channel_id=1, source_target_pairs={{0,12},{4,8},{8,4},{12,0},{16,28},{20,24},{24,20},{28,16},{1,13},{... | collective-permute-start | bytes 98312 | tf_op jit(solution)/shard_map/ppermute | solution.py:539
  17.1 0.5 collective-permute-start.4
  17.6 0.5 collective-permute-start.3
  18.1 0.2 copy.6
  18.4 1.0 %collective-permute-done.5.refs_3_ = f32[16,512]{1,0:T(8,128)S(1)} collective-permute-done((f32[16,512]{1,0:T(8,128)S(1)}, f32[16,512]{1,0:T(8,128)S(1)}, u32[]{:S(2)}, u32[]{:S(2)}) %collective-permute-start.5) | collective-permute-done | bytes 32800 | tf_op jit(solution)/shard_map/ppermute | solution.py:539
  19.5 1.8 %collective-permute-done.4.refs_2_ = f32[16,512]{1,0:T(8,128)S(1)} collective-permute-done((f32[16,512]{1,0:T(8,128)S(1)}, f32[16,512]{1,0:T(8,128)S(1)}, u32[]{:S(2)}, u32[]{:S(2)}) %collective-permute-start.4) | collective-permute-done | bytes 32800 | tf_op jit(solution)/shard_map/ppermute | solution.py:539
  21.3 0.2 collective-permute-done.3.refs_1_
  21.5 0.5 collective-permute-start.6
  22.0 9.8 %leaf_tier.1 = (f32[4,128,128]{2,1,0:T(8,128)S(1)}, f32[4,128,512]{2,1,0:T(8,128)S(1)}, f32[4,128,512]{2,1,0:T(8,128)S(1)}, f32[2,128,512]{2,1,0:T(8,128)S(1)}, ...) custom-call(bf16[5,512,128]{2,1,0:T(8,128)(2,1)S(1)} %copy-done, bf16[5,128,512]{2,1,0:T(8,128)(2,1)S(1)} %bitcast.3, ...), custom_call_target="tpu_custom_call" | custom-call | flops 20000000000 | bytes 1048576 | tf_op jit(solution)/shard_map/leaf_tier/pallas_call | solution.py:330
  31.9 1.6 %collective-permute-start.9 = (f32[64,640]{1,0:T(8,128)S(1)}, f32[64,640]{1,0:T(8,128)S(1)}, u32[]{:S(2)}, u32[]{:S(2)}) collective-permute-start(f32[64,640]{1,0:T(8,128)S(1)} %add.27.refs_0_), channel_id=1, source_target_pairs={{0,12},{4,8},{8,4},{12,0},{16,28},{20,24},{24,20},{28,16},{1,13},{... | collective-permute-start | bytes 491528 | tf_op jit(solution)/shard_map/ppermute | solution.py:539
  33.5 0.3 collective-permute-start.8
  33.7 1.7 %collective-permute-start.7 = (f32[64,640]{1,0:T(8,128)S(1)}, f32[64,640]{1,0:T(8,128)S(1)}, u32[]{:S(2)}, u32[]{:S(2)}) collective-permute-start(f32[64,640]{1,0:T(8,128)S(1)} %add.27.refs_0_), channel_id=1, source_target_pairs={{0,4},{4,0},{8,12},{12,8},{16,20},{20,16},{24,28},{28,24},{1,5},{5... | collective-permute-start | bytes 491528 | tf_op jit(solution)/shard_map/ppermute | solution.py:539
  35.4 12.5 %inner_tiers.1 = (f32[2,128,128]{2,1,0:T(8,128)S(1)}, f32[1,128,128]{2,1,0:T(8,128)S(1)}, f32[2,128,384]{2,1,0:T(8,128)S(1)}, f32[1,128,256]{2,1,0:T(8,128)S(1)}, f32[2,128,256]{2,1,0:T(8,128)S(1)}) custom-call(f32[4,128,512]{2,1,0:T(8,128)S(1)} %get-tuple-element.36.refs_0_, f32[4,128,512]{2,1,0:T(8,128)S(1)} %get-tuple-element.37.refs_1_.refs_4_.refs_3_, ...), custom_call_target="tpu_custom_call" | custom-call | flops 20000000000 | bytes 1048576 | tf_op jit(solution)/shard_map/inner_tiers/pallas_call | solution.py:330
  47.9 1.1 %forward.1 = (f32[64,256]{1,0:T(8,128)S(1)}, f32[64,384]{1,0:T(8,128)S(1)}) custom-call(f32[64,640]{1,0:T(8,128)S(1)} %add.27.refs_0_, f32[64,640]{1,0:T(8,128)S(1)} %collective-permute-done.7.refs_1_, f32[64,640]{1,0:T(8,128)S(1)} %collective-permute-done.8.refs_2_, f32[64,640]{1,0:T(8,128)S(1)} %collective-permute-done.9.refs_3_, ...), custom_call_target="tpu_custom_call" | custom-call | tf_op jit(solution)/shard_map/forward/pallas_call | solution.py:398
  49.0 0.6 collective-permute-start.11
  49.7 3.0 %collective-permute-start.10 = (f32[64,256]{1,0:T(8,128)S(1)}, f32[64,256]{1,0:T(8,128)S(1)}, u32[]{:S(2)}, u32[]{:S(2)}) collective-permute-start(f32[64,256]{1,0:T(8,128)S(1)} %get-tuple-element.50.right_ref), channel_id=1, source_target_pairs={{0,17},{1,16},{2,19},{3,18},{4,21},{5,20},{6,23},{7,22},{8,25},{9,... | collective-permute-start | bytes 196616 | tf_op jit(solution)/shard_map/ppermute | solution.py:563
  52.6 7.2 %top_and_root.1 = (f32[128,128]{1,0:T(8,128)S(1)}, f32[128,128]{1,0:T(8,128)S(1)}, f32[128,128]{1,0:T(8,128)S(1)}) custom-call(f32[256,256]{1,0:T(8,128)S(1)} %bitcast.8, f32[256,256]{1,0:T(8,128)S(1)} %collective-permute-done.11.other_ref, f32[5,128]{1,0:T(8,128)S(1)} %copy-done.3), custom_call_target="tpu_custom_call" | custom-call | flops 10000000000 | bytes 1048576 | tf_op jit(solution)/shard_map/top_and_root/pallas_call | solution.py:330
  59.9 0.0 collective-permute-done.10.other_ref
  59.9 0.0 copy-start.1
  59.9 0.0 copy-start.2
  59.9 1.7 %descend.1 = f32[64,640]{1,0:T(8,128)S(1)} custom-call(f32[64,256]{1,0:T(8,128)S(1)} %get-tuple-element.50.right_ref, f32[64,256]{1,0:T(8,128)S(1)} %collective-permute-done.10.other_ref, f32[128,128]{1,0:T(8,128)S(1)} %get-tuple-element.52.top_ref, f32[128,128]{1,0:T(8,128)S(1)} %get-tuple-element.53.coupling_ref, ...), custom_call_target="tpu_custom_call" | custom-call | flops 1000000000 | bytes 1048576 | tf_op jit(solution)/shard_map/descend/pallas_call | solution.py:330
  61.6 0.1 collective-permute-start.12
  61.7 1.3 %collective-permute-done.12 = f32[64,640]{1,0:T(8,128)S(1)} collective-permute-done((f32[64,640]{1,0:T(8,128)S(1)}, f32[64,640]{1,0:T(8,128)S(1)}, u32[]{:S(2)}, u32[]{:S(2)}) %collective-permute-start.12) | collective-permute-done | bytes 163872 | tf_op jit(solution)/shard_map/ppermute | solution.py:539
  63.1 4.6 %fitted_fields.1 = f32[64,8192]{1,0:T(8,128)} custom-call(s32[1,8192]{1,0:T(1,128)S(1)} %bitcast.6, f32[5,8192]{1,0:T(8,128)S(1)} %copy-done.1, f32[64,640]{1,0:T(8,128)S(1)} %broadcast_select_fusion.weight_ref, bf16[5,128,512]{2,1,0:T(8,128)(2,1)S(1)} %bitcast.4), custom_call_target="tpu_custom_call" | custom-call | tf_op jit(solution)/shard_map/fitted_fields/pallas_call | solution.py:520
  (16 shorter events, 0.1 us)
Async XLA Ops:
  0.0 18.1 %copy-start = (bf16[5,512,128]{2,1,0:T(8,128)(2,1)S(1)}, bf16[5,512,128]{2,1,0:T(8,128)(2,1)}, u32[]{:S(2)}) copy-start(bf16[5,512,128]{2,1,0:T(8,128)(2,1)} %basis_ref.3) | copy-start | bytes 1966084
  6.0 16.0 %copy-start.3 = (f32[5,128]{1,0:T(8,128)S(1)}, f32[5,128]{1,0:T(8,128)}, u32[]{:S(2)}) copy-start(f32[5,128]{1,0:T(8,128)} %prior_ref.3) | copy-start | bytes 7684
  6.1 1.6 %collective-permute-start = (f32[80,640]{1,0:T(8,128)S(1)}, f32[80,640]{1,0:T(8,128)S(1)}, u32[]{:S(2)}, u32[]{:S(2)}) collective-permute-start(f32[80,640]{1,0:T(8,128)S(1)} %statistics.1), channel_id=1, source_target_pairs={{0,1},{1,0},{2,3},{3,2},{4,5},{5,4},{6,7},{7,6},{8,9},{9,8},{10,11... | collective-permute-start | bytes 614408 | tf_op jit(solution)/shard_map/ppermute | solution.py:539
  7.7 4.9 %collective-permute-start.2 = (f32[16,512]{1,0:T(8,128)S(1)}, f32[16,512]{1,0:T(8,128)S(1)}, u32[]{:S(2)}, u32[]{:S(2)}) collective-permute-start(f32[16,512]{1,0:T(8,128)S(1)} %slice.8), channel_id=1, source_target_pairs={{0,2},{1,16},{2,0},{3,18},{4,6},{5,20},{6,4},{7,22},{8,10},{9,24},... | collective-permute-start | bytes 98312 | tf_op jit(solution)/shard_map/ppermute | solution.py:563
  10.6 3.9 %collective-permute-start.1 = (f32[16,512]{1,0:T(8,128)S(1)}, f32[16,512]{1,0:T(8,128)S(1)}, u32[]{:S(2)}, u32[]{:S(2)}) collective-permute-start(f32[16,512]{1,0:T(8,128)S(1)} %slice.8), channel_id=1, source_target_pairs={{0,2},{1,18},{2,0},{3,16},{4,6},{5,22},{6,4},{7,20},{8,10},{9,26},... | collective-permute-start | bytes 98312 | tf_op jit(solution)/shard_map/ppermute | solution.py:563
  14.6 4.9 %collective-permute-start.5 = (f32[16,512]{1,0:T(8,128)S(1)}, f32[16,512]{1,0:T(8,128)S(1)}, u32[]{:S(2)}, u32[]{:S(2)}) collective-permute-start(f32[16,512]{1,0:T(8,128)S(1)} %add_select_fusion.refs_0_), channel_id=1, source_target_pairs={{0,12},{4,8},{8,4},{12,0},{16,28},{20,24},{24,20},{28,16},{1,13},{... | collective-permute-start | bytes 98312 | tf_op jit(solution)/shard_map/ppermute | solution.py:539
  17.1 4.1 %collective-permute-start.4 = (f32[16,512]{1,0:T(8,128)S(1)}, f32[16,512]{1,0:T(8,128)S(1)}, u32[]{:S(2)}, u32[]{:S(2)}) collective-permute-start(f32[16,512]{1,0:T(8,128)S(1)} %add_select_fusion.refs_0_), channel_id=1, source_target_pairs={{0,8},{4,12},{8,0},{12,4},{16,24},{20,28},{24,16},{28,20},{1,9},{5... | collective-permute-start | bytes 98312 | tf_op jit(solution)/shard_map/ppermute | solution.py:539
  17.6 3.9 %collective-permute-start.3 = (f32[16,512]{1,0:T(8,128)S(1)}, f32[16,512]{1,0:T(8,128)S(1)}, u32[]{:S(2)}, u32[]{:S(2)}) collective-permute-start(f32[16,512]{1,0:T(8,128)S(1)} %add_select_fusion.refs_0_), channel_id=1, source_target_pairs={{0,4},{4,0},{8,12},{12,8},{16,20},{20,16},{24,28},{28,24},{1,5},{5... | collective-permute-start | bytes 98312 | tf_op jit(solution)/shard_map/ppermute | solution.py:539
  21.5 10.3 %collective-permute-start.6 = (f32[64,640]{1,0:T(8,128)S(1)}, f32[64,640]{1,0:T(8,128)S(1)}, u32[]{:S(2)}, u32[]{:S(2)}) collective-permute-start(f32[64,640]{1,0:T(8,128)S(1)} %slice.9), channel_id=1, source_target_pairs={{0,2},{1,3},{2,0},{3,1},{4,6},{5,7},{6,4},{7,5},{8,10},{9,11},{10,... | collective-permute-start | bytes 491528 | tf_op jit(solution)/shard_map/ppermute | solution.py:539
  31.9 16.0 %collective-permute-start.9 = (f32[64,640]{1,0:T(8,128)S(1)}, f32[64,640]{1,0:T(8,128)S(1)}, u32[]{:S(2)}, u32[]{:S(2)}) collective-permute-start(f32[64,640]{1,0:T(8,128)S(1)} %add.27.refs_0_), channel_id=1, source_target_pairs={{0,12},{4,8},{8,4},{12,0},{16,28},{20,24},{24,20},{28,16},{1,13},{... | collective-permute-start | bytes 491528 | tf_op jit(solution)/shard_map/ppermute | solution.py:539
  33.5 14.5 %collective-permute-start.8 = (f32[64,640]{1,0:T(8,128)S(1)}, f32[64,640]{1,0:T(8,128)S(1)}, u32[]{:S(2)}, u32[]{:S(2)}) collective-permute-start(f32[64,640]{1,0:T(8,128)S(1)} %add.27.refs_0_), channel_id=1, source_target_pairs={{0,8},{4,12},{8,0},{12,4},{16,24},{20,28},{24,16},{28,20},{1,9},{5... | collective-permute-start | bytes 491528 | tf_op jit(solution)/shard_map/ppermute | solution.py:539
  33.7 14.2 %collective-permute-start.7 = (f32[64,640]{1,0:T(8,128)S(1)}, f32[64,640]{1,0:T(8,128)S(1)}, u32[]{:S(2)}, u32[]{:S(2)}) collective-permute-start(f32[64,640]{1,0:T(8,128)S(1)} %add.27.refs_0_), channel_id=1, source_target_pairs={{0,4},{4,0},{8,12},{12,8},{16,20},{20,16},{24,28},{28,24},{1,5},{5... | collective-permute-start | bytes 491528 | tf_op jit(solution)/shard_map/ppermute | solution.py:539
  49.0 3.6 %collective-permute-start.11 = (f32[256,256]{1,0:T(8,128)S(1)}, f32[256,256]{1,0:T(8,128)S(1)}, u32[]{:S(2)}, u32[]{:S(2)}) collective-permute-start(f32[256,256]{1,0:T(8,128)S(1)} %bitcast.7), channel_id=1, source_target_pairs={{0,1},{1,0},{2,3},{3,2},{4,5},{5,4},{6,7},{7,6},{8,9},{9,8},{10,11... | collective-permute-start | bytes 786440 | tf_op jit(solution)/shard_map/ppermute | solution.py:539
  49.7 10.2 %collective-permute-start.10 = (f32[64,256]{1,0:T(8,128)S(1)}, f32[64,256]{1,0:T(8,128)S(1)}, u32[]{:S(2)}, u32[]{:S(2)}) collective-permute-start(f32[64,256]{1,0:T(8,128)S(1)} %get-tuple-element.50.right_ref), channel_id=1, source_target_pairs={{0,17},{1,16},{2,19},{3,18},{4,21},{5,20},{6,23},{7,22},{8,25},{9,... | collective-permute-start | bytes 196616 | tf_op jit(solution)/shard_map/ppermute | solution.py:563
  59.9 3.2 %copy-start.1 = (f32[5,8192]{1,0:T(8,128)S(1)}, f32[5,8192]{1,0:T(8,128)}, u32[]{:S(2)}) copy-start(f32[5,8192]{1,0:T(8,128)} %amplitude_ref.3) | copy-start | bytes 491524
  59.9 3.2 %copy-start.2 = (s32[8192]{0:T(1024)S(1)}, s32[8192]{0:T(1024)}, u32[]{:S(2)}) copy-start(s32[8192]{0:T(1024)} %param.5) | copy-start | bytes 98308
  61.6 1.5 %collective-permute-start.12 = (f32[64,640]{1,0:T(8,128)S(1)}, f32[64,640]{1,0:T(8,128)S(1)}, u32[]{:S(2)}, u32[]{:S(2)}) collective-permute-start(f32[64,640]{1,0:T(8,128)S(1)} %descend.1), channel_id=1, source_target_pairs={{0,1},{1,0},{2,3},{3,2},{4,5},{5,4},{6,7},{7,6},{8,9},{9,8},{10,11... | collective-permute-start | bytes 491528 | tf_op jit(solution)/shard_map/ppermute | solution.py:539

commit v2 on v1

--- a/solution.py
+++ b/solution.py
@@ -12,6 +12,7 @@
 bf16 = jnp.bfloat16
 SUB = 8
 vmem = pl.BlockSpec(memory_space=pltpu.VMEM)
+PANELS = {1: (64, 2), 2: (32, 2)}
 
 
 def pair_index(tier, other):
@@ -103,7 +104,7 @@
 def statistics(pattern, amplitude, fields, basis_table):
     tier_count, pattern_count, knots = basis_table.shape
     field_count, obs = fields.shape
-    block = min(4096, obs)
+    block = min(8192, obs)
     pair_rows = -(-pair_index(tier_count, 0) // 16) * 16
     rows = 3 * pair_rows + (1 + tier_count) * field_count
     width = max(pattern_count, tier_count * knots)
@@ -190,7 +191,8 @@
     others = list(others)
     size = refs[0].shape[0]
     count = len(refs)
-    panel, group = (min(64, size), 2) if count <= 2 else (min(32, size), 1)
+    panel, group = PANELS.get(count, (16, 1))
+    panel = min(panel, size)
     blocks = panel // SUB
     steps = size // (SUB * group)
     each = -(-len(others) // steps)
@@ -408,11 +410,37 @@
     )(*slots, *couplings)
 
 
-def top_step(total, prior_row, inverse_ref, panel_ref):
+def composites(own_ref, refs, local_ref, deep_ref):
+    count = len(refs) // 2
+    inverse_refs, coupling_refs = refs[:count], refs[count:]
+    knots = inverse_refs[0].shape[1]
+    wide = deep_ref.shape[1]
+
+    def solve(depth):
+        place = slice((count - 1 - depth) * knots, (count - depth) * knots)
+        own = own_ref[:, depth * knots:(depth + 1) * knots]
+        local_ref[:, place] = dot_hi(own, inverse_refs[depth][0])
+
+    def shorten(depth):
+        first = (count - 1 - depth) * knots
+        deep = coupling_refs[depth][0, :, :wide]
+        if first > 0:
+            between = coupling_refs[depth][0, :, wide:]
+            deep = deep - dot_hi(between, deep_ref[:first, :])
+            local_ref[:, first:first + knots] -= dot_nt(local_ref[:, :first], between, highest)
+        deep_ref[first:first + knots, :] = deep
+
+    depths = range(count - 1, -1, -1)
+    return [functools.partial(solve, d) for d in depths] + [
+        functools.partial(shorten, d) for d in depths
+    ]
+
+
+def top_step(total, prior_row, inverse_ref, panel_ref, others):
     knots = inverse_ref.shape[0]
     row = total[knots:]
     inverse_ref[...] = row[:, knots:] + diagonal(prior_row)
-    invert([inverse_ref], [panel_ref])
+    invert([inverse_ref], [panel_ref], others)
     coupling = dot_hi(inverse_ref[...], row[:, :knots])
     return coupling, total[:knots, :knots] - dot_tn(row[:, :knots], coupling)
 
@@ -422,17 +450,17 @@
     invert([inverse_ref], [panel_ref])
 
 
-def both_kernel(rest_ref, other_ref, prior_ref, top_ref, coupling_ref, root_ref, panel_ref):
+def top_kernel(rest_ref, other_ref, prior_ref, own_ref, *refs, both):
+    refs, outs = refs[:-6], refs[-6:]
+    local_ref, deep_ref, top_ref, coupling_ref, last_ref, panel_ref = outs
     coupling_ref[...], schur = top_step(
-        rest_ref[...] + other_ref[...], prior_ref[1:2, :], top_ref, panel_ref
-    )
-    root_step(schur, prior_ref[0:1, :], root_ref, panel_ref)
-
-
-def top_kernel(rest_ref, other_ref, prior_ref, top_ref, coupling_ref, schur_ref, panel_ref):
-    coupling_ref[...], schur_ref[...] = top_step(
-        rest_ref[...] + other_ref[...], prior_ref[1:2, :], top_ref, panel_ref
-    )
+        rest_ref[...] + other_ref[...], prior_ref[1:2, :], top_ref, panel_ref,
+        composites(own_ref, refs, local_ref, deep_ref),
+    )
+    if both:
+        root_step(schur, prior_ref[0:1, :], last_ref, panel_ref)
+    else:
+        last_ref[...] = schur
 
 
 def root_kernel(schur_ref, prior_ref, root_ref, panel_ref):
@@ -446,14 +474,8 @@
     out_ref[:, :knots] = right[:, :knots] - dot_hi(right[:, knots:], coupling_ref[...])
 
 
-def path_step(path, right, inverse, coupling):
-    local = dot_hi(right, inverse) - dot_nt(path, coupling, highest)
-    return jnp.concatenate([path, local], axis=1)
-
-
-def descend_kernel(right_ref, other_ref, top_ref, coupling_ref, root_ref, own_ref, *refs, reduced):
-    refs, out_ref = refs[:-1], refs[-1]
-    count = len(refs) // 2
+def descend_kernel(right_ref, other_ref, top_ref, coupling_ref, root_ref, local_ref, deep_ref,
+                   out_ref, *, reduced):
     knots = top_ref.shape[0]
     right = right_ref[...]
     if reduced:
@@ -461,12 +483,11 @@
     else:
         right = right + other_ref[...]
         root_right = right[:, :knots] - dot_hi(right[:, knots:], coupling_ref[...])
-    path = dot_hi(root_right, root_ref[...])
-    path = path_step(path, right[:, knots:], top_ref[...], coupling_ref[...])
-    for depth in range(count - 1, -1, -1):
-        own = own_ref[:, depth * knots:(depth + 1) * knots]
-        path = path_step(path, own, refs[depth][0], refs[count + depth][0])
-    out_ref[...] = path
+    first = dot_hi(root_right, root_ref[...])
+    second = dot_hi(right[:, knots:], top_ref[...]) - dot_nt(first, coupling_ref[...], highest)
+    tops = jnp.concatenate([first, second], axis=1)
+    out_ref[:, :2 * knots] = tops
+    out_ref[:, 2 * knots:] = local_ref[...] - dot_nt(tops, deep_ref[...], highest)
 
 
 def path_weights(rest, right, own, prior_precision, inverses, couplings, leaves):
@@ -475,18 +496,19 @@
     square = (knots, knots)
     region_count = lax.axis_size("region")
     other_right = moved(right, leaves, (leaves // 2, 1), (leaves // 2, 1))
-    ends = (rest, swapped(rest, "obs", 1), prior_precision)
     reduced = region_count > leaves
+    args = (rest, swapped(rest, "obs", 1), prior_precision, own, *inverses, *couplings)
+    shapes = [(fields, own.shape[1]), (own.shape[1], 2 * knots), square, square, square]
+    local, deep, top, coupling, root = whole_call(
+        functools.partial(top_kernel, both=not reduced), args, shapes, [square], "top"
+    )
     if reduced:
-        top, coupling, schur = whole_call(top_kernel, ends, [square] * 3, [square], "top")
-        schur = sum_over(schur, "region", leaves, region_count)
+        schur = sum_over(root, "region", leaves, region_count)
         root = whole_call(root_kernel, (schur, prior_precision), [square], [square], "root")[0]
         right = whole_call(right_kernel, (right, other_right, coupling), [right.shape], [], "right")[0]
         other_right = sum_over(right[:, :knots], "region", leaves, region_count)
         right = jnp.concatenate([other_right, right[:, knots:]], axis=1)
-    else:
-        top, coupling, root = whole_call(both_kernel, ends, [square] * 3, [square], "top_and_root")
-    args = (right, other_right, top, coupling, root, own, *inverses, *couplings)
+    args = (right, other_right, top, coupling, root, local, deep)
     shape = (fields, prior_precision.shape[0] * knots)
     kernel = functools.partial(descend_kernel, reduced=reduced)
     return whole_call(kernel, args, [shape], [], "descend", flops=10**9)[0]
@@ -516,7 +538,7 @@
     tier_count, knots, pattern_count = turned.shape
     obs = pattern.shape[0]
     field_count = weights.shape[0]
-    block = min(2048, obs)
+    block = min(4096, obs)
     return pl.pallas_call(
         fitted_kernel,
         grid=(obs // block,),

time: 67.9 us -> 64.6 us (0.951)
  Pallas kernels: 42.9 us -> 39.7 us
    pallas_call x4, Pallas kernels: 31.2 us -> 28.3 us  [whole_call(): pl.pallas_call(kernel, in_specs=[vmem] * len(args), out_specs=[vmem] * le...]
  transfers between devices with their start and end apart: 13 -> 13, of which waited for: 7 -> 7; matrix products, arithmetic and copies ran while one was open for 0% -> 0% of each run, Pallas kernels for 44% -> 42%
where the time goes in v2:
time: 64.6 us; the launch traced here: 64.5 us
  Pallas kernels  39.7 us (61%)
  starting transfers between devices  14.9 us (23%)
  waiting for transfers between devices  9.37 us (15%)
    pallas_call x4, Pallas kernels, whole_call(): pl.pallas_call(kernel, in_specs=[vmem] * len(args), out_specs=[vmem] * le...  28.3 us
    ppermute x10, starting transfers between devices, swapped(): return lax.ppermute(value, axis, pairs)  8.92 us
    ppermute x3, starting transfers between devices, moved(): return lax.ppermute(value, ('region', 'obs'), pairs)  5.97 us
    pallas_call x1, Pallas kernels, statistics(): pl.pallas_call(stats_kernel, grid=(obs // block,), in_specs=[pl.BlockSpec...  5.89 us
    ppermute x10, waiting for transfers between devices, swapped(): return lax.ppermute(value, axis, pairs)  5.53 us
    pallas_call x1, Pallas kernels, fitted_fields(): pl.pallas_call(fitted_kernel, grid=(obs // block,), in_specs=[pl.BlockSpe...  4.41 us
    ppermute x3, waiting for transfers between devices, moved(): return lax.ppermute(value, ('region', 'obs'), pairs)  3.84 us
  transfers between devices with their start and end apart: 13, of which 7 were waited for; matrix products, arithmetic and copies ran while one was open for 0% of the time, Pallas kernels for 42%

profile of v2, /device:TPU:0, one launch (start us, length us, event | category | flops | bytes accessed | tf_op | source)
XLA Modules:
  0.0 64.5 jit_solution(16365873619100287220)
XLA Ops:
  0.0 5.9 %statistics.1 = f32[80,640]{1,0:T(8,128)S(1)} custom-call(s32[1,8192]{1,0:T(1,128)} %bitcast.5, f32[5,8192]{1,0:T(8,128)} %amplitude_ref.3, bf16[64,8192]{1,0:T(8,128)(2,1)} %fields_ref.1, bf16[5,512,128]{2,1,0:T(8,128)(2,1)} %basis_ref.3), custom_call_target="tpu_custom_call" | custom-call | flops 3623878656 | bytes 4194304 | tf_op jit(solution)/shard_map/statistics/pallas_call | solution.py:111
  5.9 0.0 copy-start.3
  5.9 0.5 collective-permute-start
  6.4 1.1 %collective-permute-done = f32[80,640]{1,0:T(8,128)S(1)} collective-permute-done((f32[80,640]{1,0:T(8,128)S(1)}, f32[80,640]{1,0:T(8,128)S(1)}, u32[]{:S(2)}, u32[]{:S(2)}) %collective-permute-start) | collective-permute-done | bytes 204832 | tf_op jit(solution)/shard_map/ppermute | solution.py:561
  7.5 3.0 %collective-permute-start.2 = (f32[16,512]{1,0:T(8,128)S(1)}, f32[16,512]{1,0:T(8,128)S(1)}, u32[]{:S(2)}, u32[]{:S(2)}) collective-permute-start(f32[16,512]{1,0:T(8,128)S(1)} %slice.8), channel_id=1, source_target_pairs={{0,2},{1,16},{2,0},{3,18},{4,6},{5,20},{6,4},{7,22},{8,10},{9,24},... | collective-permute-start | bytes 98312 | tf_op jit(solution)/shard_map/ppermute | solution.py:585
  10.5 0.1 collective-permute-start.1
  10.6 1.8 %collective-permute-done.2 = f32[16,512]{1,0:T(8,128)S(1)} collective-permute-done((f32[16,512]{1,0:T(8,128)S(1)}, f32[16,512]{1,0:T(8,128)S(1)}, u32[]{:S(2)}, u32[]{:S(2)}) %collective-permute-start.2) | collective-permute-done | bytes 32800 | tf_op jit(solution)/shard_map/ppermute | solution.py:585
  12.4 2.0 %collective-permute-done.1 = f32[16,512]{1,0:T(8,128)S(1)} collective-permute-done((f32[16,512]{1,0:T(8,128)S(1)}, f32[16,512]{1,0:T(8,128)S(1)}, u32[]{:S(2)}, u32[]{:S(2)}) %collective-permute-start.1) | collective-permute-done | bytes 32800 | tf_op jit(solution)/shard_map/ppermute | solution.py:585
  14.4 2.6 %collective-permute-start.5 = (f32[16,512]{1,0:T(8,128)S(1)}, f32[16,512]{1,0:T(8,128)S(1)}, u32[]{:S(2)}, u32[]{:S(2)}) collective-permute-start(f32[16,512]{1,0:T(8,128)S(1)} %add_select_fusion.refs_0_), channel_id=1, source_target_pairs={{0,12},{4,8},{8,4},{12,0},{16,28},{20,24},{24,20},{28,16},{1,13},{... | collective-permute-start | bytes 98312 | tf_op jit(solution)/shard_map/ppermute | solution.py:561
  17.0 0.4 collective-permute-start.4
  17.4 0.5 collective-permute-start.3
  18.0 0.2 copy.6
  18.3 1.0 %collective-permute-done.5.refs_3_ = f32[16,512]{1,0:T(8,128)S(1)} collective-permute-done((f32[16,512]{1,0:T(8,128)S(1)}, f32[16,512]{1,0:T(8,128)S(1)}, u32[]{:S(2)}, u32[]{:S(2)}) %collective-permute-start.5) | collective-permute-done | bytes 32800 | tf_op jit(solution)/shard_map/ppermute | solution.py:561
  19.3 1.8 %collective-permute-done.4.refs_2_ = f32[16,512]{1,0:T(8,128)S(1)} collective-permute-done((f32[16,512]{1,0:T(8,128)S(1)}, f32[16,512]{1,0:T(8,128)S(1)}, u32[]{:S(2)}, u32[]{:S(2)}) %collective-permute-start.4) | collective-permute-done | bytes 32800 | tf_op jit(solution)/shard_map/ppermute | solution.py:561
  21.1 0.2 collective-permute-done.3.refs_1_
  21.4 0.5 collective-permute-start.6
  21.9 9.8 %leaf_tier.1 = (f32[4,128,128]{2,1,0:T(8,128)S(1)}, f32[4,128,512]{2,1,0:T(8,128)S(1)}, f32[4,128,512]{2,1,0:T(8,128)S(1)}, f32[2,128,512]{2,1,0:T(8,128)S(1)}, ...) custom-call(bf16[5,512,128]{2,1,0:T(8,128)(2,1)S(1)} %copy-done, bf16[5,128,512]{2,1,0:T(8,128)(2,1)S(1)} %bitcast.3, ...), custom_call_target="tpu_custom_call" | custom-call | flops 20000000000 | bytes 1048576 | tf_op jit(solution)/shard_map/leaf_tier/pallas_call | solution.py:332
  31.7 1.6 %collective-permute-start.9 = (f32[64,640]{1,0:T(8,128)S(1)}, f32[64,640]{1,0:T(8,128)S(1)}, u32[]{:S(2)}, u32[]{:S(2)}) collective-permute-start(f32[64,640]{1,0:T(8,128)S(1)} %add.27.refs_0_), channel_id=1, source_target_pairs={{0,12},{4,8},{8,4},{12,0},{16,28},{20,24},{24,20},{28,16},{1,13},{... | collective-permute-start | bytes 491528 | tf_op jit(solution)/shard_map/ppermute | solution.py:561
  33.4 0.3 collective-permute-start.8
  33.6 1.6 %collective-permute-start.7 = (f32[64,640]{1,0:T(8,128)S(1)}, f32[64,640]{1,0:T(8,128)S(1)}, u32[]{:S(2)}, u32[]{:S(2)}) collective-permute-start(f32[64,640]{1,0:T(8,128)S(1)} %add.27.refs_0_), channel_id=1, source_target_pairs={{0,4},{4,0},{8,12},{12,8},{16,20},{20,16},{24,28},{28,24},{1,5},{5... | collective-permute-start | bytes 491528 | tf_op jit(solution)/shard_map/ppermute | solution.py:561
  35.3 9.9 %inner_tiers.1 = (f32[2,128,128]{2,1,0:T(8,128)S(1)}, f32[1,128,128]{2,1,0:T(8,128)S(1)}, f32[2,128,384]{2,1,0:T(8,128)S(1)}, f32[1,128,256]{2,1,0:T(8,128)S(1)}, f32[2,128,256]{2,1,0:T(8,128)S(1)}) custom-call(f32[4,128,512]{2,1,0:T(8,128)S(1)} %get-tuple-element.38.refs_0_, f32[4,128,512]{2,1,0:T(8,128)S(1)} %get-tuple-element.39.refs_1_.refs_4_.refs_3_, ...), custom_call_target="tpu_custom_call" | custom-call | flops 20000000000 | bytes 1048576 | tf_op jit(solution)/shard_map/inner_tiers/pallas_call | solution.py:332
  45.3 1.1 %forward.1 = (f32[64,256]{1,0:T(8,128)S(1)}, f32[64,384]{1,0:T(8,128)S(1)}) custom-call(f32[64,640]{1,0:T(8,128)S(1)} %add.27.refs_0_, f32[64,640]{1,0:T(8,128)S(1)} %collective-permute-done.7.refs_1_, f32[64,640]{1,0:T(8,128)S(1)} %collective-permute-done.8.refs_2_, f32[64,640]{1,0:T(8,128)S(1)} %collective-permute-done.9.refs_3_, ...), custom_call_target="tpu_custom_call" | custom-call | tf_op jit(solution)/shard_map/forward/pallas_call | solution.py:400
  46.4 0.7 %collective-permute-start.11 = (f32[256,256]{1,0:T(8,128)S(1)}, f32[256,256]{1,0:T(8,128)S(1)}, u32[]{:S(2)}, u32[]{:S(2)}) collective-permute-start(f32[256,256]{1,0:T(8,128)S(1)} %bitcast.7), channel_id=1, source_target_pairs={{0,1},{1,0},{2,3},{3,2},{4,5},{5,4},{6,7},{7,6},{8,9},{9,8},{10,11... | collective-permute-start | bytes 786440 | tf_op jit(solution)/shard_map/ppermute | solution.py:561
  47.1 2.9 %collective-permute-start.10 = (f32[64,256]{1,0:T(8,128)S(1)}, f32[64,256]{1,0:T(8,128)S(1)}, u32[]{:S(2)}, u32[]{:S(2)}) collective-permute-start(f32[64,256]{1,0:T(8,128)S(1)} %get-tuple-element.52.right_ref), channel_id=1, source_target_pairs={{0,17},{1,16},{2,19},{3,18},{4,21},{5,20},{6,23},{7,22},{8,25},{9,... | collective-permute-start | bytes 196616 | tf_op jit(solution)/shard_map/ppermute | solution.py:585
  50.0 7.4 %top.1 = (f32[64,384]{1,0:T(8,128)S(1)}, f32[384,256]{1,0:T(8,128)S(1)}, f32[128,128]{1,0:T(8,128)S(1)}, f32[128,128]{1,0:T(8,128)S(1)}, f32[128,128]{1,0:T(8,128)S(1)}) custom-call(f32[256,256]{1,0:T(8,128)S(1)} %bitcast.8, f32[256,256]{1,0:T(8,128)S(1)} %collective-permute-done.11.other_ref, f32[5,128]{1,0:T(8,128)S(1)} %copy-done.3, ...), custom_call_target="tpu_custom_call" | custom-call | flops 10000000000 | bytes 1048576 | tf_op jit(solution)/shard_map/top/pallas_call | solution.py:332
  57.4 0.0 collective-permute-done.10.other_ref
  57.4 0.0 copy-start.1
  57.4 0.0 copy-start.2
  57.4 1.1 %descend.1 = f32[64,640]{1,0:T(8,128)S(1)} custom-call(f32[64,256]{1,0:T(8,128)S(1)} %get-tuple-element.52.right_ref, f32[64,256]{1,0:T(8,128)S(1)} %collective-permute-done.10.other_ref, f32[128,128]{1,0:T(8,128)S(1)} %get-tuple-element.58.top_ref, f32[128,128]{1,0:T(8,128)S(1)} %get-tuple-element.59.coupling_ref, ...), custom_call_target="tpu_custom_call" | custom-call | flops 1000000000 | bytes 1048576 | tf_op jit(solution)/shard_map/descend/pallas_call | solution.py:332
  58.6 0.1 collective-permute-start.12
  58.7 1.3 %collective-permute-done.12 = f32[64,640]{1,0:T(8,128)S(1)} collective-permute-done((f32[64,640]{1,0:T(8,128)S(1)}, f32[64,640]{1,0:T(8,128)S(1)}, u32[]{:S(2)}, u32[]{:S(2)}) %collective-permute-start.12) | collective-permute-done | bytes 163872 | tf_op jit(solution)/shard_map/ppermute | solution.py:561
  60.1 4.4 %fitted_fields.1 = f32[64,8192]{1,0:T(8,128)} custom-call(s32[1,8192]{1,0:T(1,128)S(1)} %bitcast.6, f32[5,8192]{1,0:T(8,128)S(1)} %copy-done.1, f32[64,640]{1,0:T(8,128)S(1)} %broadcast_select_fusion.weight_ref, bf16[5,128,512]{2,1,0:T(8,128)(2,1)S(1)} %bitcast.4), custom_call_target="tpu_custom_call" | custom-call | tf_op jit(solution)/shard_map/fitted_fields/pallas_call | solution.py:542
  (16 shorter events, 0.1 us)
Async XLA Ops:
  0.0 18.0 %copy-start = (bf16[5,512,128]{2,1,0:T(8,128)(2,1)S(1)}, bf16[5,512,128]{2,1,0:T(8,128)(2,1)}, u32[]{:S(2)}) copy-start(bf16[5,512,128]{2,1,0:T(8,128)(2,1)} %basis_ref.3) | copy-start | bytes 1966084
  5.9 16.0 %copy-start.3 = (f32[5,128]{1,0:T(8,128)S(1)}, f32[5,128]{1,0:T(8,128)}, u32[]{:S(2)}) copy-start(f32[5,128]{1,0:T(8,128)} %prior_ref.3) | copy-start | bytes 7684
  5.9 1.6 %collective-permute-start = (f32[80,640]{1,0:T(8,128)S(1)}, f32[80,640]{1,0:T(8,128)S(1)}, u32[]{:S(2)}, u32[]{:S(2)}) collective-permute-start(f32[80,640]{1,0:T(8,128)S(1)} %statistics.1), channel_id=1, source_target_pairs={{0,1},{1,0},{2,3},{3,2},{4,5},{5,4},{6,7},{7,6},{8,9},{9,8},{10,11... | collective-permute-start | bytes 614408 | tf_op jit(solution)/shard_map/ppermute | solution.py:561
  7.5 4.8 %collective-permute-start.2 = (f32[16,512]{1,0:T(8,128)S(1)}, f32[16,512]{1,0:T(8,128)S(1)}, u32[]{:S(2)}, u32[]{:S(2)}) collective-permute-start(f32[16,512]{1,0:T(8,128)S(1)} %slice.8), channel_id=1, source_target_pairs={{0,2},{1,16},{2,0},{3,18},{4,6},{5,20},{6,4},{7,22},{8,10},{9,24},... | collective-permute-start | bytes 98312 | tf_op jit(solution)/shard_map/ppermute | solution.py:585
  10.5 3.9 %collective-permute-start.1 = (f32[16,512]{1,0:T(8,128)S(1)}, f32[16,512]{1,0:T(8,128)S(1)}, u32[]{:S(2)}, u32[]{:S(2)}) collective-permute-start(f32[16,512]{1,0:T(8,128)S(1)} %slice.8), channel_id=1, source_target_pairs={{0,2},{1,18},{2,0},{3,16},{4,6},{5,22},{6,4},{7,20},{8,10},{9,26},... | collective-permute-start | bytes 98312 | tf_op jit(solution)/shard_map/ppermute | solution.py:585
  14.4 4.9 %collective-permute-start.5 = (f32[16,512]{1,0:T(8,128)S(1)}, f32[16,512]{1,0:T(8,128)S(1)}, u32[]{:S(2)}, u32[]{:S(2)}) collective-permute-start(f32[16,512]{1,0:T(8,128)S(1)} %add_select_fusion.refs_0_), channel_id=1, source_target_pairs={{0,12},{4,8},{8,4},{12,0},{16,28},{20,24},{24,20},{28,16},{1,13},{... | collective-permute-start | bytes 98312 | tf_op jit(solution)/shard_map/ppermute | solution.py:561
  17.0 4.1 %collective-permute-start.4 = (f32[16,512]{1,0:T(8,128)S(1)}, f32[16,512]{1,0:T(8,128)S(1)}, u32[]{:S(2)}, u32[]{:S(2)}) collective-permute-start(f32[16,512]{1,0:T(8,128)S(1)} %add_select_fusion.refs_0_), channel_id=1, source_target_pairs={{0,8},{4,12},{8,0},{12,4},{16,24},{20,28},{24,16},{28,20},{1,9},{5... | collective-permute-start | bytes 98312 | tf_op jit(solution)/shard_map/ppermute | solution.py:561
  17.4 3.9 %collective-permute-start.3 = (f32[16,512]{1,0:T(8,128)S(1)}, f32[16,512]{1,0:T(8,128)S(1)}, u32[]{:S(2)}, u32[]{:S(2)}) collective-permute-start(f32[16,512]{1,0:T(8,128)S(1)} %add_select_fusion.refs_0_), channel_id=1, source_target_pairs={{0,4},{4,0},{8,12},{12,8},{16,20},{20,16},{24,28},{28,24},{1,5},{5... | collective-permute-start | bytes 98312 | tf_op jit(solution)/shard_map/ppermute | solution.py:561
  21.4 10.3 %collective-permute-start.6 = (f32[64,640]{1,0:T(8,128)S(1)}, f32[64,640]{1,0:T(8,128)S(1)}, u32[]{:S(2)}, u32[]{:S(2)}) collective-permute-start(f32[64,640]{1,0:T(8,128)S(1)} %slice.9), channel_id=1, source_target_pairs={{0,2},{1,3},{2,0},{3,1},{4,6},{5,7},{6,4},{7,5},{8,10},{9,11},{10,... | collective-permute-start | bytes 491528 | tf_op jit(solution)/shard_map/ppermute | solution.py:561
  31.7 13.5 %collective-permute-start.9 = (f32[64,640]{1,0:T(8,128)S(1)}, f32[64,640]{1,0:T(8,128)S(1)}, u32[]{:S(2)}, u32[]{:S(2)}) collective-permute-start(f32[64,640]{1,0:T(8,128)S(1)} %add.27.refs_0_), channel_id=1, source_target_pairs={{0,12},{4,8},{8,4},{12,0},{16,28},{20,24},{24,20},{28,16},{1,13},{... | collective-permute-start | bytes 491528 | tf_op jit(solution)/shard_map/ppermute | solution.py:561
  33.4 11.9 %collective-permute-start.8 = (f32[64,640]{1,0:T(8,128)S(1)}, f32[64,640]{1,0:T(8,128)S(1)}, u32[]{:S(2)}, u32[]{:S(2)}) collective-permute-start(f32[64,640]{1,0:T(8,128)S(1)} %add.27.refs_0_), channel_id=1, source_target_pairs={{0,8},{4,12},{8,0},{12,4},{16,24},{20,28},{24,16},{28,20},{1,9},{5... | collective-permute-start | bytes 491528 | tf_op jit(solution)/shard_map/ppermute | solution.py:561
  33.6 11.6 %collective-permute-start.7 = (f32[64,640]{1,0:T(8,128)S(1)}, f32[64,640]{1,0:T(8,128)S(1)}, u32[]{:S(2)}, u32[]{:S(2)}) collective-permute-start(f32[64,640]{1,0:T(8,128)S(1)} %add.27.refs_0_), channel_id=1, source_target_pairs={{0,4},{4,0},{8,12},{12,8},{16,20},{20,16},{24,28},{28,24},{1,5},{5... | collective-permute-start | bytes 491528 | tf_op jit(solution)/shard_map/ppermute | solution.py:561
  46.4 3.6 %collective-permute-start.11 = (f32[256,256]{1,0:T(8,128)S(1)}, f32[256,256]{1,0:T(8,128)S(1)}, u32[]{:S(2)}, u32[]{:S(2)}) collective-permute-start(f32[256,256]{1,0:T(8,128)S(1)} %bitcast.7), channel_id=1, source_target_pairs={{0,1},{1,0},{2,3},{3,2},{4,5},{5,4},{6,7},{7,6},{8,9},{9,8},{10,11... | collective-permute-start | bytes 786440 | tf_op jit(solution)/shard_map/ppermute | solution.py:561
  47.1 10.3 %collective-permute-start.10 = (f32[64,256]{1,0:T(8,128)S(1)}, f32[64,256]{1,0:T(8,128)S(1)}, u32[]{:S(2)}, u32[]{:S(2)}) collective-permute-start(f32[64,256]{1,0:T(8,128)S(1)} %get-tuple-element.52.right_ref), channel_id=1, source_target_pairs={{0,17},{1,16},{2,19},{3,18},{4,21},{5,20},{6,23},{7,22},{8,25},{9,... | collective-permute-start | bytes 196616 | tf_op jit(solution)/shard_map/ppermute | solution.py:585
  57.4 2.7 %copy-start.1 = (f32[5,8192]{1,0:T(8,128)S(1)}, f32[5,8192]{1,0:T(8,128)}, u32[]{:S(2)}) copy-start(f32[5,8192]{1,0:T(8,128)} %amplitude_ref.3) | copy-start | bytes 491524
  57.4 2.7 %copy-start.2 = (s32[8192]{0:T(1024)S(1)}, s32[8192]{0:T(1024)}, u32[]{:S(2)}) copy-start(s32[8192]{0:T(1024)} %param.5) | copy-start | bytes 98308
  58.6 1.5 %collective-permute-start.12 = (f32[64,640]{1,0:T(8,128)S(1)}, f32[64,640]{1,0:T(8,128)S(1)}, u32[]{:S(2)}, u32[]{:S(2)}) collective-permute-start(f32[64,640]{1,0:T(8,128)S(1)} %descend.1), channel_id=1, source_target_pairs={{0,1},{1,0},{2,3},{3,2},{4,5},{5,4},{6,7},{7,6},{8,9},{9,8},{10,11... | collective-permute-start | bytes 491528 | tf_op jit(solution)/shard_map/ppermute | solution.py:561

commit v3 on v2

--- a/solution.py
+++ b/solution.py
@@ -295,16 +295,31 @@
     update(targets[0], tier - 1, row_ref, coupling_ref)
 
 
-def inner_kernel(*refs, top, count):
+def forward(source_refs, coupling_ref, target_ref, own_ref, depth):
+    nodes, knots, width = coupling_ref.shape
+    share = nodes // target_ref.shape[0]
+    own_ref[:, depth * knots:(depth + 1) * knots] = source_refs[0][:, width:]
+    for n in range(target_ref.shape[0]):
+        reduced = [
+            source_refs[c][:, :width] - dot_hi(source_refs[c][:, width:], coupling_ref[c])
+            for c in range(n * share, (n + 1) * share)
+        ]
+        target_ref[n] = tree_sum(reduced)
+
+
+def inner_kernel(*refs, top, count, leaves):
+    slot_refs, refs = refs[:leaves], refs[leaves:]
     row_ref, coupling_ref = refs[:2]
     row_refs, (rest_in, prior_ref), refs = refs[2:2 + count], refs[2 + count:4 + count], refs[4 + count:]
     inverse_refs, coupling_refs, refs = refs[:count], refs[count:2 * count], refs[2 * count:]
-    rest_ref, panel_ref, work_refs = refs[0], refs[1], refs[2:]
+    (rest_ref, right_ref, own_ref, panel_ref), refs = refs[:4], refs[4:]
+    work_refs, reduced_refs = refs[:count], refs[count:]
     knots = prior_ref.shape[1]
     for work_ref, ref in zip(work_refs, row_refs):
         work_ref[...] = ref[...]
     rest_ref[...] = rest_in[...]
     targets = list(work_refs) + [rest_ref.at[pl.ds(below, 1)] for below in range(top - 1, -1, -1)]
+    source_refs = slot_refs
     for i in range(count):
         tier = top + count - 1 - i
         nodes = work_refs[i].shape[0]
@@ -315,6 +330,9 @@
             functools.partial(update, targets[i + tier - below], below, row_ref, coupling_ref)
             for below in range(tier - 1, -1, -1)
         ]
+        others.append(functools.partial(
+            forward, source_refs, coupling_ref, reduced_refs[i], own_ref, i
+        ))
         invert(
             [inverse_refs[i].at[n] for n in range(nodes)],
             [panel_ref.at[n] for n in range(nodes)],
@@ -322,10 +340,12 @@
         )
         couple(work_refs[i], inverse_refs[i], coupling_refs[i])
         row_ref, coupling_ref = work_refs[i], coupling_refs[i]
+        source_refs = [reduced_refs[i].at[n] for n in range(nodes)]
         if i + 1 < count:
             update(targets[i + 1], tier - 1, row_ref, coupling_ref)
     for below in range(top - 1, -1, -1):
         update(targets[count + top - 1 - below], below, row_ref, coupling_ref)
+    forward(source_refs, coupling_ref, right_ref, own_ref, count)
 
 
 def whole_call(kernel, args, shapes, scratch, name, limit=8, flops=10**10):
@@ -356,58 +376,23 @@
     return inverse, coupling, row, lower, rest
 
 
-def inner_tiers(row, coupling, lower, rest, prior_precision, top):
+def inner_tiers(slots, row, coupling, lower, rest, prior_precision, top):
     knots = prior_precision.shape[1]
+    fields = slots[0].shape[0]
     count = len(lower)
     nodes = [value.shape[0] for value in lower]
     shapes = [(n, knots, knots) for n in nodes]
     shapes += [(n, knots, value.shape[2] - knots) for n, value in zip(nodes, lower)]
-    shapes.append(rest.shape)
+    shapes += [rest.shape, (1, fields, top * knots), (fields, (count + 1) * knots)]
+    scratch = [(max(nodes), knots, knots)] + [value.shape for value in lower]
+    scratch += [(n, fields, value.shape[2]) for n, value in zip(nodes, lower)]
     out = whole_call(
-        functools.partial(inner_kernel, top=top, count=count),
-        (row, coupling, *lower, rest, prior_precision),
-        shapes, [(max(nodes), knots, knots)] + [value.shape for value in lower],
-        "inner_tiers", limit=16, flops=2 * 10**10,
-    )
-    rest = out[-1].reshape(top * knots, top * knots)
-    return list(out[:count]), list(out[count:-1]), rest
-
-
-def forward_kernel(*refs, leaves):
-    slot_refs, refs = refs[:leaves], refs[leaves:]
-    out_refs = refs[-2:]
-    coupling_refs = refs[:-2]
-    knots = coupling_refs[0].shape[1]
-    current = [ref[...] for ref in slot_refs]
-    own = []
-    for ref in coupling_refs:
-        width = ref.shape[2]
-        own.append(current[0][:, width:width + knots])
-        reduced = [
-            c[:, :width] - dot_hi(c[:, width:width + knots], ref[n]) for n, c in enumerate(current)
-        ]
-        current = (
-            [reduced[2 * n] + reduced[2 * n + 1] for n in range(len(reduced) // 2)]
-            if len(reduced) > 1 else reduced
-        )
-    out_refs[0][...] = current[0]
-    out_refs[1][...] = jnp.concatenate(own, axis=1)
-
-
-def forward(slots, couplings):
-    fields = slots[0].shape[0]
-    knots, width = couplings[-1].shape[1:]
-    return pl.pallas_call(
-        functools.partial(forward_kernel, leaves=len(slots)),
-        in_specs=[vmem] * (len(slots) + len(couplings)),
-        out_specs=[vmem] * 2,
-        out_shape=[
-            jax.ShapeDtypeStruct((fields, width), f32),
-            jax.ShapeDtypeStruct((fields, knots * len(couplings)), f32),
-        ],
-        compiler_params=pltpu.CompilerParams(vmem_limit_bytes=8 * 2**20),
-        name="forward",
-    )(*slots, *couplings)
+        functools.partial(inner_kernel, top=top, count=count, leaves=len(slots)),
+        (*slots, row, coupling, *lower, rest, prior_precision),
+        shapes, scratch, "inner_tiers", limit=16, flops=2 * 10**10,
+    )
+    rest = out[-3].reshape(top * knots, top * knots)
+    return list(out[:count]), list(out[count:-3]), rest, out[-2][0], out[-1]
 
 
 def composites(own_ref, refs, local_ref, deep_ref):
@@ -619,18 +604,16 @@
     sums = sums + swapped(sums, "obs", 1)
     pairs, project = sums[:pair_rows, :basis_table.shape[1]], sums[pair_rows:, :order]
     pairs = sum_for_half(pairs, leaves)
+    project = sum_over(project, "obs", 2, lax.axis_size("obs"))
     pair_slots = gather_half(pairs, leaves)
-    pair_slots, project = lax.optimization_barrier((pair_slots, project))
+    project_slots = gather_half(project, leaves)
     inverse, coupling, row, lower, rest = leaf_tier(
         pair_slots, basis_table, turned, prior_precision, 2
     )
-    project = sum_over(project, "obs", 2, lax.axis_size("obs"))
-    lower, rest, project = lax.optimization_barrier((lower, rest, project))
-    inverses, couplings, rest = inner_tiers(row, coupling, lower, rest, prior_precision, 2)
+    inverses, couplings, rest, right, own = inner_tiers(
+        project_slots, row, coupling, lower, rest, prior_precision, 2
+    )
     inverses, couplings = [inverse] + inverses, [coupling] + couplings
-    project_slots = gather_half(project, leaves)
-    right, own = forward(project_slots, couplings)
-    rest, right = lax.optimization_barrier((rest, right))
     weights = path_weights(rest, right, own, prior_precision, inverses, couplings, leaves)
     weights = spread_weights(weights, leaves)
     return fitted_fields(pattern, amplitude, weights, turned)

time: 64.6 us -> 59.8 us (0.926)
  waiting for transfers between devices: 9.37 us -> 3.96 us
  starting transfers between devices: 14.9 us -> 16.2 us
  Pallas kernels: 39.7 us -> 39 us
    ppermute x10, waiting for transfers between devices: 5.53 us -> 2.44 us  [swapped(): return lax.ppermute(value, axis, pairs)]
    ppermute x3, waiting for transfers between devices: 3.84 us -> 1.52 us  [moved(): return lax.ppermute(value, ('region', 'obs'), pairs)]
    ppermute x10, starting transfers between devices: 8.92 us -> 10.7 us  [swapped(): return lax.ppermute(value, axis, pairs)]
    pallas_call x1 -> x0, Pallas kernels: 1.12 us -> none  [forward(): pl.pallas_call(functools.partial(forward_kernel, leaves=len(slots)), in_s...]
  transfers between devices with their start and end apart: 13 -> 13, of which waited for: 7 -> 3; matrix products, arithmetic and copies ran while one was open for 0% -> 0% of each run, Pallas kernels for 42% -> 29%
where the time goes in v3:
time: 59.8 us; the launch traced here: 59.7 us
  Pallas kernels  39 us (65%)
  starting transfers between devices  16.2 us (27%)
  waiting for transfers between devices  3.96 us (7%)
    pallas_call x4, Pallas kernels, whole_call(): pl.pallas_call(kernel, in_specs=[vmem] * len(args), out_specs=[vmem] * le...  28.7 us
    ppermute x10, starting transfers between devices, swapped(): return lax.ppermute(value, axis, pairs)  10.7 us
    pallas_call x1, Pallas kernels, statistics(): pl.pallas_call(stats_kernel, grid=(obs // block,), in_specs=[pl.BlockSpec...  5.89 us
    ppermute x3, starting transfers between devices, moved(): return lax.ppermute(value, ('region', 'obs'), pairs)  5.49 us
    pallas_call x1, Pallas kernels, fitted_fields(): pl.pallas_call(fitted_kernel, grid=(obs // block,), in_specs=[pl.BlockSpe...  4.41 us
    ppermute x10, waiting for transfers between devices, swapped(): return lax.ppermute(value, axis, pairs)  2.44 us
    ppermute x3, waiting for transfers between devices, moved(): return lax.ppermute(value, ('region', 'obs'), pairs)  1.52 us
  transfers between devices with their start and end apart: 13, of which 3 were waited for; matrix products, arithmetic and copies ran while one was open for 0% of the time, Pallas kernels for 29%

profile of v3, /device:TPU:0, one launch (start us, length us, event | category | flops | bytes accessed | tf_op | source)
XLA Modules:
  0.0 59.7 jit_solution(4434187965065635933)
XLA Ops:
  0.0 5.9 %statistics.1 = f32[80,640]{1,0:T(8,128)S(1)} custom-call(s32[1,8192]{1,0:T(1,128)} %bitcast.6, f32[5,8192]{1,0:T(8,128)} %amplitude_ref.3, bf16[64,8192]{1,0:T(8,128)(2,1)} %fields_ref.1, bf16[5,512,128]{2,1,0:T(8,128)(2,1)} %basis_ref.3), custom_call_target="tpu_custom_call" | custom-call | flops 3623878656 | bytes 4194304 | tf_op jit(solution)/shard_map/statistics/pallas_call | solution.py:111
  5.9 0.0 copy-start.3
  5.9 0.5 collective-permute-start
  6.4 1.1 %collective-permute-done = f32[80,640]{1,0:T(8,128)S(1)} collective-permute-done((f32[80,640]{1,0:T(8,128)S(1)}, f32[80,640]{1,0:T(8,128)S(1)}, u32[]{:S(2)}, u32[]{:S(2)}) %collective-permute-start) | collective-permute-done | bytes 204832 | tf_op jit(solution)/shard_map/ppermute | solution.py:546
  7.5 3.0 %collective-permute-start.6 = (f32[16,512]{1,0:T(8,128)S(1)}, f32[16,512]{1,0:T(8,128)S(1)}, u32[]{:S(2)}, u32[]{:S(2)}) collective-permute-start(f32[16,512]{1,0:T(8,128)S(1)} %slice.9), channel_id=1, source_target_pairs={{0,2},{1,16},{2,0},{3,18},{4,6},{5,20},{6,4},{7,22},{8,10},{9,24},... | collective-permute-start | bytes 98312 | tf_op jit(solution)/shard_map/ppermute | solution.py:570
  10.5 0.1 collective-permute-start.5
  10.6 0.2 copy.6
  10.9 2.0 %collective-permute-start.1 = (f32[64,640]{1,0:T(8,128)S(1)}, f32[64,640]{1,0:T(8,128)S(1)}, u32[]{:S(2)}, u32[]{:S(2)}) collective-permute-start(f32[64,640]{1,0:T(8,128)S(1)} %slice.8), channel_id=1, source_target_pairs={{0,2},{1,3},{2,0},{3,1},{4,6},{5,7},{6,4},{7,5},{8,10},{9,11},{10,... | collective-permute-start | bytes 491528 | tf_op jit(solution)/shard_map/ppermute | solution.py:546
  12.9 0.0 collective-permute-done.6
  12.9 1.5 %collective-permute-done.5 = f32[16,512]{1,0:T(8,128)S(1)} collective-permute-done((f32[16,512]{1,0:T(8,128)S(1)}, f32[16,512]{1,0:T(8,128)S(1)}, u32[]{:S(2)}, u32[]{:S(2)}) %collective-permute-start.5) | collective-permute-done | bytes 32800 | tf_op jit(solution)/shard_map/ppermute | solution.py:570
  14.4 2.6 %collective-permute-start.9 = (f32[16,512]{1,0:T(8,128)S(1)}, f32[16,512]{1,0:T(8,128)S(1)}, u32[]{:S(2)}, u32[]{:S(2)}) collective-permute-start(f32[16,512]{1,0:T(8,128)S(1)} %add_select_fusion.refs_0_), channel_id=1, source_target_pairs={{0,12},{4,8},{8,4},{12,0},{16,28},{20,24},{24,20},{28,16},{1,13},{... | collective-permute-start | bytes 98312 | tf_op jit(solution)/shard_map/ppermute | solution.py:546
  17.0 0.4 collective-permute-start.8
  17.4 0.5 collective-permute-start.7
  18.0 0.0 collective-permute-done.1
  18.0 2.7 %collective-permute-start.4 = (f32[64,640]{1,0:T(8,128)S(1)}, f32[64,640]{1,0:T(8,128)S(1)}, u32[]{:S(2)}, u32[]{:S(2)}) collective-permute-start(f32[64,640]{1,0:T(8,128)S(1)} %slice_add_fusion.refs_0_), channel_id=1, source_target_pairs={{0,12},{4,8},{8,4},{12,0},{16,28},{20,24},{24,20},{28,16},{1,13},{... | collective-permute-start | bytes 491528 | tf_op jit(solution)/shard_map/ppermute | solution.py:546
  20.7 0.4 collective-permute-start.3
  21.1 0.0 collective-permute-done.9.refs_3_
  21.1 0.4 collective-permute-start.2
  21.6 9.9 %leaf_tier.1 = (f32[4,128,128]{2,1,0:T(8,128)S(1)}, f32[4,128,512]{2,1,0:T(8,128)S(1)}, f32[4,128,512]{2,1,0:T(8,128)S(1)}, f32[2,128,512]{2,1,0:T(8,128)S(1)}, ...) custom-call(bf16[5,512,128]{2,1,0:T(8,128)(2,1)S(1)} %copy-done, bf16[5,128,512]{2,1,0:T(8,128)(2,1)S(1)} %bitcast.4, ...), custom_call_target="tpu_custom_call" | custom-call | flops 20000000000 | bytes 1048576 | tf_op jit(solution)/shard_map/leaf_tier/pallas_call | solution.py:352
  31.5 0.0 collective-permute-done.4.refs_3_
  31.5 0.0 collective-permute-done.3.refs_2_
  31.5 10.4 %inner_tiers.1 = (f32[2,128,128]{2,1,0:T(8,128)S(1)}, f32[1,128,128]{2,1,0:T(8,128)S(1)}, f32[2,128,384]{2,1,0:T(8,128)S(1)}, f32[1,128,256]{2,1,0:T(8,128)S(1)}...) custom-call(f32[64,640]{1,0:T(8,128)S(1)} %slice_add_fusion.refs_0_, ...), custom_call_target="tpu_custom_call" | custom-call | flops 20000000000 | bytes 1048576 | tf_op jit(solution)/shard_map/inner_tiers/pallas_call | solution.py:352
  41.9 0.9 %collective-permute-start.11 = (f32[256,256]{1,0:T(8,128)S(1)}, f32[256,256]{1,0:T(8,128)S(1)}, u32[]{:S(2)}, u32[]{:S(2)}) collective-permute-start(f32[256,256]{1,0:T(8,128)S(1)} %bitcast.8), channel_id=1, source_target_pairs={{0,1},{1,0},{2,3},{3,2},{4,5},{5,4},{6,7},{7,6},{8,9},{9,8},{10,11... | collective-permute-start | bytes 786440 | tf_op jit(solution)/shard_map/ppermute | solution.py:546
  42.8 2.5 %collective-permute-start.10 = (f32[64,256]{1,0:T(8,128)S(1)}, f32[64,256]{1,0:T(8,128)S(1)}, u32[]{:S(2)}, u32[]{:S(2)}) collective-permute-start(f32[64,256]{1,0:T(8,128)S(1)} %bitcast.10), channel_id=1, source_target_pairs={{0,17},{1,16},{2,19},{3,18},{4,21},{5,20},{6,23},{7,22},{8,25},{9,... | collective-permute-start | bytes 196616 | tf_op jit(solution)/shard_map/ppermute | solution.py:570
  45.2 7.4 %top.1 = (f32[64,384]{1,0:T(8,128)S(1)}, f32[384,256]{1,0:T(8,128)S(1)}, f32[128,128]{1,0:T(8,128)S(1)}, f32[128,128]{1,0:T(8,128)S(1)}, f32[128,128]{1,0:T(8,128)S(1)}) custom-call(f32[256,256]{1,0:T(8,128)S(1)} %bitcast.9, f32[256,256]{1,0:T(8,128)S(1)} %collective-permute-done.11.other_ref, f32[5,128]{1,0:T(8,128)S(1)} %copy-done.3, ...), custom_call_target="tpu_custom_call" | custom-call | flops 10000000000 | bytes 1048576 | tf_op jit(solution)/shard_map/top/pallas_call | solution.py:352
  52.6 0.0 collective-permute-done.10.other_ref
  52.6 0.0 copy-start.1
  52.6 0.0 copy-start.2
  52.6 1.1 %descend.1 = f32[64,640]{1,0:T(8,128)S(1)} custom-call(f32[64,256]{1,0:T(8,128)S(1)} %bitcast.11, f32[64,256]{1,0:T(8,128)S(1)} %collective-permute-done.10.other_ref, f32[128,128]{1,0:T(8,128)S(1)} %get-tuple-element.36.top_ref, f32[128,128]{1,0:T(8,128)S(1)} %get-tuple-element.37.coupling_ref, f32[128,128]{1,0:T(8,128)S(1)} %get-tuple-element.38.root_ref, ...), custom_call_target="tpu_custom_call" | custom-call | flops 1000000000 | bytes 1048576 | tf_op jit(solution)/shard_map/descend/pallas_call | solution.py:352
  53.8 0.1 collective-permute-start.12
  53.9 1.3 %collective-permute-done.12 = f32[64,640]{1,0:T(8,128)S(1)} collective-permute-done((f32[64,640]{1,0:T(8,128)S(1)}, f32[64,640]{1,0:T(8,128)S(1)}, u32[]{:S(2)}, u32[]{:S(2)}) %collective-permute-start.12) | collective-permute-done | bytes 163872 | tf_op jit(solution)/shard_map/ppermute | solution.py:546
  55.3 4.4 %fitted_fields.1 = f32[64,8192]{1,0:T(8,128)} custom-call(s32[1,8192]{1,0:T(1,128)S(1)} %bitcast.7, f32[5,8192]{1,0:T(8,128)S(1)} %copy-done.1, f32[64,640]{1,0:T(8,128)S(1)} %broadcast_select_fusion.weight_ref, bf16[5,128,512]{2,1,0:T(8,128)(2,1)S(1)} %bitcast.5), custom_call_target="tpu_custom_call" | custom-call | tf_op jit(solution)/shard_map/fitted_fields/pallas_call | solution.py:527
  (15 shorter events, 0.1 us)
Async XLA Ops:
  0.0 10.6 %copy-start = (bf16[5,512,128]{2,1,0:T(8,128)(2,1)S(1)}, bf16[5,512,128]{2,1,0:T(8,128)(2,1)}, u32[]{:S(2)}) copy-start(bf16[5,512,128]{2,1,0:T(8,128)(2,1)} %basis_ref.3) | copy-start | bytes 1966084
  5.9 15.7 %copy-start.3 = (f32[5,128]{1,0:T(8,128)S(1)}, f32[5,128]{1,0:T(8,128)}, u32[]{:S(2)}) copy-start(f32[5,128]{1,0:T(8,128)} %prior_ref.3) | copy-start | bytes 7684
  5.9 1.6 %collective-permute-start = (f32[80,640]{1,0:T(8,128)S(1)}, f32[80,640]{1,0:T(8,128)S(1)}, u32[]{:S(2)}, u32[]{:S(2)}) collective-permute-start(f32[80,640]{1,0:T(8,128)S(1)} %statistics.1), channel_id=1, source_target_pairs={{0,1},{1,0},{2,3},{3,2},{4,5},{5,4},{6,7},{7,6},{8,9},{9,8},{10,11... | collective-permute-start | bytes 614408 | tf_op jit(solution)/shard_map/ppermute | solution.py:546
  7.5 5.4 %collective-permute-start.6 = (f32[16,512]{1,0:T(8,128)S(1)}, f32[16,512]{1,0:T(8,128)S(1)}, u32[]{:S(2)}, u32[]{:S(2)}) collective-permute-start(f32[16,512]{1,0:T(8,128)S(1)} %slice.9), channel_id=1, source_target_pairs={{0,2},{1,16},{2,0},{3,18},{4,6},{5,20},{6,4},{7,22},{8,10},{9,24},... | collective-permute-start | bytes 98312 | tf_op jit(solution)/shard_map/ppermute | solution.py:570
  10.5 3.9 %collective-permute-start.5 = (f32[16,512]{1,0:T(8,128)S(1)}, f32[16,512]{1,0:T(8,128)S(1)}, u32[]{:S(2)}, u32[]{:S(2)}) collective-permute-start(f32[16,512]{1,0:T(8,128)S(1)} %slice.9), channel_id=1, source_target_pairs={{0,2},{1,18},{2,0},{3,16},{4,6},{5,22},{6,4},{7,20},{8,10},{9,26},... | collective-permute-start | bytes 98312 | tf_op jit(solution)/shard_map/ppermute | solution.py:570
  10.9 7.1 %collective-permute-start.1 = (f32[64,640]{1,0:T(8,128)S(1)}, f32[64,640]{1,0:T(8,128)S(1)}, u32[]{:S(2)}, u32[]{:S(2)}) collective-permute-start(f32[64,640]{1,0:T(8,128)S(1)} %slice.8), channel_id=1, source_target_pairs={{0,2},{1,3},{2,0},{3,1},{4,6},{5,7},{6,4},{7,5},{8,10},{9,11},{10,... | collective-permute-start | bytes 491528 | tf_op jit(solution)/shard_map/ppermute | solution.py:546
  14.4 6.7 %collective-permute-start.9 = (f32[16,512]{1,0:T(8,128)S(1)}, f32[16,512]{1,0:T(8,128)S(1)}, u32[]{:S(2)}, u32[]{:S(2)}) collective-permute-start(f32[16,512]{1,0:T(8,128)S(1)} %add_select_fusion.refs_0_), channel_id=1, source_target_pairs={{0,12},{4,8},{8,4},{12,0},{16,28},{20,24},{24,20},{28,16},{1,13},{... | collective-permute-start | bytes 98312 | tf_op jit(solution)/shard_map/ppermute | solution.py:546
  17.0 4.6 %collective-permute-start.8 = (f32[16,512]{1,0:T(8,128)S(1)}, f32[16,512]{1,0:T(8,128)S(1)}, u32[]{:S(2)}, u32[]{:S(2)}) collective-permute-start(f32[16,512]{1,0:T(8,128)S(1)} %add_select_fusion.refs_0_), channel_id=1, source_target_pairs={{0,8},{4,12},{8,0},{12,4},{16,24},{20,28},{24,16},{28,20},{1,9},{5... | collective-permute-start | bytes 98312 | tf_op jit(solution)/shard_map/ppermute | solution.py:546
  17.4 4.1 %collective-permute-start.7 = (f32[16,512]{1,0:T(8,128)S(1)}, f32[16,512]{1,0:T(8,128)S(1)}, u32[]{:S(2)}, u32[]{:S(2)}) collective-permute-start(f32[16,512]{1,0:T(8,128)S(1)} %add_select_fusion.refs_0_), channel_id=1, source_target_pairs={{0,4},{4,0},{8,12},{12,8},{16,20},{20,16},{24,28},{28,24},{1,5},{5... | collective-permute-start | bytes 98312 | tf_op jit(solution)/shard_map/ppermute | solution.py:546
  18.0 13.4 %collective-permute-start.4 = (f32[64,640]{1,0:T(8,128)S(1)}, f32[64,640]{1,0:T(8,128)S(1)}, u32[]{:S(2)}, u32[]{:S(2)}) collective-permute-start(f32[64,640]{1,0:T(8,128)S(1)} %slice_add_fusion.refs_0_), channel_id=1, source_target_pairs={{0,12},{4,8},{8,4},{12,0},{16,28},{20,24},{24,20},{28,16},{1,13},{... | collective-permute-start | bytes 491528 | tf_op jit(solution)/shard_map/ppermute | solution.py:546
  20.7 10.8 %collective-permute-start.3 = (f32[64,640]{1,0:T(8,128)S(1)}, f32[64,640]{1,0:T(8,128)S(1)}, u32[]{:S(2)}, u32[]{:S(2)}) collective-permute-start(f32[64,640]{1,0:T(8,128)S(1)} %slice_add_fusion.refs_0_), channel_id=1, source_target_pairs={{0,8},{4,12},{8,0},{12,4},{16,24},{20,28},{24,16},{28,20},{1,9},{5... | collective-permute-start | bytes 491528 | tf_op jit(solution)/shard_map/ppermute | solution.py:546
  21.1 10.3 %collective-permute-start.2 = (f32[64,640]{1,0:T(8,128)S(1)}, f32[64,640]{1,0:T(8,128)S(1)}, u32[]{:S(2)}, u32[]{:S(2)}) collective-permute-start(f32[64,640]{1,0:T(8,128)S(1)} %slice_add_fusion.refs_0_), channel_id=1, source_target_pairs={{0,4},{4,0},{8,12},{12,8},{16,20},{20,16},{24,28},{28,24},{1,5},{5... | collective-permute-start | bytes 491528 | tf_op jit(solution)/shard_map/ppermute | solution.py:546
  41.9 3.4 %collective-permute-start.11 = (f32[256,256]{1,0:T(8,128)S(1)}, f32[256,256]{1,0:T(8,128)S(1)}, u32[]{:S(2)}, u32[]{:S(2)}) collective-permute-start(f32[256,256]{1,0:T(8,128)S(1)} %bitcast.8), channel_id=1, source_target_pairs={{0,1},{1,0},{2,3},{3,2},{4,5},{5,4},{6,7},{7,6},{8,9},{9,8},{10,11... | collective-permute-start | bytes 786440 | tf_op jit(solution)/shard_map/ppermute | solution.py:546
  42.8 9.8 %collective-permute-start.10 = (f32[64,256]{1,0:T(8,128)S(1)}, f32[64,256]{1,0:T(8,128)S(1)}, u32[]{:S(2)}, u32[]{:S(2)}) collective-permute-start(f32[64,256]{1,0:T(8,128)S(1)} %bitcast.10), channel_id=1, source_target_pairs={{0,17},{1,16},{2,19},{3,18},{4,21},{5,20},{6,23},{7,22},{8,25},{9,... | collective-permute-start | bytes 196616 | tf_op jit(solution)/shard_map/ppermute | solution.py:570
  52.6 2.7 %copy-start.1 = (f32[5,8192]{1,0:T(8,128)S(1)}, f32[5,8192]{1,0:T(8,128)}, u32[]{:S(2)}) copy-start(f32[5,8192]{1,0:T(8,128)} %amplitude_ref.3) | copy-start | bytes 491524
  52.6 2.7 %copy-start.2 = (s32[8192]{0:T(1024)S(1)}, s32[8192]{0:T(1024)}, u32[]{:S(2)}) copy-start(s32[8192]{0:T(1024)} %param.5) | copy-start | bytes 98308
  53.8 1.5 %collective-permute-start.12 = (f32[64,640]{1,0:T(8,128)S(1)}, f32[64,640]{1,0:T(8,128)S(1)}, u32[]{:S(2)}, u32[]{:S(2)}) collective-permute-start(f32[64,640]{1,0:T(8,128)S(1)} %descend.1), channel_id=1, source_target_pairs={{0,1},{1,0},{2,3},{3,2},{4,5},{5,4},{6,7},{7,6},{8,9},{9,8},{10,11... | collective-permute-start | bytes 491528 | tf_op jit(solution)/shard_map/ppermute | solution.py:546

commit v4 on v3

--- a/solution.py
+++ b/solution.py
@@ -242,21 +242,21 @@
     return product[:size] + (product[size:2 * size] + product[2 * size:])
 
 
-def update(target_ref, below, row_ref, coupling_ref):
+def update(target_ref, below, row_ref, coupling_ref, begin=0, end=None):
     nodes, knots = row_ref.shape[:2]
     share = nodes // target_ref.shape[0]
     first, last = below * knots, (below + 1) * knots
+    end = last if end is None else end
     for n in range(target_ref.shape[0]):
         part = slice(n * share, (n + 1) * share)
         left = row_ref[part, :, first:last].reshape(share * knots, knots)
-        right = coupling_ref[part, :, :last].reshape(share * knots, last)
-        target_ref[n, :, :last] -= dot_tn(left, right)
-
-
-def couple(row_ref, inverse_ref, coupling_ref):
-    width = coupling_ref.shape[2]
+        right = coupling_ref[part, :, begin:end].reshape(share * knots, end - begin)
+        target_ref[n, :, begin:end] -= dot_tn(left, right)
+
+
+def couple(row_ref, inverse_ref, coupling_ref, begin, end):
     for n in range(inverse_ref.shape[0]):
-        coupling_ref[n] = dot_hi(inverse_ref[n], row_ref[n, :, :width])
+        coupling_ref[n, :, begin:end] = dot_hi(inverse_ref[n], row_ref[n, :, begin:end])
 
 
 def leaf_kernel(basis_ref, turned_ref, prior_ref, *refs, top):
@@ -291,8 +291,9 @@
     invert(
         [inverse_ref.at[n] for n in range(leaves)], [panel_ref.at[n] for n in range(leaves)], others
     )
-    couple(row_ref, inverse_ref, coupling_ref)
-    update(targets[0], tier - 1, row_ref, coupling_ref)
+    first, last = (tier - 1) * knots, tier * knots
+    couple(row_ref, inverse_ref, coupling_ref, first, last)
+    update(targets[0], tier - 1, row_ref, coupling_ref, first, last)
 
 
 def forward(source_refs, coupling_ref, target_ref, own_ref, depth):
@@ -309,8 +310,9 @@
 
 def inner_kernel(*refs, top, count, leaves):
     slot_refs, refs = refs[:leaves], refs[leaves:]
-    row_ref, coupling_ref = refs[:2]
-    row_refs, (rest_in, prior_ref), refs = refs[2:2 + count], refs[2 + count:4 + count], refs[4 + count:]
+    row_ref, inverse_ref, coupling_in = refs[:3]
+    row_refs, (rest_in, prior_ref), refs = refs[3:3 + count], refs[3 + count:5 + count], refs[5 + count:]
+    coupling_ref, refs = refs[0], refs[1:]
     inverse_refs, coupling_refs, refs = refs[:count], refs[count:2 * count], refs[2 * count:]
     (rest_ref, right_ref, own_ref, panel_ref), refs = refs[:4], refs[4:]
     work_refs, reduced_refs = refs[:count], refs[count:]
@@ -320,6 +322,8 @@
     rest_ref[...] = rest_in[...]
     targets = list(work_refs) + [rest_ref.at[pl.ds(below, 1)] for below in range(top - 1, -1, -1)]
     source_refs = slot_refs
+    last = coupling_in.shape[2]
+    coupling_ref[:, :, last - knots:] = coupling_in[:, :, last - knots:]
     for i in range(count):
         tier = top + count - 1 - i
         nodes = work_refs[i].shape[0]
@@ -327,6 +331,12 @@
         for n in range(nodes):
             inverse_refs[i][n] = work_refs[i][n, :, tier * knots:] + prior
         others = [
+            functools.partial(couple, row_ref, inverse_ref, coupling_ref, 0, tier * knots),
+            functools.partial(
+                update, targets[i], tier, row_ref, coupling_ref, 0, tier * knots
+            ),
+        ]
+        others += [
             functools.partial(update, targets[i + tier - below], below, row_ref, coupling_ref)
             for below in range(tier - 1, -1, -1)
         ]
@@ -338,11 +348,12 @@
             [panel_ref.at[n] for n in range(nodes)],
             others,
         )
-        couple(work_refs[i], inverse_refs[i], coupling_refs[i])
-        row_ref, coupling_ref = work_refs[i], coupling_refs[i]
+        row_ref, inverse_ref, coupling_ref = work_refs[i], inverse_refs[i], coupling_refs[i]
+        first = (tier - 1) * knots if i + 1 < count else 0
+        couple(row_ref, inverse_ref, coupling_ref, first, tier * knots)
         source_refs = [reduced_refs[i].at[n] for n in range(nodes)]
         if i + 1 < count:
-            update(targets[i + 1], tier - 1, row_ref, coupling_ref)
+            update(targets[i + 1], tier - 1, row_ref, coupling_ref, first, tier * knots)
     for below in range(top - 1, -1, -1):
         update(targets[count + top - 1 - below], below, row_ref, coupling_ref)
     forward(source_refs, coupling_ref, right_ref, own_ref, count)
@@ -376,23 +387,24 @@
     return inverse, coupling, row, lower, rest
 
 
-def inner_tiers(slots, row, coupling, lower, rest, prior_precision, top):
+def inner_tiers(slots, row, inverse, coupling, lower, rest, prior_precision, top):
     knots = prior_precision.shape[1]
     fields = slots[0].shape[0]
     count = len(lower)
     nodes = [value.shape[0] for value in lower]
-    shapes = [(n, knots, knots) for n in nodes]
+    shapes = [coupling.shape] + [(n, knots, knots) for n in nodes]
     shapes += [(n, knots, value.shape[2] - knots) for n, value in zip(nodes, lower)]
     shapes += [rest.shape, (1, fields, top * knots), (fields, (count + 1) * knots)]
     scratch = [(max(nodes), knots, knots)] + [value.shape for value in lower]
     scratch += [(n, fields, value.shape[2]) for n, value in zip(nodes, lower)]
     out = whole_call(
         functools.partial(inner_kernel, top=top, count=count, leaves=len(slots)),
-        (*slots, row, coupling, *lower, rest, prior_precision),
+        (*slots, row, inverse, coupling, *lower, rest, prior_precision),
         shapes, scratch, "inner_tiers", limit=16, flops=2 * 10**10,
     )
     rest = out[-3].reshape(top * knots, top * knots)
-    return list(out[:count]), list(out[count:-3]), rest, out[-2][0], out[-1]
+    inverses, couplings = [inverse, *out[1:count + 1]], [out[0], *out[count + 1:-3]]
+    return inverses, couplings, rest, out[-2][0], out[-1]
 
 
 def composites(own_ref, refs, local_ref, deep_ref):
@@ -611,9 +623,8 @@
         pair_slots, basis_table, turned, prior_precision, 2
     )
     inverses, couplings, rest, right, own = inner_tiers(
-        project_slots, row, coupling, lower, rest, prior_precision, 2
-    )
-    inverses, couplings = [inverse] + inverses, [coupling] + couplings
+        project_slots, row, inverse, coupling, lower, rest, prior_precision, 2
+    )
     weights = path_weights(rest, right, own, prior_precision, inverses, couplings, leaves)
     weights = spread_weights(weights, leaves)
     return fitted_fields(pattern, amplitude, weights, turned)

time: 59.8 us -> 59.7 us (level)
  transfers between devices with their start and end apart: 13 -> 13, of which waited for: 3 -> 3; matrix products, arithmetic and copies ran while one was open for 0% -> 0% of each run, Pallas kernels for 29% -> 27%
where the time goes in v4:
time: 59.7 us; the launch traced here: 59.5 us
  Pallas kernels  38.8 us (65%)
  starting transfers between devices  16.2 us (27%)
  waiting for transfers between devices  3.95 us (7%)
    pallas_call x4, Pallas kernels, whole_call(): pl.pallas_call(kernel, in_specs=[vmem] * len(args), out_specs=[vmem] * le...  28.5 us
    ppermute x10, starting transfers between devices, swapped(): return lax.ppermute(value, axis, pairs)  10.7 us
    pallas_call x1, Pallas kernels, statistics(): pl.pallas_call(stats_kernel, grid=(obs // block,), in_specs=[pl.BlockSpec...  5.89 us
    ppermute x3, starting transfers between devices, moved(): return lax.ppermute(value, ('region', 'obs'), pairs)  5.5 us
    pallas_call x1, Pallas kernels, fitted_fields(): pl.pallas_call(fitted_kernel, grid=(obs // block,), in_specs=[pl.BlockSpe...  4.41 us
    ppermute x10, waiting for transfers between devices, swapped(): return lax.ppermute(value, axis, pairs)  2.43 us
    ppermute x3, waiting for transfers between devices, moved(): return lax.ppermute(value, ('region', 'obs'), pairs)  1.52 us
  transfers between devices with their start and end apart: 13, of which 3 were waited for; matrix products, arithmetic and copies ran while one was open for 0% of the time, Pallas kernels for 27%

profile of v4, /device:TPU:0, one launch (start us, length us, event | category | flops | bytes accessed | tf_op | source)
XLA Modules:
  0.0 59.5 jit_solution(16921717414369473307)
XLA Ops:
  0.0 5.9 %statistics.1 = f32[80,640]{1,0:T(8,128)S(1)} custom-call(s32[1,8192]{1,0:T(1,128)} %bitcast.6, f32[5,8192]{1,0:T(8,128)} %amplitude_ref.3, bf16[64,8192]{1,0:T(8,128)(2,1)} %fields_ref.1, bf16[5,512,128]{2,1,0:T(8,128)(2,1)} %basis_ref.3), custom_call_target="tpu_custom_call" | custom-call | flops 3623878656 | bytes 4194304 | tf_op jit(solution)/shard_map/statistics/pallas_call | solution.py:111
  5.9 0.0 copy-start.3
  5.9 0.5 collective-permute-start
  6.4 1.1 %collective-permute-done = f32[80,640]{1,0:T(8,128)S(1)} collective-permute-done((f32[80,640]{1,0:T(8,128)S(1)}, f32[80,640]{1,0:T(8,128)S(1)}, u32[]{:S(2)}, u32[]{:S(2)}) %collective-permute-start) | collective-permute-done | bytes 204832 | tf_op jit(solution)/shard_map/ppermute | solution.py:558
  7.5 3.0 %collective-permute-start.6 = (f32[16,512]{1,0:T(8,128)S(1)}, f32[16,512]{1,0:T(8,128)S(1)}, u32[]{:S(2)}, u32[]{:S(2)}) collective-permute-start(f32[16,512]{1,0:T(8,128)S(1)} %slice.9), channel_id=1, source_target_pairs={{0,2},{1,16},{2,0},{3,18},{4,6},{5,20},{6,4},{7,22},{8,10},{9,24},... | collective-permute-start | bytes 98312 | tf_op jit(solution)/shard_map/ppermute | solution.py:582
  10.5 0.1 collective-permute-start.5
  10.6 0.2 copy.6
  10.9 2.0 %collective-permute-start.1 = (f32[64,640]{1,0:T(8,128)S(1)}, f32[64,640]{1,0:T(8,128)S(1)}, u32[]{:S(2)}, u32[]{:S(2)}) collective-permute-start(f32[64,640]{1,0:T(8,128)S(1)} %slice.8), channel_id=1, source_target_pairs={{0,2},{1,3},{2,0},{3,1},{4,6},{5,7},{6,4},{7,5},{8,10},{9,11},{10,... | collective-permute-start | bytes 491528 | tf_op jit(solution)/shard_map/ppermute | solution.py:558
  12.9 1.5 %collective-permute-done.5 = f32[16,512]{1,0:T(8,128)S(1)} collective-permute-done((f32[16,512]{1,0:T(8,128)S(1)}, f32[16,512]{1,0:T(8,128)S(1)}, u32[]{:S(2)}, u32[]{:S(2)}) %collective-permute-start.5) | collective-permute-done | bytes 32800 | tf_op jit(solution)/shard_map/ppermute | solution.py:582
  14.4 2.6 %collective-permute-start.9 = (f32[16,512]{1,0:T(8,128)S(1)}, f32[16,512]{1,0:T(8,128)S(1)}, u32[]{:S(2)}, u32[]{:S(2)}) collective-permute-start(f32[16,512]{1,0:T(8,128)S(1)} %add_select_fusion.refs_0_), channel_id=1, source_target_pairs={{0,12},{4,8},{8,4},{12,0},{16,28},{20,24},{24,20},{28,16},{1,13},{... | collective-permute-start | bytes 98312 | tf_op jit(solution)/shard_map/ppermute | solution.py:558
  17.0 0.4 collective-permute-start.8
  17.4 0.5 collective-permute-start.7
  18.0 0.0 collective-permute-done.1
  18.0 2.7 %collective-permute-start.4 = (f32[64,640]{1,0:T(8,128)S(1)}, f32[64,640]{1,0:T(8,128)S(1)}, u32[]{:S(2)}, u32[]{:S(2)}) collective-permute-start(f32[64,640]{1,0:T(8,128)S(1)} %slice_add_fusion.refs_0_), channel_id=1, source_target_pairs={{0,12},{4,8},{8,4},{12,0},{16,28},{20,24},{24,20},{28,16},{1,13},{... | collective-permute-start | bytes 491528 | tf_op jit(solution)/shard_map/ppermute | solution.py:558
  20.7 0.4 collective-permute-start.3
  21.1 0.0 collective-permute-done.9.refs_3_
  21.2 0.4 collective-permute-start.2
  21.6 0.0 collective-permute-done.8.refs_2_
  21.6 0.0 collective-permute-done.7.refs_1_
  21.6 9.0 %leaf_tier.1 = (f32[4,128,128]{2,1,0:T(8,128)S(1)}, f32[4,128,512]{2,1,0:T(8,128)S(1)}, f32[4,128,512]{2,1,0:T(8,128)S(1)}, f32[2,128,512]{2,1,0:T(8,128)S(1)}, ...) custom-call(bf16[5,512,128]{2,1,0:T(8,128)(2,1)S(1)} %copy-done, bf16[5,128,512]{2,1,0:T(8,128)(2,1)S(1)} %bitcast.4, ...), custom_call_target="tpu_custom_call" | custom-call | flops 20000000000 | bytes 1048576 | tf_op jit(solution)/shard_map/leaf_tier/pallas_call | solution.py:363
  30.6 0.0 collective-permute-done.4.refs_3_
  30.6 11.1 %inner_tiers.1 = (f32[4,128,512]{2,1,0:T(8,128)S(1)}, f32[2,128,128]{2,1,0:T(8,128)S(1)}, f32[1,128,128]{2,1,0:T(8,128)S(1)}, f32[2,128,384]{2,1,0:T(8,128)S(1)}...) custom-call(f32[64,640]{1,0:T(8,128)S(1)} %slice_add_fusion.refs_0_,, ...), custom_call_target="tpu_custom_call" | custom-call | flops 20000000000 | bytes 1048576 | tf_op jit(solution)/shard_map/inner_tiers/pallas_call | solution.py:363
  41.7 0.9 %collective-permute-start.11 = (f32[256,256]{1,0:T(8,128)S(1)}, f32[256,256]{1,0:T(8,128)S(1)}, u32[]{:S(2)}, u32[]{:S(2)}) collective-permute-start(f32[256,256]{1,0:T(8,128)S(1)} %bitcast.8), channel_id=1, source_target_pairs={{0,1},{1,0},{2,3},{3,2},{4,5},{5,4},{6,7},{7,6},{8,9},{9,8},{10,11... | collective-permute-start | bytes 786440 | tf_op jit(solution)/shard_map/ppermute | solution.py:558
  42.6 2.5 %collective-permute-start.10 = (f32[64,256]{1,0:T(8,128)S(1)}, f32[64,256]{1,0:T(8,128)S(1)}, u32[]{:S(2)}, u32[]{:S(2)}) collective-permute-start(f32[64,256]{1,0:T(8,128)S(1)} %bitcast.10), channel_id=1, source_target_pairs={{0,17},{1,16},{2,19},{3,18},{4,21},{5,20},{6,23},{7,22},{8,25},{9,... | collective-permute-start | bytes 196616 | tf_op jit(solution)/shard_map/ppermute | solution.py:582
  45.0 7.4 %top.1 = (f32[64,384]{1,0:T(8,128)S(1)}, f32[384,256]{1,0:T(8,128)S(1)}, f32[128,128]{1,0:T(8,128)S(1)}, f32[128,128]{1,0:T(8,128)S(1)}, f32[128,128]{1,0:T(8,128)S(1)}) custom-call(f32[256,256]{1,0:T(8,128)S(1)} %bitcast.9, f32[256,256]{1,0:T(8,128)S(1)} %collective-permute-done.11.other_ref, f32[5,128]{1,0:T(8,128)S(1)} %copy-done.3, ...), custom_call_target="tpu_custom_call" | custom-call | flops 10000000000 | bytes 1048576 | tf_op jit(solution)/shard_map/top/pallas_call | solution.py:363
  52.4 0.0 collective-permute-done.10.other_ref
  52.4 0.0 copy-start.1
  52.4 0.0 copy-start.2
  52.4 1.1 %descend.1 = f32[64,640]{1,0:T(8,128)S(1)} custom-call(f32[64,256]{1,0:T(8,128)S(1)} %bitcast.11, f32[64,256]{1,0:T(8,128)S(1)} %collective-permute-done.10.other_ref, f32[128,128]{1,0:T(8,128)S(1)} %get-tuple-element.38.top_ref, f32[128,128]{1,0:T(8,128)S(1)} %get-tuple-element.39.coupling_ref, f32[128,128]{1,0:T(8,128)S(1)} %get-tuple-element.40.root_ref, ...), custom_call_target="tpu_custom_call" | custom-call | flops 1000000000 | bytes 1048576 | tf_op jit(solution)/shard_map/descend/pallas_call | solution.py:363
  53.6 0.1 collective-permute-start.12
  53.7 1.3 %collective-permute-done.12 = f32[64,640]{1,0:T(8,128)S(1)} collective-permute-done((f32[64,640]{1,0:T(8,128)S(1)}, f32[64,640]{1,0:T(8,128)S(1)}, u32[]{:S(2)}, u32[]{:S(2)}) %collective-permute-start.12) | collective-permute-done | bytes 163872 | tf_op jit(solution)/shard_map/ppermute | solution.py:558
  55.1 4.4 %fitted_fields.1 = f32[64,8192]{1,0:T(8,128)} custom-call(s32[1,8192]{1,0:T(1,128)S(1)} %bitcast.7, f32[5,8192]{1,0:T(8,128)S(1)} %copy-done.1, f32[64,640]{1,0:T(8,128)S(1)} %broadcast_select_fusion.weight_ref, bf16[5,128,512]{2,1,0:T(8,128)(2,1)S(1)} %bitcast.5), custom_call_target="tpu_custom_call" | custom-call | tf_op jit(solution)/shard_map/fitted_fields/pallas_call | solution.py:539
  (15 shorter events, 0.1 us)
Async XLA Ops:
  0.0 10.6 %copy-start = (bf16[5,512,128]{2,1,0:T(8,128)(2,1)S(1)}, bf16[5,512,128]{2,1,0:T(8,128)(2,1)}, u32[]{:S(2)}) copy-start(bf16[5,512,128]{2,1,0:T(8,128)(2,1)} %basis_ref.3) | copy-start | bytes 1966084
  5.9 15.7 %copy-start.3 = (f32[5,128]{1,0:T(8,128)S(1)}, f32[5,128]{1,0:T(8,128)}, u32[]{:S(2)}) copy-start(f32[5,128]{1,0:T(8,128)} %prior_ref.3) | copy-start | bytes 7684
  5.9 1.6 %collective-permute-start = (f32[80,640]{1,0:T(8,128)S(1)}, f32[80,640]{1,0:T(8,128)S(1)}, u32[]{:S(2)}, u32[]{:S(2)}) collective-permute-start(f32[80,640]{1,0:T(8,128)S(1)} %statistics.1), channel_id=1, source_target_pairs={{0,1},{1,0},{2,3},{3,2},{4,5},{5,4},{6,7},{7,6},{8,9},{9,8},{10,11... | collective-permute-start | bytes 614408 | tf_op jit(solution)/shard_map/ppermute | solution.py:558
  7.5 5.4 %collective-permute-start.6 = (f32[16,512]{1,0:T(8,128)S(1)}, f32[16,512]{1,0:T(8,128)S(1)}, u32[]{:S(2)}, u32[]{:S(2)}) collective-permute-start(f32[16,512]{1,0:T(8,128)S(1)} %slice.9), channel_id=1, source_target_pairs={{0,2},{1,16},{2,0},{3,18},{4,6},{5,20},{6,4},{7,22},{8,10},{9,24},... | collective-permute-start | bytes 98312 | tf_op jit(solution)/shard_map/ppermute | solution.py:582
  10.5 3.9 %collective-permute-start.5 = (f32[16,512]{1,0:T(8,128)S(1)}, f32[16,512]{1,0:T(8,128)S(1)}, u32[]{:S(2)}, u32[]{:S(2)}) collective-permute-start(f32[16,512]{1,0:T(8,128)S(1)} %slice.9), channel_id=1, source_target_pairs={{0,2},{1,18},{2,0},{3,16},{4,6},{5,22},{6,4},{7,20},{8,10},{9,26},... | collective-permute-start | bytes 98312 | tf_op jit(solution)/shard_map/ppermute | solution.py:582
  10.9 7.1 %collective-permute-start.1 = (f32[64,640]{1,0:T(8,128)S(1)}, f32[64,640]{1,0:T(8,128)S(1)}, u32[]{:S(2)}, u32[]{:S(2)}) collective-permute-start(f32[64,640]{1,0:T(8,128)S(1)} %slice.8), channel_id=1, source_target_pairs={{0,2},{1,3},{2,0},{3,1},{4,6},{5,7},{6,4},{7,5},{8,10},{9,11},{10,... | collective-permute-start | bytes 491528 | tf_op jit(solution)/shard_map/ppermute | solution.py:558
  14.4 6.7 %collective-permute-start.9 = (f32[16,512]{1,0:T(8,128)S(1)}, f32[16,512]{1,0:T(8,128)S(1)}, u32[]{:S(2)}, u32[]{:S(2)}) collective-permute-start(f32[16,512]{1,0:T(8,128)S(1)} %add_select_fusion.refs_0_), channel_id=1, source_target_pairs={{0,12},{4,8},{8,4},{12,0},{16,28},{20,24},{24,20},{28,16},{1,13},{... | collective-permute-start | bytes 98312 | tf_op jit(solution)/shard_map/ppermute | solution.py:558
  17.0 4.6 %collective-permute-start.8 = (f32[16,512]{1,0:T(8,128)S(1)}, f32[16,512]{1,0:T(8,128)S(1)}, u32[]{:S(2)}, u32[]{:S(2)}) collective-permute-start(f32[16,512]{1,0:T(8,128)S(1)} %add_select_fusion.refs_0_), channel_id=1, source_target_pairs={{0,8},{4,12},{8,0},{12,4},{16,24},{20,28},{24,16},{28,20},{1,9},{5... | collective-permute-start | bytes 98312 | tf_op jit(solution)/shard_map/ppermute | solution.py:558
  17.4 4.1 %collective-permute-start.7 = (f32[16,512]{1,0:T(8,128)S(1)}, f32[16,512]{1,0:T(8,128)S(1)}, u32[]{:S(2)}, u32[]{:S(2)}) collective-permute-start(f32[16,512]{1,0:T(8,128)S(1)} %add_select_fusion.refs_0_), channel_id=1, source_target_pairs={{0,4},{4,0},{8,12},{12,8},{16,20},{20,16},{24,28},{28,24},{1,5},{5... | collective-permute-start | bytes 98312 | tf_op jit(solution)/shard_map/ppermute | solution.py:558
  18.0 12.5 %collective-permute-start.4 = (f32[64,640]{1,0:T(8,128)S(1)}, f32[64,640]{1,0:T(8,128)S(1)}, u32[]{:S(2)}, u32[]{:S(2)}) collective-permute-start(f32[64,640]{1,0:T(8,128)S(1)} %slice_add_fusion.refs_0_), channel_id=1, source_target_pairs={{0,12},{4,8},{8,4},{12,0},{16,28},{20,24},{24,20},{28,16},{1,13},{... | collective-permute-start | bytes 491528 | tf_op jit(solution)/shard_map/ppermute | solution.py:558
  20.7 9.9 %collective-permute-start.3 = (f32[64,640]{1,0:T(8,128)S(1)}, f32[64,640]{1,0:T(8,128)S(1)}, u32[]{:S(2)}, u32[]{:S(2)}) collective-permute-start(f32[64,640]{1,0:T(8,128)S(1)} %slice_add_fusion.refs_0_), channel_id=1, source_target_pairs={{0,8},{4,12},{8,0},{12,4},{16,24},{20,28},{24,16},{28,20},{1,9},{5... | collective-permute-start | bytes 491528 | tf_op jit(solution)/shard_map/ppermute | solution.py:558
  21.2 9.4 %collective-permute-start.2 = (f32[64,640]{1,0:T(8,128)S(1)}, f32[64,640]{1,0:T(8,128)S(1)}, u32[]{:S(2)}, u32[]{:S(2)}) collective-permute-start(f32[64,640]{1,0:T(8,128)S(1)} %slice_add_fusion.refs_0_), channel_id=1, source_target_pairs={{0,4},{4,0},{8,12},{12,8},{16,20},{20,16},{24,28},{28,24},{1,5},{5... | collective-permute-start | bytes 491528 | tf_op jit(solution)/shard_map/ppermute | solution.py:558
  41.7 3.4 %collective-permute-start.11 = (f32[256,256]{1,0:T(8,128)S(1)}, f32[256,256]{1,0:T(8,128)S(1)}, u32[]{:S(2)}, u32[]{:S(2)}) collective-permute-start(f32[256,256]{1,0:T(8,128)S(1)} %bitcast.8), channel_id=1, source_target_pairs={{0,1},{1,0},{2,3},{3,2},{4,5},{5,4},{6,7},{7,6},{8,9},{9,8},{10,11... | collective-permute-start | bytes 786440 | tf_op jit(solution)/shard_map/ppermute | solution.py:558
  42.6 9.8 %collective-permute-start.10 = (f32[64,256]{1,0:T(8,128)S(1)}, f32[64,256]{1,0:T(8,128)S(1)}, u32[]{:S(2)}, u32[]{:S(2)}) collective-permute-start(f32[64,256]{1,0:T(8,128)S(1)} %bitcast.10), channel_id=1, source_target_pairs={{0,17},{1,16},{2,19},{3,18},{4,21},{5,20},{6,23},{7,22},{8,25},{9,... | collective-permute-start | bytes 196616 | tf_op jit(solution)/shard_map/ppermute | solution.py:582
  52.4 2.7 %copy-start.1 = (f32[5,8192]{1,0:T(8,128)S(1)}, f32[5,8192]{1,0:T(8,128)}, u32[]{:S(2)}) copy-start(f32[5,8192]{1,0:T(8,128)} %amplitude_ref.3) | copy-start | bytes 491524
  52.4 2.7 %copy-start.2 = (s32[8192]{0:T(1024)S(1)}, s32[8192]{0:T(1024)}, u32[]{:S(2)}) copy-start(s32[8192]{0:T(1024)} %param.5) | copy-start | bytes 98308
  53.6 1.5 %collective-permute-start.12 = (f32[64,640]{1,0:T(8,128)S(1)}, f32[64,640]{1,0:T(8,128)S(1)}, u32[]{:S(2)}, u32[]{:S(2)}) collective-permute-start(f32[64,640]{1,0:T(8,128)S(1)} %descend.1), channel_id=1, source_target_pairs={{0,1},{1,0},{2,3},{3,2},{4,5},{5,4},{6,7},{7,6},{8,9},{9,8},{10,11... | collective-permute-start | bytes 491528 | tf_op jit(solution)/shard_map/ppermute | solution.py:558

commit v5 on v4

--- a/solution.py
+++ b/solution.py
@@ -254,8 +254,8 @@
         target_ref[n, :, begin:end] -= dot_tn(left, right)
 
 
-def couple(row_ref, inverse_ref, coupling_ref, begin, end):
-    for n in range(inverse_ref.shape[0]):
+def couple(row_ref, inverse_ref, coupling_ref, begin, end, nodes=None):
+    for n in nodes or range(inverse_ref.shape[0]):
         coupling_ref[n, :, begin:end] = dot_hi(inverse_ref[n], row_ref[n, :, begin:end])
 
 
@@ -296,11 +296,12 @@
     update(targets[0], tier - 1, row_ref, coupling_ref, first, last)
 
 
-def forward(source_refs, coupling_ref, target_ref, own_ref, depth):
+def forward(source_refs, coupling_ref, target_ref, own_ref, depth, targets):
     nodes, knots, width = coupling_ref.shape
     share = nodes // target_ref.shape[0]
-    own_ref[:, depth * knots:(depth + 1) * knots] = source_refs[0][:, width:]
-    for n in range(target_ref.shape[0]):
+    if 0 in targets:
+        own_ref[:, depth * knots:(depth + 1) * knots] = source_refs[0][:, width:]
+    for n in targets:
         reduced = [
             source_refs[c][:, :width] - dot_hi(source_refs[c][:, width:], coupling_ref[c])
             for c in range(n * share, (n + 1) * share)
@@ -330,8 +331,14 @@
         prior = diagonal(prior_ref[tier:tier + 1, :])
         for n in range(nodes):
             inverse_refs[i][n] = work_refs[i][n, :, tier * knots:] + prior
+        above = inverse_ref.shape[0]
         others = [
-            functools.partial(couple, row_ref, inverse_ref, coupling_ref, 0, tier * knots),
+            functools.partial(
+                couple, row_ref, inverse_ref, coupling_ref, 0, tier * knots, part
+            )
+            for part in (range(above // 2), range(above // 2, above))
+        ]
+        others += [
             functools.partial(
                 update, targets[i], tier, row_ref, coupling_ref, 0, tier * knots
             ),
@@ -340,9 +347,12 @@
             functools.partial(update, targets[i + tier - below], below, row_ref, coupling_ref)
             for below in range(tier - 1, -1, -1)
         ]
-        others.append(functools.partial(
-            forward, source_refs, coupling_ref, reduced_refs[i], own_ref, i
-        ))
+        others += [
+            functools.partial(
+                forward, source_refs, coupling_ref, reduced_refs[i], own_ref, i, [n]
+            )
+            for n in range(nodes)
+        ]
         invert(
             [inverse_refs[i].at[n] for n in range(nodes)],
             [panel_ref.at[n] for n in range(nodes)],
@@ -356,7 +366,7 @@
             update(targets[i + 1], tier - 1, row_ref, coupling_ref, first, tier * knots)
     for below in range(top - 1, -1, -1):
         update(targets[count + top - 1 - below], below, row_ref, coupling_ref)
-    forward(source_refs, coupling_ref, right_ref, own_ref, count)
+    forward(source_refs, coupling_ref, right_ref, own_ref, count, [0])
 
 
 def whole_call(kernel, args, shapes, scratch, name, limit=8, flops=10**10):

time: 59.7 us -> 59.3 us (level)
  transfers between devices with their start and end apart: 13 -> 13, of which waited for: 3 -> 3; matrix products, arithmetic and copies ran while one was open for 0% -> 0% of each run, Pallas kernels for 27% -> 28%
where the time goes in v5:
time: 59.3 us; the launch traced here: 59.2 us
  Pallas kernels  38.5 us (65%)
  starting transfers between devices  16.2 us (27%)
  waiting for transfers between devices  3.95 us (7%)
    pallas_call x4, Pallas kernels, whole_call(): pl.pallas_call(kernel, in_specs=[vmem] * len(args), out_specs=[vmem] * le...  28.2 us
    ppermute x10, starting transfers between devices, swapped(): return lax.ppermute(value, axis, pairs)  10.7 us
    pallas_call x1, Pallas kernels, statistics(): pl.pallas_call(stats_kernel, grid=(obs // block,), in_specs=[pl.BlockSpec...  5.89 us
    ppermute x3, starting transfers between devices, moved(): return lax.ppermute(value, ('region', 'obs'), pairs)  5.5 us
    pallas_call x1, Pallas kernels, fitted_fields(): pl.pallas_call(fitted_kernel, grid=(obs // block,), in_specs=[pl.BlockSpe...  4.41 us
    ppermute x10, waiting for transfers between devices, swapped(): return lax.ppermute(value, axis, pairs)  2.43 us
    ppermute x3, waiting for transfers between devices, moved(): return lax.ppermute(value, ('region', 'obs'), pairs)  1.52 us
  transfers between devices with their start and end apart: 13, of which 3 were waited for; matrix products, arithmetic and copies ran while one was open for 0% of the time, Pallas kernels for 28%

profile of v5, /device:TPU:0, one launch (start us, length us, event | category | flops | bytes accessed | tf_op | source)
XLA Modules:
  0.0 59.2 jit_solution(16763179961977065113)
XLA Ops:
  0.0 5.9 %statistics.1 = f32[80,640]{1,0:T(8,128)S(1)} custom-call(s32[1,8192]{1,0:T(1,128)} %bitcast.6, f32[5,8192]{1,0:T(8,128)} %amplitude_ref.3, bf16[64,8192]{1,0:T(8,128)(2,1)} %fields_ref.1, bf16[5,512,128]{2,1,0:T(8,128)(2,1)} %basis_ref.3), custom_call_target="tpu_custom_call" | custom-call | flops 3623878656 | bytes 4194304 | tf_op jit(solution)/shard_map/statistics/pallas_call | solution.py:111
  5.9 0.0 copy-start.3
  5.9 0.5 collective-permute-start
  6.4 1.1 %collective-permute-done = f32[80,640]{1,0:T(8,128)S(1)} collective-permute-done((f32[80,640]{1,0:T(8,128)S(1)}, f32[80,640]{1,0:T(8,128)S(1)}, u32[]{:S(2)}, u32[]{:S(2)}) %collective-permute-start) | collective-permute-done | bytes 204832 | tf_op jit(solution)/shard_map/ppermute | solution.py:568
  7.5 3.0 %collective-permute-start.6 = (f32[16,512]{1,0:T(8,128)S(1)}, f32[16,512]{1,0:T(8,128)S(1)}, u32[]{:S(2)}, u32[]{:S(2)}) collective-permute-start(f32[16,512]{1,0:T(8,128)S(1)} %slice.9), channel_id=1, source_target_pairs={{0,2},{1,16},{2,0},{3,18},{4,6},{5,20},{6,4},{7,22},{8,10},{9,24},... | collective-permute-start | bytes 98312 | tf_op jit(solution)/shard_map/ppermute | solution.py:592
  10.5 0.1 collective-permute-start.5
  10.6 0.2 copy.6
  10.9 2.0 %collective-permute-start.1 = (f32[64,640]{1,0:T(8,128)S(1)}, f32[64,640]{1,0:T(8,128)S(1)}, u32[]{:S(2)}, u32[]{:S(2)}) collective-permute-start(f32[64,640]{1,0:T(8,128)S(1)} %slice.8), channel_id=1, source_target_pairs={{0,2},{1,3},{2,0},{3,1},{4,6},{5,7},{6,4},{7,5},{8,10},{9,11},{10,... | collective-permute-start | bytes 491528 | tf_op jit(solution)/shard_map/ppermute | solution.py:568
  12.9 1.5 %collective-permute-done.5 = f32[16,512]{1,0:T(8,128)S(1)} collective-permute-done((f32[16,512]{1,0:T(8,128)S(1)}, f32[16,512]{1,0:T(8,128)S(1)}, u32[]{:S(2)}, u32[]{:S(2)}) %collective-permute-start.5) | collective-permute-done | bytes 32800 | tf_op jit(solution)/shard_map/ppermute | solution.py:592
  14.4 2.6 %collective-permute-start.9 = (f32[16,512]{1,0:T(8,128)S(1)}, f32[16,512]{1,0:T(8,128)S(1)}, u32[]{:S(2)}, u32[]{:S(2)}) collective-permute-start(f32[16,512]{1,0:T(8,128)S(1)} %add_select_fusion.refs_0_), channel_id=1, source_target_pairs={{0,12},{4,8},{8,4},{12,0},{16,28},{20,24},{24,20},{28,16},{1,13},{... | collective-permute-start | bytes 98312 | tf_op jit(solution)/shard_map/ppermute | solution.py:568
  17.0 0.4 collective-permute-start.8
  17.4 0.5 collective-permute-start.7
  18.0 0.0 collective-permute-done.1
  18.0 2.7 %collective-permute-start.4 = (f32[64,640]{1,0:T(8,128)S(1)}, f32[64,640]{1,0:T(8,128)S(1)}, u32[]{:S(2)}, u32[]{:S(2)}) collective-permute-start(f32[64,640]{1,0:T(8,128)S(1)} %slice_add_fusion.refs_0_), channel_id=1, source_target_pairs={{0,12},{4,8},{8,4},{12,0},{16,28},{20,24},{24,20},{28,16},{1,13},{... | collective-permute-start | bytes 491528 | tf_op jit(solution)/shard_map/ppermute | solution.py:568
  20.7 0.4 collective-permute-start.3
  21.1 0.0 collective-permute-done.9.refs_3_
  21.2 0.4 collective-permute-start.2
  21.6 0.0 collective-permute-done.8.refs_2_
  21.6 0.0 collective-permute-done.7.refs_1_
  21.6 9.0 %leaf_tier.1 = (f32[4,128,128]{2,1,0:T(8,128)S(1)}, f32[4,128,512]{2,1,0:T(8,128)S(1)}, f32[4,128,512]{2,1,0:T(8,128)S(1)}, f32[2,128,512]{2,1,0:T(8,128)S(1)}, ...) custom-call(bf16[5,512,128]{2,1,0:T(8,128)(2,1)S(1)} %copy-done, bf16[5,128,512]{2,1,0:T(8,128)(2,1)S(1)} %bitcast.4, ...), custom_call_target="tpu_custom_call" | custom-call | flops 20000000000 | bytes 1048576 | tf_op jit(solution)/shard_map/leaf_tier/pallas_call | solution.py:373
  30.6 0.0 collective-permute-done.4.refs_3_
  30.6 10.7 %inner_tiers.1 = (f32[4,128,512]{2,1,0:T(8,128)S(1)}, f32[2,128,128]{2,1,0:T(8,128)S(1)}, f32[1,128,128]{2,1,0:T(8,128)S(1)}, f32[2,128,384]{2,1,0:T(8,128)S(1)}...) custom-call(f32[64,640]{1,0:T(8,128)S(1)} %slice_add_fusion.refs_0_,, ...), custom_call_target="tpu_custom_call" | custom-call | flops 20000000000 | bytes 1048576 | tf_op jit(solution)/shard_map/inner_tiers/pallas_call | solution.py:373
  41.3 0.9 %collective-permute-start.11 = (f32[256,256]{1,0:T(8,128)S(1)}, f32[256,256]{1,0:T(8,128)S(1)}, u32[]{:S(2)}, u32[]{:S(2)}) collective-permute-start(f32[256,256]{1,0:T(8,128)S(1)} %bitcast.8), channel_id=1, source_target_pairs={{0,1},{1,0},{2,3},{3,2},{4,5},{5,4},{6,7},{7,6},{8,9},{9,8},{10,11... | collective-permute-start | bytes 786440 | tf_op jit(solution)/shard_map/ppermute | solution.py:568
  42.2 2.5 %collective-permute-start.10 = (f32[64,256]{1,0:T(8,128)S(1)}, f32[64,256]{1,0:T(8,128)S(1)}, u32[]{:S(2)}, u32[]{:S(2)}) collective-permute-start(f32[64,256]{1,0:T(8,128)S(1)} %bitcast.10), channel_id=1, source_target_pairs={{0,17},{1,16},{2,19},{3,18},{4,21},{5,20},{6,23},{7,22},{8,25},{9,... | collective-permute-start | bytes 196616 | tf_op jit(solution)/shard_map/ppermute | solution.py:592
  44.7 7.4 %top.1 = (f32[64,384]{1,0:T(8,128)S(1)}, f32[384,256]{1,0:T(8,128)S(1)}, f32[128,128]{1,0:T(8,128)S(1)}, f32[128,128]{1,0:T(8,128)S(1)}, f32[128,128]{1,0:T(8,128)S(1)}) custom-call(f32[256,256]{1,0:T(8,128)S(1)} %bitcast.9, f32[256,256]{1,0:T(8,128)S(1)} %collective-permute-done.11.other_ref, f32[5,128]{1,0:T(8,128)S(1)} %copy-done.3, ...), custom_call_target="tpu_custom_call" | custom-call | flops 10000000000 | bytes 1048576 | tf_op jit(solution)/shard_map/top/pallas_call | solution.py:373
  52.1 0.0 collective-permute-done.10.other_ref
  52.1 0.0 copy-start.1
  52.1 0.0 copy-start.2
  52.1 1.1 %descend.1 = f32[64,640]{1,0:T(8,128)S(1)} custom-call(f32[64,256]{1,0:T(8,128)S(1)} %bitcast.11, f32[64,256]{1,0:T(8,128)S(1)} %collective-permute-done.10.other_ref, f32[128,128]{1,0:T(8,128)S(1)} %get-tuple-element.38.top_ref, f32[128,128]{1,0:T(8,128)S(1)} %get-tuple-element.39.coupling_ref, f32[128,128]{1,0:T(8,128)S(1)} %get-tuple-element.40.root_ref, ...), custom_call_target="tpu_custom_call" | custom-call | flops 1000000000 | bytes 1048576 | tf_op jit(solution)/shard_map/descend/pallas_call | solution.py:373
  53.3 0.1 collective-permute-start.12
  53.4 1.3 %collective-permute-done.12 = f32[64,640]{1,0:T(8,128)S(1)} collective-permute-done((f32[64,640]{1,0:T(8,128)S(1)}, f32[64,640]{1,0:T(8,128)S(1)}, u32[]{:S(2)}, u32[]{:S(2)}) %collective-permute-start.12) | collective-permute-done | bytes 163872 | tf_op jit(solution)/shard_map/ppermute | solution.py:568
  54.8 4.4 %fitted_fields.1 = f32[64,8192]{1,0:T(8,128)} custom-call(s32[1,8192]{1,0:T(1,128)S(1)} %bitcast.7, f32[5,8192]{1,0:T(8,128)S(1)} %copy-done.1, f32[64,640]{1,0:T(8,128)S(1)} %broadcast_select_fusion.weight_ref, bf16[5,128,512]{2,1,0:T(8,128)(2,1)S(1)} %bitcast.5), custom_call_target="tpu_custom_call" | custom-call | tf_op jit(solution)/shard_map/fitted_fields/pallas_call | solution.py:549
  (15 shorter events, 0.1 us)
Async XLA Ops:
  0.0 10.6 %copy-start = (bf16[5,512,128]{2,1,0:T(8,128)(2,1)S(1)}, bf16[5,512,128]{2,1,0:T(8,128)(2,1)}, u32[]{:S(2)}) copy-start(bf16[5,512,128]{2,1,0:T(8,128)(2,1)} %basis_ref.3) | copy-start | bytes 1966084
  5.9 15.7 %copy-start.3 = (f32[5,128]{1,0:T(8,128)S(1)}, f32[5,128]{1,0:T(8,128)}, u32[]{:S(2)}) copy-start(f32[5,128]{1,0:T(8,128)} %prior_ref.3) | copy-start | bytes 7684
  5.9 1.6 %collective-permute-start = (f32[80,640]{1,0:T(8,128)S(1)}, f32[80,640]{1,0:T(8,128)S(1)}, u32[]{:S(2)}, u32[]{:S(2)}) collective-permute-start(f32[80,640]{1,0:T(8,128)S(1)} %statistics.1), channel_id=1, source_target_pairs={{0,1},{1,0},{2,3},{3,2},{4,5},{5,4},{6,7},{7,6},{8,9},{9,8},{10,11... | collective-permute-start | bytes 614408 | tf_op jit(solution)/shard_map/ppermute | solution.py:568
  7.5 5.4 %collective-permute-start.6 = (f32[16,512]{1,0:T(8,128)S(1)}, f32[16,512]{1,0:T(8,128)S(1)}, u32[]{:S(2)}, u32[]{:S(2)}) collective-permute-start(f32[16,512]{1,0:T(8,128)S(1)} %slice.9), channel_id=1, source_target_pairs={{0,2},{1,16},{2,0},{3,18},{4,6},{5,20},{6,4},{7,22},{8,10},{9,24},... | collective-permute-start | bytes 98312 | tf_op jit(solution)/shard_map/ppermute | solution.py:592
  10.5 3.9 %collective-permute-start.5 = (f32[16,512]{1,0:T(8,128)S(1)}, f32[16,512]{1,0:T(8,128)S(1)}, u32[]{:S(2)}, u32[]{:S(2)}) collective-permute-start(f32[16,512]{1,0:T(8,128)S(1)} %slice.9), channel_id=1, source_target_pairs={{0,2},{1,18},{2,0},{3,16},{4,6},{5,22},{6,4},{7,20},{8,10},{9,26},... | collective-permute-start | bytes 98312 | tf_op jit(solution)/shard_map/ppermute | solution.py:592
  10.9 7.1 %collective-permute-start.1 = (f32[64,640]{1,0:T(8,128)S(1)}, f32[64,640]{1,0:T(8,128)S(1)}, u32[]{:S(2)}, u32[]{:S(2)}) collective-permute-start(f32[64,640]{1,0:T(8,128)S(1)} %slice.8), channel_id=1, source_target_pairs={{0,2},{1,3},{2,0},{3,1},{4,6},{5,7},{6,4},{7,5},{8,10},{9,11},{10,... | collective-permute-start | bytes 491528 | tf_op jit(solution)/shard_map/ppermute | solution.py:568
  14.4 6.7 %collective-permute-start.9 = (f32[16,512]{1,0:T(8,128)S(1)}, f32[16,512]{1,0:T(8,128)S(1)}, u32[]{:S(2)}, u32[]{:S(2)}) collective-permute-start(f32[16,512]{1,0:T(8,128)S(1)} %add_select_fusion.refs_0_), channel_id=1, source_target_pairs={{0,12},{4,8},{8,4},{12,0},{16,28},{20,24},{24,20},{28,16},{1,13},{... | collective-permute-start | bytes 98312 | tf_op jit(solution)/shard_map/ppermute | solution.py:568
  17.0 4.6 %collective-permute-start.8 = (f32[16,512]{1,0:T(8,128)S(1)}, f32[16,512]{1,0:T(8,128)S(1)}, u32[]{:S(2)}, u32[]{:S(2)}) collective-permute-start(f32[16,512]{1,0:T(8,128)S(1)} %add_select_fusion.refs_0_), channel_id=1, source_target_pairs={{0,8},{4,12},{8,0},{12,4},{16,24},{20,28},{24,16},{28,20},{1,9},{5... | collective-permute-start | bytes 98312 | tf_op jit(solution)/shard_map/ppermute | solution.py:568
  17.4 4.1 %collective-permute-start.7 = (f32[16,512]{1,0:T(8,128)S(1)}, f32[16,512]{1,0:T(8,128)S(1)}, u32[]{:S(2)}, u32[]{:S(2)}) collective-permute-start(f32[16,512]{1,0:T(8,128)S(1)} %add_select_fusion.refs_0_), channel_id=1, source_target_pairs={{0,4},{4,0},{8,12},{12,8},{16,20},{20,16},{24,28},{28,24},{1,5},{5... | collective-permute-start | bytes 98312 | tf_op jit(solution)/shard_map/ppermute | solution.py:568
  18.0 12.5 %collective-permute-start.4 = (f32[64,640]{1,0:T(8,128)S(1)}, f32[64,640]{1,0:T(8,128)S(1)}, u32[]{:S(2)}, u32[]{:S(2)}) collective-permute-start(f32[64,640]{1,0:T(8,128)S(1)} %slice_add_fusion.refs_0_), channel_id=1, source_target_pairs={{0,12},{4,8},{8,4},{12,0},{16,28},{20,24},{24,20},{28,16},{1,13},{... | collective-permute-start | bytes 491528 | tf_op jit(solution)/shard_map/ppermute | solution.py:568
  20.7 9.9 %collective-permute-start.3 = (f32[64,640]{1,0:T(8,128)S(1)}, f32[64,640]{1,0:T(8,128)S(1)}, u32[]{:S(2)}, u32[]{:S(2)}) collective-permute-start(f32[64,640]{1,0:T(8,128)S(1)} %slice_add_fusion.refs_0_), channel_id=1, source_target_pairs={{0,8},{4,12},{8,0},{12,4},{16,24},{20,28},{24,16},{28,20},{1,9},{5... | collective-permute-start | bytes 491528 | tf_op jit(solution)/shard_map/ppermute | solution.py:568
  21.2 9.4 %collective-permute-start.2 = (f32[64,640]{1,0:T(8,128)S(1)}, f32[64,640]{1,0:T(8,128)S(1)}, u32[]{:S(2)}, u32[]{:S(2)}) collective-permute-start(f32[64,640]{1,0:T(8,128)S(1)} %slice_add_fusion.refs_0_), channel_id=1, source_target_pairs={{0,4},{4,0},{8,12},{12,8},{16,20},{20,16},{24,28},{28,24},{1,5},{5... | collective-permute-start | bytes 491528 | tf_op jit(solution)/shard_map/ppermute | solution.py:568
  41.3 3.4 %collective-permute-start.11 = (f32[256,256]{1,0:T(8,128)S(1)}, f32[256,256]{1,0:T(8,128)S(1)}, u32[]{:S(2)}, u32[]{:S(2)}) collective-permute-start(f32[256,256]{1,0:T(8,128)S(1)} %bitcast.8), channel_id=1, source_target_pairs={{0,1},{1,0},{2,3},{3,2},{4,5},{5,4},{6,7},{7,6},{8,9},{9,8},{10,11... | collective-permute-start | bytes 786440 | tf_op jit(solution)/shard_map/ppermute | solution.py:568
  42.2 9.9 %collective-permute-start.10 = (f32[64,256]{1,0:T(8,128)S(1)}, f32[64,256]{1,0:T(8,128)S(1)}, u32[]{:S(2)}, u32[]{:S(2)}) collective-permute-start(f32[64,256]{1,0:T(8,128)S(1)} %bitcast.10), channel_id=1, source_target_pairs={{0,17},{1,16},{2,19},{3,18},{4,21},{5,20},{6,23},{7,22},{8,25},{9,... | collective-permute-start | bytes 196616 | tf_op jit(solution)/shard_map/ppermute | solution.py:592
  52.1 2.7 %copy-start.1 = (f32[5,8192]{1,0:T(8,128)S(1)}, f32[5,8192]{1,0:T(8,128)}, u32[]{:S(2)}) copy-start(f32[5,8192]{1,0:T(8,128)} %amplitude_ref.3) | copy-start | bytes 491524
  52.1 2.7 %copy-start.2 = (s32[8192]{0:T(1024)S(1)}, s32[8192]{0:T(1024)}, u32[]{:S(2)}) copy-start(s32[8192]{0:T(1024)} %param.5) | copy-start | bytes 98308
  53.3 1.5 %collective-permute-start.12 = (f32[64,640]{1,0:T(8,128)S(1)}, f32[64,640]{1,0:T(8,128)S(1)}, u32[]{:S(2)}, u32[]{:S(2)}) collective-permute-start(f32[64,640]{1,0:T(8,128)S(1)} %descend.1), channel_id=1, source_target_pairs={{0,1},{1,0},{2,3},{3,2},{4,5},{5,4},{6,7},{7,6},{8,9},{9,8},{10,11... | collective-permute-start | bytes 491528 | tf_op jit(solution)/shard_map/ppermute | solution.py:568
